TPU v7x, 32 devices: a whole 2x2x4 slice. The times are simulated.
32 devices in a mesh: seq: 4 (over y, x), fsdp: 8 (over z, core).
Axes of the slice: x: 2, y: 2, z: 4, core: 2. Of those that a mesh axis runs over, the one named last changes fastest.
Arguments:
- tokens: bfloat16 [8192, 2048], P(('fsdp', 'seq')), may hold values from -6 to 6
- seq_lengths: int32 [8, 3], P('fsdp'), may hold values from 1 to 1022, as said below
- pic_starts: int32 [8, 2], P('fsdp'), may hold values from 0 to 768, as said below
- pic_lengths: int32 [8, 2], P('fsdp'), may hold values from 64 to 256, as said below
- norm1_gain: bfloat16 [2048], P(('seq', 'fsdp')), may hold values from 0.5 to 1.5
- w_query: bfloat16 [2048, 2048], P(('seq', 'fsdp')), may hold values from -0.125 to 0.125
- w_key: bfloat16 [2048, 1024], P(('seq', 'fsdp')), may hold values from -0.125 to 0.125
- w_value: bfloat16 [2048, 1024], P(('seq', 'fsdp')), may hold values from -0.125 to 0.125
- q_gain: bfloat16 [128], P(('seq', 'fsdp')), may hold values from 0.099609375 to 1.8984375
- k_gain: bfloat16 [128], P(('seq', 'fsdp')), may hold values from 0.099609375 to 1.8984375
- w_out: bfloat16 [2048, 2048], P(('seq', 'fsdp')), may hold values from -2 to 2
- norm2_gain: bfloat16 [2048], P(('seq', 'fsdp')), may hold values from 0.5 to 1.5
- w_gate: bfloat16 [2048, 6144], P(('seq', 'fsdp')), may hold values from -0.125 to 0.125
- w_up: bfloat16 [2048, 6144], P(('seq', 'fsdp')), may hold values from -0.125 to 0.125
- w_down: bfloat16 [6144, 2048], P(None, ('seq', 'fsdp')), may hold values from -0.625 to 0.625
- cotangent: bfloat16 [8192, 2048], P(('fsdp', 'seq')), may hold values from -6 to 6
Outputs:
- output: bfloat16 [8192, 2048], P(('fsdp', 'seq'))
- input_grad: bfloat16 [8192, 2048], P(('fsdp', 'seq'))
- norm1_gain_grad: float32 [2048], P(('seq', 'fsdp'))
- w_query_grad: float32 [2048, 2048], P(('seq', 'fsdp'))
- w_key_grad: float32 [2048, 1024], P(('seq', 'fsdp'))
- w_value_grad: float32 [2048, 1024], P(('seq', 'fsdp'))
- q_gain_grad: float32 [128], P(('seq', 'fsdp'))
- k_gain_grad: float32 [128], P(('seq', 'fsdp'))
- w_out_grad: float32 [2048, 2048], P(('seq', 'fsdp'))
- norm2_gain_grad: float32 [2048], P(('seq', 'fsdp'))
- w_gate_grad: float32 [2048, 6144], P(('seq', 'fsdp'))
- w_up_grad: float32 [2048, 6144], P(('seq', 'fsdp'))
- w_down_grad: float32 [6144, 2048], P(None, ('seq', 'fsdp'))
Inputs may be any that keep to these rules, and one draw needn't show every extreme that they name: `seq_lengths`: each group's three lengths sum to 1024; the first and the last have 1 to 32 tokens; in some group both of these have 1. `pic_starts`: picture i of a group starts at a place from 2 i * 256 to 2 i * 256 + 256; pictures don't intersect; in some group the first picture starts at 0 and the last at 768. `pic_lengths`: in every group one picture has exactly 256 tokens.
All inputs are finite; a program needn't handle non-finite values.
Results may differ from a plain program's by a relative error of at most 0.025.
Values may be sent and summed in bfloat16 or wider, within the bound.
A program may use at most 640 MiB of HBM per device.

v0:
```python
import jax
import jax.numpy as jnp
from jax import lax
from jax.sharding import PartitionSpec as P

epsilon = 1e-06
theta = 1000000.0
masked_score = -1e30


def normalize(values):
    return values * lax.rsqrt(jnp.mean(values * values, axis=-1, keepdims=True) + epsilon)


def rotate(values, position):
    half_size = values.shape[-1] // 2
    frequency = jnp.float32(theta) ** (
        -(jnp.arange(half_size, dtype=jnp.float32) * 2.0 / values.shape[-1])
    )
    angles = position.astype(jnp.float32)[:, None] * frequency[None, :]
    cosine = jnp.cos(angles)[:, None, :]
    sine_part = jnp.sin(angles)[:, None, :]
    leading = values[..., :half_size]
    trailing = values[..., half_size:]
    return jnp.concatenate(
        [leading * cosine - trailing * sine_part, trailing * cosine + leading * sine_part], axis=-1
    )


def head_prep(values, gain, position):
    row_count = values.shape[0]
    shaped = values.reshape(row_count, -1, gain.shape[0])
    return rotate(normalize(shaped) * gain, position).reshape(row_count, -1)


def layout(lengths, starts, sizes, places):
    border_one = lengths[0]
    border_two = border_one + lengths[1]
    member = (places >= border_one).astype(jnp.int32) + (places >= border_two).astype(jnp.int32)
    begins = jnp.where(member == 0, 0, jnp.where(member == 1, border_one, border_two))
    inside = (places[:, None] >= starts[None, :]) & (
        places[:, None] < starts[None, :] + sizes[None, :]
    )
    numbers = jnp.arange(1, starts.shape[0] + 1, dtype=jnp.int32)
    label = jnp.sum(jnp.where(inside, numbers[None, :], 0), axis=1) - 1
    return (member, places - begins, label)


def visible(query_member, query_place, query_label, key_member, key_place, key_label):
    same_sequence = query_member[:, None] == key_member[None, :]
    causal = query_place[:, None] >= key_place[None, :]
    picture = (query_label[:, None] == key_label[None, :]) & (query_label[:, None] >= 0)
    return same_sequence & (causal | picture)


def contract_rows(left_rows, right_rows):
    return lax.dot_general(
        left_rows, right_rows, (((0,), (0,)), ((), ())), preferred_element_type=jnp.float32
    )


def contract_cols(left_rows, right_rows):
    return lax.dot_general(
        left_rows, right_rows, (((1,), (1,)), ((), ())), preferred_element_type=jnp.float32
    )


def swiglu(gate, up_part):
    return jax.nn.silu(gate) * up_part


def scaled_norm(values, gain):
    return normalize(values) * gain


def shards(
    tokens,
    seq_lengths,
    pic_starts,
    pic_lengths,
    norm1_gain,
    w_query,
    w_key,
    w_value,
    q_gain,
    k_gain,
    w_out,
    norm2_gain,
    w_gate,
    w_up,
    w_down,
    cotangent,
):
    tok_rows, width = tokens.shape
    group_rows = tok_rows * lax.axis_size("seq")
    places = jnp.arange(group_rows, dtype=jnp.int32)
    member, position, label = layout(seq_lengths[0], pic_starts[0], pic_lengths[0], places)
    local_start = lax.axis_index("seq") * tok_rows
    own_place = local_start + jnp.arange(tok_rows, dtype=jnp.int32)
    own_member = lax.dynamic_slice_in_dim(member, local_start, tok_rows, 0)
    own_position = lax.dynamic_slice_in_dim(position, local_start, tok_rows, 0)
    own_label = lax.dynamic_slice_in_dim(label, local_start, tok_rows, 0)
    allowed = visible(own_member, own_place, own_label, member, places, label)
    gathered = (
        lax.all_gather(norm1_gain, ("seq", "fsdp"), axis=0, tiled=True),
        lax.all_gather(norm2_gain, ("seq", "fsdp"), axis=0, tiled=True),
        lax.all_gather(w_query, ("seq", "fsdp"), axis=0, tiled=True),
        lax.all_gather(w_key, ("seq", "fsdp"), axis=0, tiled=True),
        lax.all_gather(w_value, ("seq", "fsdp"), axis=0, tiled=True),
        lax.all_gather(q_gain, ("seq", "fsdp"), axis=0, tiled=True),
        lax.all_gather(k_gain, ("seq", "fsdp"), axis=0, tiled=True),
    )
    gain_one = gathered[0].astype(jnp.float32)
    gain_two = gathered[1].astype(jnp.float32)
    query_full = gathered[2]
    key_full = gathered[3]
    value_full = gathered[4]
    query_gain = gathered[5].astype(jnp.float32)
    key_gain = gathered[6].astype(jnp.float32)
    head_size = query_gain.shape[0]
    kv_heads = key_full.shape[1] // head_size
    group_ratio = query_full.shape[1] // head_size // kv_heads
    scale = head_size ** (-0.5)
    inputs = tokens.astype(jnp.float32)
    normed_one = scaled_norm(inputs, gain_one).astype(jnp.bfloat16)
    query_raw = jnp.dot(normed_one, query_full, preferred_element_type=jnp.float32)
    key_raw = jnp.dot(normed_one, key_full, preferred_element_type=jnp.float32)
    value_b = jnp.dot(normed_one, value_full, preferred_element_type=jnp.float32).astype(
        jnp.bfloat16
    )
    query_b = head_prep(query_raw, query_gain, own_position).astype(jnp.bfloat16)
    key_b = head_prep(key_raw, key_gain, own_position).astype(jnp.bfloat16)
    group_keys, group_values = (
        lax.all_gather(key_b, "seq", axis=0, tiled=True),
        lax.all_gather(value_b, "seq", axis=0, tiled=True),
    )

    def split_heads(keys_in, values_in):
        return (
            keys_in.reshape(group_rows, kv_heads, head_size).transpose(1, 0, 2),
            values_in.reshape(group_rows, kv_heads, head_size).transpose(1, 0, 2),
        )

    query_heads = query_b.reshape(tok_rows, kv_heads, group_ratio, head_size).transpose(1, 0, 2, 3)

    def masked_scores(query_head, key_head):
        scores = (
            jnp.einsum("trd,kd->trk", query_head, key_head, preferred_element_type=jnp.float32)
            * scale
        )
        return jnp.where(allowed[:, None, :], scores, masked_score)

    def head_forward(items):
        query_head, key_head, value_head = items
        scores = masked_scores(query_head, key_head)
        highest = jnp.max(scores, axis=-1, keepdims=True)
        log_total = highest + jnp.log(jnp.sum(jnp.exp(scores - highest), axis=-1, keepdims=True))
        softmax_weights = jnp.exp(scores - log_total).astype(jnp.bfloat16)
        mixed_head = jnp.einsum(
            "trk,kd->trd", softmax_weights, value_head, preferred_element_type=jnp.float32
        )
        return (mixed_head, log_total)

    key_heads, value_heads = split_heads(group_keys, group_values)
    mixed, log_totals = lax.map(head_forward, (query_heads, key_heads, value_heads))
    attn_b = mixed.transpose(1, 0, 2, 3).reshape(tok_rows, -1).astype(jnp.bfloat16)
    columns = attn_b
    branch = jnp.dot(
        columns,
        lax.all_gather(w_out, ("seq", "fsdp"), axis=0, tiled=True),
        preferred_element_type=jnp.float32,
    )
    middle = inputs + branch
    normed_two = scaled_norm(middle, gain_two).astype(jnp.bfloat16)
    hidden_units = w_gate.shape[1]
    blocks = (
        lax.all_gather(w_gate, ("seq", "fsdp"), axis=0, tiled=True),
        lax.all_gather(w_up, ("seq", "fsdp"), axis=0, tiled=True),
    )
    columns = normed_two
    gate = jnp.dot(columns, blocks[0], preferred_element_type=jnp.float32)
    up_part = jnp.dot(columns, blocks[1], preferred_element_type=jnp.float32)
    hidden_b = swiglu(gate, up_part).astype(jnp.bfloat16)
    down_part = jnp.dot(
        hidden_b,
        lax.all_gather(w_down, ("seq", "fsdp"), axis=1, tiled=True),
        preferred_element_type=jnp.float32,
    )
    output = (middle + down_part).astype(jnp.bfloat16)
    grad_out = cotangent.astype(jnp.float32)
    columns = cotangent
    grad_hidden = contract_cols(
        columns, lax.all_gather(w_down, ("seq", "fsdp"), axis=1, tiled=True)
    )
    _, swiglu_pull = jax.vjp(swiglu, gate, up_part)
    grad_gate, grad_up = swiglu_pull(grad_hidden)
    grad_gate_b = grad_gate.astype(jnp.bfloat16)
    grad_up_b = grad_up.astype(jnp.bfloat16)
    blocks = lax.all_gather((w_gate, w_up), ("seq", "fsdp"), axis=0, tiled=True)
    grad_normed_two = contract_cols(grad_gate_b, blocks[0]) + contract_cols(grad_up_b, blocks[1])
    _, norm_two_pull = jax.vjp(scaled_norm, middle, gain_two)
    grad_middle_norm, grad_gain_two = norm_two_pull(grad_normed_two)
    grad_middle = grad_out + grad_middle_norm
    grad_branch_b = grad_middle.astype(jnp.bfloat16)
    paired_ffn = jnp.concatenate([grad_gate_b, grad_up_b], axis=1)
    left_rows = normed_two
    ffn_share = lax.psum_scatter(
        jnp.concatenate(
            [contract_rows(left_rows, paired_ffn), contract_rows(cotangent, hidden_b)], axis=1
        ),
        ("seq", "fsdp"),
        scatter_dimension=0,
        tiled=True,
    )
    w_gate_grad = ffn_share[:, :hidden_units]
    w_up_grad = ffn_share[:, hidden_units : 2 * hidden_units]
    w_down_grad = ffn_share[:, 2 * hidden_units :].T
    grad_attn_b = contract_cols(
        grad_branch_b, lax.all_gather(w_out, ("seq", "fsdp"), axis=0, tiled=True)
    ).astype(jnp.bfloat16)
    back_keys, back_values = (group_keys, group_values)
    back_key_heads, back_value_heads = split_heads(back_keys, back_values)
    grad_heads = grad_attn_b.reshape(tok_rows, kv_heads, group_ratio, head_size).transpose(
        1, 0, 2, 3
    )

    def head_backward(items):
        query_head, key_head, value_head, grad_head, log_total = items
        scores = masked_scores(query_head, key_head)
        softmax_weights = jnp.exp(scores - log_total)
        grad_weights = jnp.einsum(
            "trd,kd->trk", grad_head, value_head, preferred_element_type=jnp.float32
        )
        inner = jnp.sum(softmax_weights * grad_weights, axis=-1, keepdims=True)
        grad_scores = (softmax_weights * (grad_weights - inner)).astype(jnp.bfloat16)
        grad_query = (
            jnp.einsum("trk,kd->trd", grad_scores, key_head, preferred_element_type=jnp.float32)
            * scale
        )
        grad_key = (
            jnp.einsum("trk,trd->kd", grad_scores, query_head, preferred_element_type=jnp.float32)
            * scale
        )
        grad_value = jnp.einsum(
            "trk,trd->kd",
            softmax_weights.astype(jnp.bfloat16),
            grad_head,
            preferred_element_type=jnp.float32,
        )
        return (grad_query, grad_key, grad_value)

    grad_query_heads, grad_key_part, grad_value_part = lax.map(
        head_backward, (query_heads, back_key_heads, back_value_heads, grad_heads, log_totals)
    )
    grad_key_own, grad_value_own = (
        lax.psum_scatter(
            grad_key_part.astype(jnp.bfloat16), "seq", scatter_dimension=1, tiled=True
        ).astype(jnp.float32),
        lax.psum_scatter(
            grad_value_part.astype(jnp.bfloat16), "seq", scatter_dimension=1, tiled=True
        ).astype(jnp.float32),
    )
    grad_query_rot = grad_query_heads.transpose(1, 0, 2, 3).reshape(tok_rows, -1)
    grad_key_rot = grad_key_own.transpose(1, 0, 2).reshape(tok_rows, -1)
    grad_value_b = grad_value_own.transpose(1, 0, 2).reshape(tok_rows, -1).astype(jnp.bfloat16)
    _, query_pull = jax.vjp(
        lambda values, gain: head_prep(values, gain, own_position), query_raw, query_gain
    )
    grad_query_raw, grad_query_gain = query_pull(grad_query_rot)
    _, key_pull = jax.vjp(
        lambda values, gain: head_prep(values, gain, own_position), key_raw, key_gain
    )
    grad_key_raw, grad_key_gain = key_pull(grad_key_rot)
    grad_query_b = grad_query_raw.astype(jnp.bfloat16)
    grad_key_b = grad_key_raw.astype(jnp.bfloat16)
    paired_attn = jnp.concatenate([grad_query_b, grad_key_b, grad_value_b], axis=1)
    query_cols = grad_query_b.shape[1]
    key_cols = grad_key_b.shape[1]
    left_rows = normed_one
    attn_share = lax.psum_scatter(
        jnp.concatenate(
            [contract_rows(left_rows, paired_attn), contract_rows(attn_b, grad_branch_b)], axis=1
        ),
        ("seq", "fsdp"),
        scatter_dimension=0,
        tiled=True,
    )
    w_query_grad = attn_share[:, :query_cols]
    w_key_grad = attn_share[:, query_cols : query_cols + key_cols]
    w_value_grad = attn_share[:, query_cols + key_cols : query_cols + 2 * key_cols]
    w_out_grad = attn_share[:, query_cols + 2 * key_cols :]
    blocks = lax.all_gather((w_query, w_key, w_value), ("seq", "fsdp"), axis=0, tiled=True)
    grad_normed_one = (
        contract_cols(grad_query_b, blocks[0])
        + contract_cols(grad_key_b, blocks[1])
        + contract_cols(grad_value_b, blocks[2])
    )
    _, norm_one_pull = jax.vjp(scaled_norm, inputs, gain_one)
    grad_inputs_norm, grad_gain_one = norm_one_pull(grad_normed_one)
    input_grad = (grad_middle + grad_inputs_norm).astype(jnp.bfloat16)
    gain_one_grad, gain_two_grad, query_gain_grad, key_gain_grad = (
        lax.psum_scatter(grad_gain_one, ("seq", "fsdp"), scatter_dimension=0, tiled=True),
        lax.psum_scatter(grad_gain_two, ("seq", "fsdp"), scatter_dimension=0, tiled=True),
        lax.psum_scatter(grad_query_gain, ("seq", "fsdp"), scatter_dimension=0, tiled=True),
        lax.psum_scatter(grad_key_gain, ("seq", "fsdp"), scatter_dimension=0, tiled=True),
    )
    return (
        output,
        input_grad,
        gain_one_grad,
        w_query_grad,
        w_key_grad,
        w_value_grad,
        query_gain_grad,
        key_gain_grad,
        w_out_grad,
        gain_two_grad,
        w_gate_grad,
        w_up_grad,
        w_down_grad,
    )


def solution(mesh):
    return jax.shard_map(
        shards,
        mesh=mesh,
        in_specs=(
            P(("fsdp", "seq"), None),
            P("fsdp", None),
            P("fsdp", None),
            P("fsdp", None),
            P(("seq", "fsdp")),
            P(("seq", "fsdp"), None),
            P(("seq", "fsdp"), None),
            P(("seq", "fsdp"), None),
            P(("seq", "fsdp")),
            P(("seq", "fsdp")),
            P(("seq", "fsdp"), None),
            P(("seq", "fsdp")),
            P(("seq", "fsdp"), None),
            P(("seq", "fsdp"), None),
            P(None, ("seq", "fsdp")),
            P(("fsdp", "seq"), None),
        ),
        out_specs=(
            P(("fsdp", "seq"), None),
            P(("fsdp", "seq"), None),
            P(("seq", "fsdp")),
            P(("seq", "fsdp"), None),
            P(("seq", "fsdp"), None),
            P(("seq", "fsdp"), None),
            P(("seq", "fsdp")),
            P(("seq", "fsdp")),
            P(("seq", "fsdp"), None),
            P(("seq", "fsdp")),
            P(("seq", "fsdp"), None),
            P(("seq", "fsdp"), None),
            P(None, ("seq", "fsdp")),
        ),
        check_vma=False,
    )
```

profile of v0, /device:TPU:0, one launch (start us, length us, event | category | flops | bytes accessed | tf_op | source)
XLA Modules:
  0.0 2848.3 jit_solution(6867857408194109752)
XLA Ops:
  12.1 42.2 %all-reduce.13 = (bf16[128]{0:T(256)(128)(2,1)S(1)}, bf16[2048]{0:T(1024)(128)(2,1)S(1)}, bf16[128]{0:T(256)(128)(2,1)S(1)}, bf16[2048]{0:T(1024)(128)(2,1)S(1)}) all-reduce(bf16[128]{0:T(256)(128)(2,1)S(1)} %dynamic-update-slice.1, bf16[2048]{0:T(1024)(128)(2,1)S(1)} %dynamic-update-slice, ...), channel_id=1, replica_groups=mesh['seq'=4,'fsdp'=8] {'seq','fsdp'}, use_global_device_ids=true, to_apply=%add.5 | all-reduce | flops 4352 | bytes 17408
  60.1 16.1 all-gather.12.cloned.1.call-done
  76.2 3.8 convolution_bitcast_fusion.5
  82.5 57.2 %all-gather.16.cloned.1.call-done = bf16[2048,1024]{1,0:T(8,128)(2,1)} async-done(((bf16[64,1024]{1,0:T(8,128)(2,1)}), bf16[2048,1024]{1,0:T(8,128)(2,1)}) %all-gather.16.cloned.1.call-update) | async-done | bytes 4194320 | tf_op jit(solution)/shard_map/all_gather | solution.py:109
  139.7 4.3 convolution_convert_fusion.1
  151.1 24.8 all-gather.14.cloned.1.call-done
  175.9 4.0 copy.169
  179.8 33.7 %all-gather.18.cloned.1.call-done = bf16[1024,1024]{1,0:T(8,128)(2,1)} async-done(((bf16[256,1024]{1,0:T(8,128)(2,1)}), bf16[1024,1024]{1,0:T(8,128)(2,1)}) %all-gather.18.cloned.1.call-update) | async-done | bytes 2097168 | tf_op jit(solution)/shard_map/all_gather | solution.py:135
  213.5 3.3 bitcast_bitcast_fusion
  216.8 77.0 %all-gather.10.cloned.1.call-done = bf16[2048,2048]{1,0:T(8,128)(2,1)} async-done(((bf16[64,2048]{1,0:T(8,128)(2,1)}), bf16[2048,2048]{1,0:T(8,128)(2,1)}) %all-gather.10.cloned.1.call-update) | async-done | bytes 8388624 | tf_op jit(solution)/shard_map/all_gather | solution.py:107
  293.8 5.7 convolution_bitcast_fusion.4
  307.4 48.6 %while.28 = (s32[]{:T(128)}, bf16[8,256,2,128]{1,3,2,0:T(8,128)(2,1)}, f32[8,256,2,1]{1,2,3,0:T(2,128)}, bf16[8,256,2,128]{3,1,2,0:T(8,128)(2,1)}, bf16[8,1024,1...) while((s32[]{:T(128)}, ...), condition=%wide.region_7.8_spmd.clone, body=%wide.region_4.7_spmd.clone.sunk | while | flops 273677824 | bytes 7763337 | solution.py:165
  347.8 2.2 fusion.145
  356.1 16.6 all-gather.20.cloned.1.call-done
  372.7 6.2 multiply_reduce_fusion.5
  380.5 148.5 %all-gather.24.cloned.1.call-done = bf16[2048,6144]{1,0:T(8,128)(2,1)} async-done(((bf16[64,6144]{1,0:T(8,128)(2,1)}), bf16[2048,6144]{1,0:T(8,128)(2,1)}) %all-gather.24.cloned.1.call-update) | async-done | bytes 25165840 | tf_op jit(solution)/shard_map/all_gather | solution.py:178
  529.0 14.5 fusion.92
  543.4 141.4 %all-gather.22.cloned.1.call-done = bf16[2048,6144]{1,0:T(8,128)(2,1)} async-done(((bf16[64,6144]{1,0:T(8,128)(2,1)}), bf16[2048,6144]{1,0:T(8,128)(2,1)}) %all-gather.22.cloned.1.call-update) | async-done | bytes 25165840 | tf_op jit(solution)/shard_map/all_gather | solution.py:177
  684.9 14.3 fusion.91
  699.2 141.6 %all-gather.26.cloned.1.call-done = bf16[6144,2048]{0,1:T(8,128)(2,1)} async-done(((bf16[6144,64]{0,1:T(8,128)(2,1)}), bf16[6144,2048]{0,1:T(8,128)(2,1)}) %all-gather.26.cloned.1.call-update) | async-done | bytes 25165840 | tf_op jit(solution)/shard_map/all_gather | solution.py:186
  840.8 18.7 multiply_convert_fusion.1
  859.5 14.0 fusion.93
  873.5 15.6 multiply_reduce_fusion.1
  889.1 2.8 fusion.58
  893.2 6.7 convolution_convert_fusion
  903.0 108.2 %while.29 = (s32[]{:T(128)}, f32[8,256,2,128]{3,1,2,0:T(8,128)}, bf16[8,1024,128]{1,2,0:T(8,128)(2,1)}, bf16[8,1024,128]{1,2,0:T(8,128)(2,1)}, bf16[8,256,2,128]...) while((s32[]{:T(128)}, f32[8,256,2,128]{3,1,2,0:T(8,128)}, ...), condition=%wide.region_12.13_spmd.clone, body=%wide.region_10.12_spmd.clone.sunk | while | flops 677707264 | bytes 19686824 | solution.py:252
  1012.1 3.0 fusion.87
  1015.1 2.6 multiply_add_fusion.1
  1017.7 2.9 multiply_reduce_fusion.2
  1020.9 4.1 fusion.59
  1027.3 8.1 fusion.71
  1035.4 9.4 reduce-scatter.5.cloned.1.call-done
  1047.6 35.7 %reduce-scatter.7.cloned.1.call-done = bf16[8,256,128]{1,2,0:T(8,128)(2,1)} async-done(((bf16[8,1024,128]{1,2,0:T(8,128)(2,1)}), bf16[8,256,128]{1,2,0:T(8,128)(2,1)}) %reduce-scatter.7.cloned.1.call-update) | async-done | bytes 524304 | tf_op jit(solution)/shard_map/reduce_scatter | solution.py:259
  1085.3 14.3 fusion.64
  1099.6 33.6 %pad_maximum_fusion.1 = f32[2048,6144]{1,0:T(8,128)} fusion(f32[2048,2048]{1,0:T(8,128)} %fusion.71, f32[2048,4096]{1,0:T(8,128)} %fusion.64), kind=kLoop, calls=%fused_computation.60 | loop fusion | flops 12582912 | bytes 100663296 | tf_op jit(solution)/shard_map/concatenate | solution.py:281
  1134.5 32.4 %convolution_bitcast_fusion.3 = f32[2048,6144]{1,0:T(8,128)} fusion(bf16[256,6144]{1,0:T(8,128)(2,1)} %get-tuple-element.422, bf16[256,2048]{1,0:T(8,128)(2,1)S(1)} %copy-done.22), kind=kOutput, calls=%fused_computation.61 | convolution fusion | flops 6442450944 | bytes 54525952 | tf_op jit(solution)/shard_map/dot_general | solution.py:57
  1166.9 50.1 %fusion.48 = f32[2048,12288]{1,0:T(8,128)} fusion(bf16[256,2048]{1,0:T(8,128)(2,1)S(1)} %copy-done.16, bf16[256,6144]{1,0:T(8,128)(2,1)} %get-tuple-element.420, bf16[256,6144]{1,0:T(8,128)(2,1)} %get-tuple-element.421), kind=kOutput, calls=%fused_computation.66 | convolution fusion | flops 12897484800 | bytes 108003328 | tf_op jit(solution)/shard_map/dot_general | solution.py:57
  1217.0 100.7 %pad_maximum_fusion = f32[2048,18432]{1,0:T(8,128)} fusion(f32[2048,6144]{1,0:T(8,128)} %convolution_bitcast_fusion.3, f32[2048,12288]{1,0:T(8,128)} %fusion.48), kind=kLoop, calls=%fused_computation.59 | loop fusion | flops 37748736 | bytes 301989888 | tf_op jit(solution)/shard_map/concatenate | solution.py:208
  1319.0 7.2 fusion.81
  1326.3 13.9 fusion.53
  1340.2 4.4 convolution_add_fusion.3
  1344.8 2.9 fusion.57
  1347.7 40.9 %all-reduce.12 = (f32[2048]{0:T(1024)S(1)}, f32[128]{0:T(128)S(1)}, f32[128]{0:T(128)S(1)}, f32[2048]{0:T(1024)S(1)}) all-reduce(f32[2048]{0:T(1024)S(1)} %get-tuple-element.346, f32[128]{0:T(128)S(1)} %copy-done.50, f32[128]{0:T(128)S(1)} %copy-done.51, f32[2048]{0:T(1024)S(1)} %copy-done.46), channel_id=4, replica_groups=mesh['seq'=4,'fsdp'=8] {'seq','fsdp'}, use_global_device_ids=true, to_apply=%region_19.20.clone | all-reduce | flops 4352 | bytes 34816
  1391.0 3.2 fusion.61
  1394.1 172.1 %reduce-scatter.9.cloned.1.call-done = f32[64,6144]{1,0:T(8,128)} async-done(((f32[2048,6144]{1,0:T(8,128)}), f32[64,6144]{1,0:T(8,128)}) %reduce-scatter.9.cloned.1.call-update) | async-done | bytes 1572880 | tf_op jit(solution)/shard_map/reduce_scatter | solution.py:280
  1568.1 2.3 fusion.88
  1570.4 1266.2 %reduce-scatter.11.cloned.1.call-done = f32[64,18432]{1,0:T(8,128)} async-done(((f32[2048,18432]{1,0:T(8,128)}), f32[64,18432]{1,0:T(8,128)}) %reduce-scatter.11.cloned.1.call-update) | async-done | bytes 4718608 | tf_op jit(solution)/shard_map/reduce_scatter | solution.py:207
  2836.6 4.6 slice_bitcast_fusion
  (326 shorter events, 201.4 us)
Async XLA Ops:
  7.2 69.0 %all-gather.12.cloned.1.call-start = ((), (), s32[]{:S(2)}) async-start(), calls=%async_computation.5 | async-start | bytes 4325376 | tf_op jit(solution)/shard_map/all_gather | solution.py:108
  7.9 131.8 %all-gather.16.cloned.1.call-start = ((), (), s32[]{:S(2)}) async-start(), calls=%async_computation.7 | async-start | bytes 4325376 | tf_op jit(solution)/shard_map/all_gather | solution.py:109
  8.7 167.2 %all-gather.14.cloned.1.call-start = ((), (), s32[]{:S(2)}) async-start(), calls=%async_computation.6 | async-start | bytes 2621440 | tf_op jit(solution)/shard_map/all_gather | solution.py:134
  54.3 26.8 copy-start.48
  54.3 239.4 %copy-start.32 = (f32[2048]{0:T(1024)}, f32[2048]{0:T(1024)S(1)}, u32[]{:S(2)}) copy-start(f32[2048]{0:T(1024)S(1)} %convert_element_type.125) | copy-start | bytes 24580
  59.8 234.0 %copy-start.38 = (f32[256]{0:T(256)}, f32[256]{0:T(256)S(1)}, u32[]{:S(2)}) copy-start(f32[256]{0:T(256)S(1)} %fusion.77) | copy-start | bytes 3076
  60.1 87.6 %copy-start.28 = (f32[256,64]{0,1:T(8,128)}, f32[256,64]{0,1:T(8,128)S(1)}, u32[]{:S(2)}) copy-start(f32[256,64]{0,1:T(8,128)S(1)} %get-tuple-element.440) | copy-start | bytes 196612
  60.1 87.7 %copy-start.30 = (f32[256,64]{0,1:T(8,128)}, f32[256,64]{0,1:T(8,128)S(1)}, u32[]{:S(2)}) copy-start(f32[256,64]{0,1:T(8,128)S(1)} %get-tuple-element.441) | copy-start | bytes 196612
  81.3 58.4 %copy-start = (bf16[256,2048]{1,0:T(8,128)(2,1)S(1)}, bf16[256,2048]{1,0:T(8,128)(2,1)}, u32[]{:S(2)}) copy-start(bf16[256,2048]{1,0:T(8,128)(2,1)} %param.20) | copy-start | bytes 3145732
  82.5 131.0 %all-gather.18.cloned.1.call-start = ((), (), s32[]{:S(2)}) async-start(), calls=%async_computation.8 | async-start | bytes 2621440 | tf_op jit(solution)/shard_map/all_gather | solution.py:135
  144.0 6.4 copy-start.52
  144.0 6.4 copy-start.53
  144.0 149.7 %all-gather.10.cloned.1.call-start = ((), (), s32[]{:S(2)}) async-start(), calls=%async_computation.4 | async-start | bytes 8650752 | tf_op jit(solution)/shard_map/all_gather | solution.py:107
  144.6 228.1 %all-gather.20.cloned.1.call-start = ((), (), s32[]{:S(2)}) async-start(), calls=%async_computation.9 | async-start | bytes 8650752 | tf_op jit(solution)/shard_map/all_gather | solution.py:170
  145.2 383.8 %all-gather.24.cloned.1.call-start = ((), (), s32[]{:S(2)}) async-start(), calls=%async_computation.11 | async-start | bytes 25952256 | tf_op jit(solution)/shard_map/all_gather | solution.py:178
  145.9 538.9 %all-gather.22.cloned.1.call-start = ((), (), s32[]{:S(2)}) async-start(), calls=%async_computation.10 | async-start | bytes 25952256 | tf_op jit(solution)/shard_map/all_gather | solution.py:177
  146.7 694.1 %all-gather.26.cloned.1.call-start = ((), (), s32[]{:S(2)}) async-start(), calls=%async_computation.12 | async-start | bytes 25952256 | tf_op jit(solution)/shard_map/all_gather | solution.py:186
  147.4 897.4 %reduce-scatter.5.cloned.1.call-start = ((), (), s32[]{:S(2)}) async-start(), calls=%async_computation.13 | async-start | bytes 2621440 | tf_op jit(solution)/shard_map/reduce_scatter | solution.py:256
  147.8 157.0 %copy-start.24 = (f32[256,64]{1,0:T(8,128)}, f32[256,64]{1,0:T(8,128)S(1)}, u32[]{:S(2)}) copy-start(f32[256,64]{1,0:T(8,128)S(1)} %copy.163) | copy-start | bytes 196612
  147.9 156.9 %copy-start.26 = (f32[256,64]{1,0:T(8,128)}, f32[256,64]{1,0:T(8,128)S(1)}, u32[]{:S(2)}) copy-start(f32[256,64]{1,0:T(8,128)S(1)} %copy.164) | copy-start | bytes 196612
  372.7 7.6 copy-start.41
  380.5 304.4 %copy-start.15 = (bf16[256,2048]{1,0:T(8,128)(2,1)}, bf16[256,2048]{1,0:T(8,128)(2,1)S(1)}, u32[]{:S(2)}) copy-start(bf16[256,2048]{1,0:T(8,128)(2,1)S(1)} %multiply_convert_fusion.3) | copy-start | bytes 3145732
  873.5 15.6 copy-start.21
  1011.3 72.0 %reduce-scatter.7.cloned.1.call-start = ((), (), s32[]{:S(2)}) async-start(), calls=%async_computation.14 | async-start | bytes 2621440 | tf_op jit(solution)/shard_map/reduce_scatter | solution.py:259
  1012.0 554.2 %reduce-scatter.9.cloned.1.call-start = ((), (), s32[]{:S(2)}) async-start(), calls=%async_computation.15 | async-start | bytes 51904512 | tf_op jit(solution)/shard_map/reduce_scatter | solution.py:280
  1012.0 3.0 copy-start.25
  1020.9 6.4 copy-start.12
  1027.2 18.7 copy-start.29
  1027.3 18.7 copy-start.31
  1035.4 10.7 copy-start.11
  1035.4 10.7 copy-start.37
  1035.4 10.8 copy-start.49
  1047.0 38.3 %copy-start.1 = (bf16[256,2048]{1,0:T(8,128)(2,1)S(1)}, bf16[256,2048]{1,0:T(8,128)(2,1)}, u32[]{:S(2)}) copy-start(bf16[256,2048]{1,0:T(8,128)(2,1)} %param.20) | copy-start | bytes 3145732
  1047.0 38.3 %copy-start.33 = (f32[2048]{0:T(1024)S(1)}, f32[2048]{0:T(1024)}, u32[]{:S(2)}) copy-start(f32[2048]{0:T(1024)} %copy-done.32) | copy-start | bytes 24580
  1047.0 38.3 %copy-start.39 = (f32[256]{0:T(256)S(1)}, f32[256]{0:T(256)}, u32[]{:S(2)}) copy-start(f32[256]{0:T(256)} %copy-done.38) | copy-start | bytes 3076
  1047.3 52.3 %copy-start.13 = (bf16[256,8,128]{0,2,1:T(8,128)(2,1)}, bf16[256,8,128]{0,2,1:T(8,128)(2,1)S(1)}, u32[]{:S(2)}) copy-start(bf16[256,8,128]{0,2,1:T(8,128)(2,1)S(1)} %fusion.70) | copy-start | bytes 1572868
  1047.3 38.0 %copy-start.17 = (bf16[32,8,16,128]{3,1,2,0:T(8,128)(2,1)S(1)}, bf16[32,8,16,128]{3,1,2,0:T(8,128)(2,1)}, u32[]{:S(2)}) copy-start(bf16[32,8,16,128]{3,1,2,0:T(8,128)(2,1)} %copy.225) | copy-start | bytes 3145732
  1133.3 1703.3 %reduce-scatter.11.cloned.1.call-start = ((), (), s32[]{:S(2)}) async-start(), calls=%async_computation.16 | async-start | bytes 155713536 | tf_op jit(solution)/shard_map/reduce_scatter | solution.py:207
  1134.5 32.4 %copy-start.16 = (bf16[256,2048]{1,0:T(8,128)(2,1)S(1)}, bf16[256,2048]{1,0:T(8,128)(2,1)}, u32[]{:S(2)}) copy-start(bf16[256,2048]{1,0:T(8,128)(2,1)} %copy-done.15) | copy-start | bytes 3145732
  1319.0 7.3 copy-start.7
  1326.3 13.9 copy-start.14
  1340.2 4.5 copy-start.2
  1340.2 4.5 copy-start.18
  1340.2 4.6 copy-start.23
  1340.2 4.5 copy-start.34
  1340.2 4.5 copy-start.40
  1344.8 46.2 %copy-start.45 = (f32[256]{0:T(256)S(1)}, f32[256]{0:T(256)}, u32[]{:S(2)}) copy-start(f32[256]{0:T(256)} %copy-done.44) | copy-start | bytes 3076
  1344.8 46.2 %copy-start.5 = (f32[256,2048]{1,0:T(8,128)S(1)}, f32[256,2048]{1,0:T(8,128)}, u32[]{:S(2)}) copy-start(f32[256,2048]{1,0:T(8,128)} %copy-done.3) | copy-start | bytes 6291460
  (19 other events, 37.2 us)
Sparse Core Ops, SparseCore 0:
  11.0 65.1 all-gather.11
  79.2 60.4 all-gather.15
  142.1 33.7 all-gather.13
  178.1 35.3 all-gather.17
  216.3 77.3 all-gather.9
  296.6 76.0 all-gather.19
  375.7 153.2 all-gather.23
  532.0 152.8 all-gather.21
  687.9 152.8 all-gather.25
  1011.4 33.3 reduce-scatter.4
  1048.0 35.1 reduce-scatter.6
  1133.4 432.7 reduce-scatter.8
  1572.7 1263.8 reduce-scatter.10
where the time goes:
time: 2860 us; the launch traced here: 2850 us
  waiting for transfers between devices  2150 us (75%)
  matrix products  345 us (12%)
  other arithmetic  194 us (7%)
  blocking collectives  83 us (3%)
  local copies, waits for them, and re-layouts  63.6 us (2%)
    reduce_scatter x1, waiting for transfers between devices, shards(): lax.psum_scatter(jnp.concatenate([contract_rows(left_rows, paired_ffn), c...  1270 us
    reduce_scatter x1, waiting for transfers between devices, shards(): lax.psum_scatter(jnp.concatenate([contract_rows(left_rows, paired_attn),...  172 us
    all_gather x1, waiting for transfers between devices, shards(): lax.all_gather(w_up, ('seq', 'fsdp'), axis=0, tiled=True)  148 us
    all_gather x1, waiting for transfers between devices, shards(): lax.all_gather(w_down, ('seq', 'fsdp'), axis=1, tiled=True)  142 us
    all_gather x1, waiting for transfers between devices, shards(): lax.all_gather(w_gate, ('seq', 'fsdp'), axis=0, tiled=True)  141 us
    dot_general x4, matrix products, contract_rows(): lax.dot_general(left_rows, right_rows, (((0,), (0,)), ((), ())), preferre...  105 us
    concatenate x1, other arithmetic, shards(): jnp.concatenate([contract_rows(left_rows, paired_ffn), contract_rows(cota...  101 us
    unnamed x2, blocking collectives  83 us
  transfers between devices with their start and end apart: 13, of which 13 were waited for; matrix products, arithmetic and copies ran while one was open for 13% of the time, Pallas kernels for 0%

commit v1 on v0

v1 whole, which is shorter than its diff:
```python
import functools

import jax
import jax.numpy as jnp
from jax import lax
from jax.experimental import pallas as pl
from jax.experimental.pallas import tpu as pltpu
from jax.sharding import PartitionSpec as P

epsilon = 1e-06
theta = 1000000.0
masked_score = -1e30
log2e = 1.4426950408889634

MESH = pl.DeviceIdType.MESH
ANY = pl.BlockSpec(memory_space=pl.ANY)
VMEM = pl.BlockSpec(memory_space=pltpu.VMEM)
BF = jnp.bfloat16
F32 = jnp.float32
LIMIT = 60 * 1024 * 1024


def dot(a, b):
    return jnp.dot(a, b, preferred_element_type=F32)


def dot_nt(a, b):
    return lax.dot_general(a, b, (((1,), (1,)), ((), ())), preferred_element_type=F32)


def dot_tn(a, b):
    return lax.dot_general(a, b, (((0,), (0,)), ((), ())), preferred_element_type=F32)


def shape(dims, dtype):
    return jax.ShapeDtypeStruct(dims, dtype)


def comm_params(number):
    return pltpu.CompilerParams(
        collective_id=number, has_side_effects=True, vmem_limit_bytes=LIMIT
    )


def plain_params():
    return pltpu.CompilerParams(vmem_limit_bytes=LIMIT)


def remote(src, dst, send, recv, axis, index):
    return pltpu.make_async_remote_copy(
        src_ref=src,
        dst_ref=dst,
        send_sem=send,
        recv_sem=recv,
        device_id={axis: index},
        device_id_type=MESH,
    )


def greet(places):
    barrier = pltpu.get_barrier_semaphore()
    for axis, index in places:
        pl.semaphore_signal(barrier, inc=1, device_id={axis: index}, device_id_type=MESH)
    pl.semaphore_wait(barrier, len(places))


def others(axis, n):
    me = lax.axis_index(axis)
    return [(axis, lax.rem(me + j, n)) for j in range(1, n)]


def square(me):
    return me + 1 - 2 * lax.rem(me, 2), lax.rem(me + 2, 4), 3 - me


def ring_places(n):
    me = lax.axis_index("seq")
    if n == 4:
        across, along, _ = square(me)
        return [("seq", across), ("seq", along)]
    return others("seq", n)


def gather_copies(n):
    return 6 if n == 4 else n - 1


def gather(n, own, out, send, recv, local):
    me = lax.axis_index("seq")
    keep = pltpu.make_async_copy(own, out.at[me], local)
    keep.start()
    if n == 4:
        across, along, _ = square(me)
        half = own.shape[0] // 2
        low, high = pl.ds(0, half), pl.ds(half, half)

        def piece(number, rows, to):
            return remote(
                own.at[rows], out.at[me, rows], send.at[number], recv.at[number], "seq", to
            )

        first = [
            piece(0, low, across),
            piece(1, high, along),
            piece(2, high, across),
            piece(3, low, along),
        ]
        for copy in first:
            copy.start()
        first[0].wait_recv()
        on_a = remote(
            out.at[across, low], out.at[across, low], send.at[4], recv.at[4], "seq", along
        )
        on_a.start()
        first[1].wait_recv()
        on_b = remote(
            out.at[along, high], out.at[along, high], send.at[5], recv.at[5], "seq", across
        )
        on_b.start()
        first[2].wait_recv()
        first[3].wait_recv()
        on_a.wait_recv()
        on_b.wait_recv()
        for copy in first + [on_a, on_b]:
            copy.wait_send()
    else:
        copies = []
        for j in range(1, n):
            to = lax.rem(me + j, n)
            copies.append(
                remote(own, out.at[me], send.at[j - 1], recv.at[j - 1], "seq", to)
            )
        for copy in copies:
            copy.start()
        for copy in copies:
            copy.wait()
    keep.wait()


def scatter_slots(n):
    return 4 if n == 4 else n - 1


def scatter_sum(n, part, slots, stage, send, recv, finish):
    me = lax.axis_index("seq")
    rows = part.shape[1]
    if n == 4:
        across, along, corner = square(me)
        half = rows // 2
        low, high = pl.ds(0, half), pl.ds(half, half)
        c0 = remote(part.at[corner, low], slots.at[2, low], send.at[0], recv.at[0], "seq", along)
        c1 = remote(part.at[corner, high], slots.at[2, high], send.at[1], recv.at[1], "seq", across)
        c2 = remote(part.at[across, high], slots.at[0, high], send.at[2], recv.at[2], "seq", across)
        c3 = remote(part.at[along, low], slots.at[1, low], send.at[3], recv.at[3], "seq", along)
        c4 = remote(stage.at[low], slots.at[0, low], send.at[4], recv.at[4], "seq", across)
        c5 = remote(stage.at[high], slots.at[1, high], send.at[5], recv.at[5], "seq", along)
        for copy in (c0, c1, c2, c3):
            copy.start()
        c0.wait_recv()
        stage[low] = (
            part[across, low].astype(F32) + slots[2, low].astype(F32)
        ).astype(BF)
        c4.start()
        c1.wait_recv()
        stage[high] = (
            part[along, high].astype(F32) + slots[2, high].astype(F32)
        ).astype(BF)
        c5.start()
        for copy in (c2, c3, c4, c5):
            copy.wait_recv()
        copies = (c0, c1, c2, c3, c4, c5)
        count = 2
    else:
        copies = []
        for j in range(1, n):
            to = lax.rem(me + j, n)
            copies.append(
                remote(part.at[to], slots.at[j - 1], send.at[j - 1], recv.at[j - 1], "seq", to)
            )
        for copy in copies:
            copy.start()
        for copy in copies:
            copy.wait_recv()
        count = n - 1
    step = 32

    def chunk(number, carry):
        at = pl.ds(pl.multiple_of(number * step, step), step)
        total = part[me, at].astype(F32)
        for slot in range(count):
            total += slots[slot, at].astype(F32)
        finish(at, total)
        return carry

    lax.fori_loop(0, rows // step, chunk, 0)
    for copy in copies:
        copy.wait_send()


def inverse_rms(values):
    return lax.rsqrt(jnp.mean(values * values, axis=-1, keepdims=True) + epsilon)


def norm_back(values, gain, grad):
    inverse = inverse_rms(values)
    scaled = grad * gain
    back = inverse * scaled - values * (
        inverse * inverse * inverse * jnp.mean(scaled * values, axis=-1, keepdims=True)
    )
    return back, jnp.sum(grad * values * inverse, axis=0, keepdims=True)


def attention_weights_out(n, nf, wq, wk, wv, gains, out, all_gains, seen, send, recv, gsend, grecv, local):
    me, spot = lax.axis_index("seq"), lax.axis_index("fsdp")
    greet(others("seq", n) + others("fsdp", nf))
    widths = [wq.shape[1] // n, wk.shape[1] // n, wv.shape[1] // n]
    begins = [0, widths[0], widths[0] + widths[1]]
    copies = []
    small = []
    for j in range(1, n):
        to = lax.rem(me + j, n)
        copy = remote(gains, seen.at[me], gsend.at[j - 1], grecv.at[j - 1], "seq", to)
        copy.start()
        small.append(copy)
        for i, ref in enumerate((wq, wk, wv)):
            columns = pl.ds(pl.multiple_of(to * widths[i], 128), widths[i])
            copies.append(
                remote(
                    ref.at[:, columns],
                    out.at[me, :, pl.ds(begins[i], widths[i])],
                    send.at[3 * j - 3 + i],
                    recv.at[3 * j - 3 + i],
                    "seq",
                    to,
                )
            )
    for copy in copies:
        copy.start()
    keeps = []
    for i, ref in enumerate((wq, wk, wv)):
        columns = pl.ds(pl.multiple_of(me * widths[i], 128), widths[i])
        keeps.append(
            pltpu.make_async_copy(
                ref.at[:, columns], out.at[me, :, pl.ds(begins[i], widths[i])], local.at[i]
            )
        )
    keeps.append(pltpu.make_async_copy(gains, seen.at[me], local.at[3]))
    for keep in keeps:
        keep.start()
    keeps[3].wait()
    for copy in small:
        copy.wait()
    last = pltpu.make_async_copy(seen, all_gains.at[spot], local.at[4])
    last.start()
    wide = []
    for j in range(1, nf):
        to = lax.rem(spot + j, nf)
        copy = remote(
            seen, all_gains.at[spot], gsend.at[n + j - 2], grecv.at[n + j - 2], "fsdp", to
        )
        copy.start()
        wide.append(copy)
    for copy in copies + wide:
        copy.wait()
    for keep in keeps[:3] + [last]:
        keep.wait()


def hidden_weights_out(n, x, wg, wu, wd, xg, gu, dn, send, recv, asend, arecv, local):
    me = lax.axis_index("seq")
    greet(others("seq", n))
    width = wg.shape[1] // n
    copies, keeps = [], []
    views = [(wg, gu, 0), (wu, gu, 1), (wd, dn, 0)]
    for i, (ref, out, place) in enumerate(views):
        for j in range(1, n):
            to = lax.rem(me + j, n)
            columns = pl.ds(pl.multiple_of(to * width, 128), width)
            k = i * (n - 1) + j - 1
            copies.append(
                remote(
                    ref.at[:, columns],
                    out.at[me, :, pl.ds(place * width, width)],
                    send.at[k],
                    recv.at[k],
                    "seq",
                    to,
                )
            )
        columns = pl.ds(pl.multiple_of(me * width, 128), width)
        keeps.append(
            pltpu.make_async_copy(
                ref.at[:, columns], out.at[me, :, pl.ds(place * width, width)], local.at[i]
            )
        )
    for copy in copies:
        copy.start()
    for keep in keeps:
        keep.start()
    gather(n, x, xg, asend, arecv, local.at[3])
    for copy in copies:
        copy.wait()
    for keep in keeps:
        keep.wait()


def gather_alone(n, x, out, send, recv, local):
    greet(ring_places(n))
    gather(n, x, out, send, recv, local)


def project(x_ref, gain_ref, w_ref, gq_ref, gk_ref, cos_ref, sin_ref, n1_ref, qraw_ref, kraw_ref, q_ref, k_ref, v_ref, kt_ref, vt_ref):
    x = x_ref[...].astype(F32)
    normed = (x * inverse_rms(x) * gain_ref[...]).astype(BF)
    n1_ref[...] = normed
    full = dot(normed, w_ref[...])
    qw, kw = q_ref.shape[1], k_ref.shape[1]
    cos, sin = cos_ref[...], sin_ref[...]

    def prep(head, gain):
        u = head * inverse_rms(head) * gain
        return u * cos + pltpu.roll(u, 64, 1) * sin

    qraw_ref[...] = full[:, :qw]
    kraw_ref[...] = full[:, qw : qw + kw]
    v = full[:, qw + kw :]
    v_ref[...] = v.astype(BF)
    vt_ref[...] = v.T.astype(BF)
    for h in range(qw // 128):
        q_ref[:, h * 128 : h * 128 + 128] = prep(
            full[:, h * 128 : h * 128 + 128], gq_ref[...]
        ).astype(BF)
    for h in range(kw // 128):
        turned = prep(full[:, qw + h * 128 : qw + h * 128 + 128], gk_ref[...])
        k_ref[:, h * 128 : h * 128 + 128] = turned.astype(BF)
        kt_ref[h * 128 : h * 128 + 128, :] = turned.T.astype(BF)


def bias_of(low_ref, high_ref, keys):
    key = lax.broadcasted_iota(jnp.int32, (keys, low_ref.shape[1]), 0)
    fine = (key >= low_ref[0:1, :]) & (key <= high_ref[0:1, :])
    return jnp.where(fine, 0.0, masked_score)


def attend(q_ref, k_ref, vt_ref, wo_ref, low_ref, high_ref, attn_ref, lse_ref, part_ref, bias):
    keys = k_ref.shape[0]
    bias[...] = bias_of(low_ref, high_ref, keys)
    heads = q_ref.shape[1] // 128
    ratio = heads // (k_ref.shape[1] // 128)
    factor = 128 ** (-0.5) * log2e
    for h in range(heads):
        kv = h // ratio
        scores = dot_nt(
            k_ref[:, kv * 128 : kv * 128 + 128], q_ref[:, h * 128 : h * 128 + 128]
        )
        scores = scores * factor + bias[...]
        top = jnp.max(scores, axis=0, keepdims=True)
        probs = jnp.exp2(scores - top)
        total = jnp.sum(probs, axis=0, keepdims=True)
        mixed = dot(vt_ref[kv * 128 : kv * 128 + 128, :], probs.astype(BF))
        lse_ref[h : h + 1, :] = top + jnp.log2(total)
        attn_ref[:, h * 128 : h * 128 + 128] = (mixed / total).T.astype(BF)
    part_ref[...] = dot(attn_ref[...], wo_ref[...]).astype(BF)


def middle_stage(n, part, x, gain, x2, n2, slots, stage, own, send, recv, asend, arecv, local):
    greet(ring_places(n))

    def finish(at, total):
        value = x[at].astype(F32) + total
        x2[at] = value
        own[at] = (value * inverse_rms(value) * gain[...]).astype(BF)

    scatter_sum(n, part, slots, stage, send, recv, finish)
    gather(n, own, n2, asend, arecv, local)


def ffn_forward(n2_ref, wg_ref, wu_ref, gate_ref, up_ref, hidden_ref):
    gate = dot(n2_ref[...], wg_ref[...])
    up = dot(n2_ref[...], wu_ref[...])
    gate_ref[...] = gate
    up_ref[...] = up
    hidden_ref[...] = (gate * jax.nn.sigmoid(gate) * up).astype(BF)


def ffn_back(cot_ref, wd_ref, gate_ref, up_ref, dgate_ref, dup_ref):
    dh = dot(cot_ref[...], wd_ref[...])
    gate = gate_ref[...]
    s = jax.nn.sigmoid(gate)
    dgate_ref[...] = (dh * up_ref[...] * (s * (1.0 + gate * (1.0 - s)))).astype(BF)
    dup_ref[...] = (dh * (gate * s)).astype(BF)


def two_nt(a_ref, b_ref, wa_ref, wb_ref, out_ref):
    out_ref[...] = (dot_nt(a_ref[...], wa_ref[...]) + dot_nt(b_ref[...], wb_ref[...])).astype(BF)


def one_nt(a_ref, w_ref, out_ref):
    out_ref[...] = dot_nt(a_ref[...], w_ref[...]).astype(BF)


def back_stage(n, part, x2, cot, gain, dx2, dz, dgain, slots, stage, own, send, recv, asend, arecv, local):
    greet(ring_places(n))
    dgain[...] = jnp.zeros_like(dgain)

    def finish(at, total):
        back, dg = norm_back(x2[at], gain[...], total)
        value = cot[at].astype(F32) + back
        dx2[at] = value
        own[at] = value.astype(BF)
        dgain[0:1] += dg

    scatter_sum(n, part, slots, stage, send, recv, finish)
    gather(n, own, dz, asend, arecv, local)


def out_stage(n, part, x2, out, slots, stage, send, recv):
    greet(ring_places(n))

    def finish(at, total):
        out[at] = (x2[at] + total).astype(BF)

    scatter_sum(n, part, slots, stage, send, recv, finish)


def input_stage(n, part, x, dx2, gain, out, dgain, slots, stage, send, recv):
    greet(ring_places(n))
    dgain[...] = jnp.zeros_like(dgain)

    def finish(at, total):
        back, dg = norm_back(x[at].astype(F32), gain[...], total)
        out[at] = (dx2[at] + back).astype(BF)
        dgain[0:1] += dg

    scatter_sum(n, part, slots, stage, send, recv, finish)


def attend_back(q_ref, qraw_ref, k_ref, kt_ref, v_ref, kraw_ref, dz_ref, wo_ref, lse_ref, low_ref, high_ref, cq_ref, sq_ref, ck_ref, sk_ref, gq_ref, gk_ref, dq_ref, dk_ref, dv_ref, dgq_ref, dgk_ref, dk_sum, dv_sum):
    kv, block = pl.program_id(0), pl.program_id(1)
    keys = k_ref.shape[0]
    ratio = q_ref.shape[1] // 128
    scale = 128 ** (-0.5)

    @pl.when((kv == 0) & (block == 0))
    def _():
        dgq_ref[...] = jnp.zeros_like(dgq_ref)
        dgk_ref[...] = jnp.zeros_like(dgk_ref)

    @pl.when(block == 0)
    def _():
        dk_sum[...] = jnp.zeros_like(dk_sum)
        dv_sum[...] = jnp.zeros_like(dv_sum)

    bias = bias_of(low_ref, high_ref, keys)
    dattn = dot_nt(dz_ref[...], wo_ref[...]).astype(BF)

    def prep_back(grad, raw, gain, cos, sin):
        du = grad * cos - pltpu.roll(grad, 64, 1) * sin
        return norm_back(raw, gain, du)

    for r in range(ratio):
        span = slice(r * 128, r * 128 + 128)
        qh, dah = q_ref[:, span], dattn[:, span]
        lse = lse_ref[pl.ds(kv * ratio + r, 1), :]
        scores = dot_nt(k_ref[...], qh) * (scale * log2e) + bias
        probs = jnp.exp2(scores - lse)
        dprobs = dot_nt(v_ref[...], dah)
        delta = jnp.sum(probs * dprobs, axis=0, keepdims=True)
        ds = (probs * (dprobs - delta)).astype(BF)
        dv_sum[...] += dot(probs.astype(BF), dah)
        dk_sum[...] += dot(ds, qh)
        dqr = dot(kt_ref[...], ds).T * scale
        back, dg = prep_back(dqr, qraw_ref[:, span], gq_ref[...], cq_ref[...], sq_ref[...])
        dq_ref[:, span] = back.astype(BF)
        dgq_ref[0:1] += dg

    @pl.when(block == pl.num_programs(1) - 1)
    def _():
        dv_ref[...] = dv_sum[...].astype(BF)
        back, dg = prep_back(
            dk_sum[...] * scale, kraw_ref[...], gk_ref[...], ck_ref[...], sk_ref[...]
        )
        dk_ref[...] = back.astype(BF)
        dgk_ref[0:1] += dg


def qkv_back(dq_ref, dk_ref, dv_ref, w_ref, out_ref):
    qw, kw = dq_ref.shape[1], dk_ref.shape[1]
    out_ref[...] = (
        dot_nt(dq_ref[...], w_ref[:, :qw])
        + dot_nt(dk_ref[...], w_ref[:, qw : qw + kw])
        + dot_nt(dv_ref[...], w_ref[:, qw + kw :])
    ).astype(BF)


def exchange(n, count, *refs):
    ins, outs = refs[:count], refs[count : 2 * count]
    send, recv, local = refs[2 * count :]
    me = lax.axis_index("seq")
    greet(others("seq", n))
    copies, keeps = [], []
    for i in range(count):
        for j in range(1, n):
            to = lax.rem(me + j, n)
            k = i * (n - 1) + j - 1
            copies.append(
                remote(ins[i].at[to], outs[i].at[me], send.at[k], recv.at[k], "seq", to)
            )
        keeps.append(pltpu.make_async_copy(ins[i].at[me], outs[i].at[me], local.at[i]))
    for copy in copies + keeps:
        copy.start()
    for copy in copies + keeps:
        copy.wait()


def gains_back(n, nf, part, out, wide, mid, seen, send, recv, local):
    me, spot = lax.axis_index("seq"), lax.axis_index("fsdp")
    greet(others("seq", n) + others("fsdp", nf))
    copies = []
    for j in range(1, nf):
        to = lax.rem(spot + j, nf)
        copies.append(
            remote(part.at[to], wide.at[j - 1], send.at[j - 1], recv.at[j - 1], "fsdp", to)
        )
    for copy in copies:
        copy.start()
    for copy in copies:
        copy.wait_recv()
    total = part[spot]
    for j in range(nf - 1):
        total += wide[j]
    mid[...] = total
    near = []
    for j in range(1, n):
        to = lax.rem(me + j, n)
        k = nf + j - 2
        near.append(remote(mid.at[to], seen.at[j - 1], send.at[k], recv.at[k], "seq", to))
    for copy in near:
        copy.start()
    for copy in near:
        copy.wait_recv()
    result = mid[me]
    for j in range(n - 1):
        result += seen[j]
    out[...] = result
    for copy in copies + near:
        copy.wait_send()


def dma(count):
    return pltpu.SemaphoreType.DMA((count,))


def shards(
    n,
    nf,
    tokens,
    seq_lengths,
    pic_starts,
    pic_lengths,
    norm1_gain,
    w_query,
    w_key,
    w_value,
    q_gain,
    k_gain,
    w_out,
    norm2_gain,
    w_gate,
    w_up,
    w_down,
    cotangent,
):
    rows, width = tokens.shape
    group = rows * n
    depth = w_query.shape[0]
    head = q_gain.shape[0] * n * nf
    qw, kw = w_query.shape[1] // n, w_key.shape[1] // n
    cw = qw + 2 * kw
    fw = w_gate.shape[1] // n
    qheads, kheads = qw // head, kw // head
    ratio = qheads // kheads
    own_gain = norm1_gain.shape[0]
    own_head = q_gain.shape[0]

    packed = jnp.zeros((8, 128), F32)
    packed = packed.at[0, :own_gain].set(norm1_gain.astype(F32))
    packed = packed.at[1, :own_gain].set(norm2_gain.astype(F32))
    packed = packed.at[2, :own_head].set(q_gain.astype(F32))
    packed = packed.at[3, :own_head].set(k_gain.astype(F32))
    wo = lax.all_gather(w_out, "fsdp", axis=0, tiled=True)
    w_att, all_gains = pl.pallas_call(
        functools.partial(attention_weights_out, n, nf),
        out_shape=(shape((n, depth, cw), BF), shape((nf, n, 8, 128), F32)),
        in_specs=[ANY] * 4,
        out_specs=(ANY, ANY),
        scratch_shapes=[
            pltpu.VMEM((n, 8, 128), F32),
            dma(3 * (n - 1)),
            dma(3 * (n - 1)),
            dma(n + nf - 2),
            dma(n + nf - 2),
            dma(5),
        ],
        compiler_params=comm_params(0),
    )(w_query, w_key, w_value, packed)
    w_att = lax.all_gather(w_att, "fsdp", axis=1, tiled=True).reshape(width, cw)
    ordered = all_gains.transpose(1, 0, 2, 3)
    gain_one = ordered[:, :, 0, :own_gain].reshape(1, width)
    gain_two = ordered[:, :, 1, :own_gain].reshape(1, width)
    gain_q = ordered[:, :, 2, :own_head].reshape(1, head)
    gain_k = ordered[:, :, 3, :own_head].reshape(1, head)

    wdt = w_down.T
    xg, gu, dn = pl.pallas_call(
        functools.partial(hidden_weights_out, n),
        out_shape=(
            shape((n, rows, width), BF),
            shape((n, depth, 2 * fw), BF),
            shape((n, depth, fw), BF),
        ),
        in_specs=[ANY] * 4,
        out_specs=(ANY,) * 3,
        scratch_shapes=[
            dma(3 * (n - 1)),
            dma(3 * (n - 1)),
            dma(gather_copies(n)),
            dma(gather_copies(n)),
            dma(4),
        ],
        compiler_params=comm_params(1),
    )(tokens, w_gate, w_up, wdt)
    gu = lax.all_gather(gu, "fsdp", axis=1, tiled=True).reshape(width, 2 * fw)
    dn = lax.all_gather(dn, "fsdp", axis=1, tiled=True).reshape(width, fw)

    places = jnp.arange(group, dtype=jnp.int32)
    lengths = seq_lengths[0]
    border_one = lengths[0]
    border_two = border_one + lengths[1]
    begins = jnp.where(places >= border_two, border_two, jnp.where(places >= border_one, border_one, 0))
    ends = jnp.where(places >= border_two, group, jnp.where(places >= border_one, border_two, border_one))
    starts, sizes = pic_starts[0], pic_lengths[0]
    inside = (places[:, None] >= starts[None, :]) & (places[:, None] < (starts + sizes)[None, :])
    pic_end = jnp.max(jnp.where(inside, (starts + sizes)[None, :], 0), axis=1)
    last = jnp.maximum(places, jnp.minimum(pic_end, ends) - 1)
    low = jnp.broadcast_to(begins[None, :], (8, group))
    high = jnp.broadcast_to(last[None, :], (8, group))
    half = head // 2
    frequency = F32(theta) ** (-(jnp.arange(half, dtype=F32) * 2.0 / head))
    angles = (places - begins).astype(F32)[:, None] * frequency[None, :]
    cosine, sine = jnp.cos(angles), jnp.sin(angles)
    cos = jnp.concatenate([cosine, cosine], axis=1)
    sin = jnp.concatenate([-sine, sine], axis=1)

    def whole(dims):
        return pl.BlockSpec(dims, lambda *ids: (0,) * len(dims))

    def by_rows(count, columns):
        return pl.BlockSpec((count, columns), lambda i: (i, 0))

    def by_cols(count, columns):
        return pl.BlockSpec((count, columns), lambda i: (0, i))

    blocks = group // 256
    n1, qraw, kraw, q, k, v, kt, vt = pl.pallas_call(
        project,
        grid=(blocks,),
        out_shape=(
            shape((group, width), BF),
            shape((group, qw), F32),
            shape((group, kw), F32),
            shape((group, qw), BF),
            shape((group, kw), BF),
            shape((group, kw), BF),
            shape((kw, group), BF),
            shape((kw, group), BF),
        ),
        in_specs=[
            by_rows(256, width),
            whole((1, width)),
            whole((width, cw)),
            whole((1, head)),
            whole((1, head)),
            by_rows(256, head),
            by_rows(256, head),
        ],
        out_specs=(
            by_rows(256, width),
            by_rows(256, qw),
            by_rows(256, kw),
            by_rows(256, qw),
            by_rows(256, kw),
            by_rows(256, kw),
            by_cols(kw, 256),
            by_cols(kw, 256),
        ),
        compiler_params=plain_params(),
    )(xg.reshape(group, width), gain_one, w_att, gain_q, gain_k, cos, sin)

    attn, lse, part_out = pl.pallas_call(
        attend,
        grid=(blocks,),
        out_shape=(
            shape((group, qw), BF),
            shape((8, group), F32),
            shape((group, width), BF),
        ),
        in_specs=[
            by_rows(256, qw),
            whole((group, kw)),
            whole((kw, group)),
            whole((qw, width)),
            by_cols(8, 256),
            by_cols(8, 256),
        ],
        out_specs=(by_rows(256, qw), by_cols(8, 256), by_rows(256, width)),
        scratch_shapes=[pltpu.VMEM((group, 256), F32)],
        compiler_params=plain_params(),
    )(q, k, vt, wo, low, high)

    slots = [
        pltpu.VMEM((scatter_slots(n), rows, width), BF),
        pltpu.VMEM((rows, width), BF),
    ]
    sems = [dma(max(6, n - 1)), dma(max(6, n - 1))]
    gather_sems = [dma(gather_copies(n)), dma(gather_copies(n)), pltpu.SemaphoreType.DMA]

    x2, n2 = pl.pallas_call(
        functools.partial(middle_stage, n),
        out_shape=(shape((rows, width), F32), shape((n, rows, width), BF)),
        in_specs=[VMEM] * 3,
        out_specs=(VMEM, ANY),
        scratch_shapes=slots + [pltpu.VMEM((rows, width), BF)] + sems + gather_sems,
        compiler_params=comm_params(2),
    )(part_out.reshape(n, rows, width), tokens, gain_two)
    n2 = n2.reshape(group, width)

    (cotangent_late,) = lax.optimization_barrier((cotangent, n2))[:1]
    cg = pl.pallas_call(
        functools.partial(gather_alone, n),
        out_shape=shape((n, rows, width), BF),
        in_specs=[ANY],
        out_specs=ANY,
        scratch_shapes=gather_sems,
        compiler_params=comm_params(3),
    )(cotangent_late).reshape(group, width)

    tile = 256
    tiles = fw // tile
    gate, up, hidden = pl.pallas_call(
        ffn_forward,
        grid=(tiles,),
        out_shape=(
            shape((group, fw), F32),
            shape((group, fw), F32),
            shape((group, fw), BF),
        ),
        in_specs=[
            whole((group, width)),
            by_cols(width, tile),
            pl.BlockSpec((width, tile), lambda i: (0, i + tiles)),
        ],
        out_specs=(by_cols(group, tile),) * 3,
        compiler_params=plain_params(),
    )(n2, gu, gu)

    def reduce_rows(grad, columns):
        return lax.psum_scatter(
            grad.reshape(n, width // n, columns), "fsdp", scatter_dimension=1, tiled=True
        )

    dn_share = reduce_rows(dot_tn(cg, hidden).astype(BF), fw)

    dgate, dup = pl.pallas_call(
        ffn_back,
        grid=(tiles,),
        out_shape=(shape((group, fw), BF), shape((group, fw), BF)),
        in_specs=[
            whole((group, width)),
            by_cols(width, tile),
            by_cols(group, tile),
            by_cols(group, tile),
        ],
        out_specs=(by_cols(group, tile),) * 2,
        compiler_params=plain_params(),
    )(cg, dn, gate, up)

    dgu = jnp.concatenate([dot_tn(n2, dgate).astype(BF), dot_tn(n2, dup).astype(BF)], axis=1)
    gu_share = reduce_rows(dgu, 2 * fw)

    part_n2 = pl.pallas_call(
        two_nt,
        grid=(blocks,),
        out_shape=shape((group, width), BF),
        in_specs=[
            by_rows(256, fw),
            by_rows(256, fw),
            pl.BlockSpec((width, fw), lambda i: (0, 0)),
            pl.BlockSpec((width, fw), lambda i: (0, 1)),
        ],
        out_specs=by_rows(256, width),
        compiler_params=plain_params(),
    )(dgate, dup, gu, gu)

    dx2, dz, dgain_two = pl.pallas_call(
        functools.partial(back_stage, n),
        out_shape=(
            shape((rows, width), F32),
            shape((n, rows, width), BF),
            shape((8, width), F32),
        ),
        in_specs=[VMEM] * 4,
        out_specs=(VMEM, ANY, VMEM),
        scratch_shapes=slots + [pltpu.VMEM((rows, width), BF)] + sems + gather_sems,
        compiler_params=comm_params(4),
    )(part_n2.reshape(n, rows, width), x2, cotangent, gain_two)
    dz = dz.reshape(group, width)

    part_y = pl.pallas_call(
        one_nt,
        grid=(blocks,),
        out_shape=shape((group, width), BF),
        in_specs=[by_rows(256, fw), whole((width, fw))],
        out_specs=by_rows(256, width),
        compiler_params=plain_params(),
    )(hidden, dn)
    output = pl.pallas_call(
        functools.partial(out_stage, n),
        out_shape=shape((rows, width), BF),
        in_specs=[VMEM] * 2,
        out_specs=VMEM,
        scratch_shapes=slots + sems,
        compiler_params=comm_params(5),
    )(part_y.reshape(n, rows, width), x2)

    wide = ratio * head
    dq, dk, dv, dgain_q, dgain_k = pl.pallas_call(
        attend_back,
        grid=(kheads, blocks),
        out_shape=(
            shape((group, qw), BF),
            shape((group, kw), BF),
            shape((group, kw), BF),
            shape((8, head), F32),
            shape((8, head), F32),
        ),
        in_specs=[
            pl.BlockSpec((256, wide), lambda h, b: (b, h)),
            pl.BlockSpec((256, wide), lambda h, b: (b, h)),
            pl.BlockSpec((group, head), lambda h, b: (0, h)),
            pl.BlockSpec((head, group), lambda h, b: (h, 0)),
            pl.BlockSpec((group, head), lambda h, b: (0, h)),
            pl.BlockSpec((group, head), lambda h, b: (0, h)),
            pl.BlockSpec((256, width), lambda h, b: (b, 0)),
            pl.BlockSpec((wide, width), lambda h, b: (h, 0)),
            pl.BlockSpec((8, 256), lambda h, b: (0, b)),
            pl.BlockSpec((8, 256), lambda h, b: (0, b)),
            pl.BlockSpec((8, 256), lambda h, b: (0, b)),
            pl.BlockSpec((256, head), lambda h, b: (b, 0)),
            pl.BlockSpec((256, head), lambda h, b: (b, 0)),
            whole((group, head)),
            whole((group, head)),
            whole((1, head)),
            whole((1, head)),
        ],
        out_specs=(
            pl.BlockSpec((256, wide), lambda h, b: (b, h)),
            pl.BlockSpec((group, head), lambda h, b: (0, h)),
            pl.BlockSpec((group, head), lambda h, b: (0, h)),
            whole((8, head)),
            whole((8, head)),
        ),
        scratch_shapes=[pltpu.VMEM((group, head), F32), pltpu.VMEM((group, head), F32)],
        compiler_params=plain_params(),
    )(q, qraw, k, kt, v, kraw, dz, wo, lse, low, high, cos, sin, cos, sin, gain_q, gain_k)

    wo_share = lax.psum_scatter(
        dot_tn(attn, dz).astype(BF), "fsdp", scatter_dimension=0, tiled=True
    )
    dqkv = jnp.concatenate([dq, dk, dv], axis=1)
    att_share = reduce_rows(dot_tn(n1, dqkv).astype(BF), cw)

    part_n1 = pl.pallas_call(
        qkv_back,
        grid=(blocks,),
        out_shape=shape((group, width), BF),
        in_specs=[
            by_rows(256, qw),
            by_rows(256, kw),
            by_rows(256, kw),
            whole((width, cw)),
        ],
        out_specs=by_rows(256, width),
        compiler_params=plain_params(),
    )(dq, dk, dv, w_att)
    input_grad, dgain_one = pl.pallas_call(
        functools.partial(input_stage, n),
        out_shape=(shape((rows, width), BF), shape((8, width), F32)),
        in_specs=[VMEM] * 4,
        out_specs=(VMEM, VMEM),
        scratch_shapes=slots + sems,
        compiler_params=comm_params(6),
    )(part_n1.reshape(n, rows, width), tokens, dx2, gain_one)

    def owned(row, count):
        cut = row.reshape(n, nf, 1, count)
        return jnp.pad(cut, ((0, 0), (0, 0), (0, 0), (0, 128 - count)))

    blocks_of = jnp.concatenate(
        [
            owned(dgain_one[0], own_gain),
            owned(dgain_two[0], own_gain),
            owned(dgain_q[0], own_head),
            owned(dgain_k[0], own_head),
            jnp.zeros((n, nf, 4, 128), F32),
        ],
        axis=2,
    ).transpose(1, 0, 2, 3)
    gains = pl.pallas_call(
        functools.partial(gains_back, n, nf),
        out_shape=shape((8, 128), F32),
        in_specs=[VMEM],
        out_specs=VMEM,
        scratch_shapes=[
            pltpu.VMEM((nf - 1, n, 8, 128), F32),
            pltpu.VMEM((n, 8, 128), F32),
            pltpu.VMEM((n - 1, 8, 128), F32),
            dma(n + nf - 2),
            dma(n + nf - 2),
            pltpu.SemaphoreType.DMA,
        ],
        compiler_params=comm_params(7),
    )(blocks_of)

    def swap(number, *arrays):
        count = len(arrays)
        return pl.pallas_call(
            functools.partial(exchange, n, count),
            out_shape=tuple(shape(a.shape, a.dtype) for a in arrays),
            in_specs=[ANY] * count,
            out_specs=(ANY,) * count,
            scratch_shapes=[dma(count * (n - 1)), dma(count * (n - 1)), dma(count)],
            compiler_params=comm_params(number),
        )(*arrays)

    gu_mine, dn_mine = swap(8, gu_share, dn_share)
    (att_mine,) = swap(9, att_share)

    def assemble(array, begin, count):
        return array[:, :, begin : begin + count].transpose(1, 0, 2).reshape(depth, -1).astype(F32)

    return (
        output,
        input_grad,
        gains[0, :own_gain],
        assemble(att_mine, 0, qw),
        assemble(att_mine, qw, kw),
        assemble(att_mine, qw + kw, kw),
        gains[2, :own_head],
        gains[3, :own_head],
        wo_share.astype(F32),
        gains[1, :own_gain],
        assemble(gu_mine, 0, fw),
        assemble(gu_mine, fw, fw),
        assemble(dn_mine, 0, fw).T,
    )


def solution(mesh):
    return jax.shard_map(
        functools.partial(shards, mesh.shape["seq"], mesh.shape["fsdp"]),
        mesh=mesh,
        in_specs=(
            P(("fsdp", "seq"), None),
            P("fsdp", None),
            P("fsdp", None),
            P("fsdp", None),
            P(("seq", "fsdp")),
            P(("seq", "fsdp"), None),
            P(("seq", "fsdp"), None),
            P(("seq", "fsdp"), None),
            P(("seq", "fsdp")),
            P(("seq", "fsdp")),
            P(("seq", "fsdp"), None),
            P(("seq", "fsdp")),
            P(("seq", "fsdp"), None),
            P(("seq", "fsdp"), None),
            P(None, ("seq", "fsdp")),
            P(("fsdp", "seq"), None),
        ),
        out_specs=(
            P(("fsdp", "seq"), None),
            P(("fsdp", "seq"), None),
            P(("seq", "fsdp")),
            P(("seq", "fsdp"), None),
            P(("seq", "fsdp"), None),
            P(("seq", "fsdp"), None),
            P(("seq", "fsdp")),
            P(("seq", "fsdp")),
            P(("seq", "fsdp"), None),
            P(("seq", "fsdp")),
            P(("seq", "fsdp"), None),
            P(("seq", "fsdp"), None),
            P(None, ("seq", "fsdp")),
        ),
        check_vma=False,
    )
```

time: 2860 us -> 737 us (0.26)
  waiting for transfers between devices: 2150 us -> 77.8 us
  Pallas kernels: 0 us -> 527 us
  matrix products: 345 us -> 44.1 us
  other arithmetic: 194 us -> 27.8 us
  blocking collectives: 83 us -> 0 us
    reduce_scatter x4, waiting for transfers between devices: 1480 us -> 53.2 us  [the longest x3 53.2 us: reduce_rows(): lax.psum_scatter(grad.reshape(n, width // n, columns), 'fsdp', scatter_di...]
    all_gather x9 -> x4, waiting for transfers between devices: 657 us -> 23.3 us  [the longest x1 23.2 us: shards(): dn = lax.all_gather(dn, 'fsdp', axis=1, tiled=True).reshape(width, fw)]
    pallas_call x0 -> x18, Pallas kernels: none -> 527 us  [the longest x1 79.1 us: shards(): pl.pallas_call(functools.partial(back_stage, n), out_shape=(shape((rows,...]
    dot_general x74 -> x5, matrix products: 345 us -> 44.1 us  [dot_tn(): lax.dot_general(a, b, (((0,), (0,)), ((), ())), preferred_element_type=F32)]
    concatenate x4 -> x2, other arithmetic: 136 us -> 16.2 us  [the longest x1 14.9 us: shards(): jnp.concatenate([dot_tn(n2, dgate).astype(BF), dot_tn(n2, dup).astype(BF)...]
    unnamed x2 -> x0, blocking collectives: 83 us -> none
  transfers between devices with their start and end apart: 13 -> 8, of which waited for: 13 -> 2; matrix products, arithmetic and copies ran while one was open for 13% -> 13% of each run, Pallas kernels for 0% -> 51%
where the time goes in v1:
time: 737 us; the launch traced here: 732 us
  Pallas kernels  527 us (72%)
  waiting for transfers between devices  77.8 us (11%)
  matrix products  44.1 us (6%)
  local copies, waits for them, and re-layouts  38.8 us (5%)
  other arithmetic  27.8 us (4%)
  between operations  16.1 us (2%)
    pallas_call x1, Pallas kernels, shards(): pl.pallas_call(functools.partial(back_stage, n), out_shape=(shape((rows,...  79.1 us
    pallas_call x1, Pallas kernels, shards(): pl.pallas_call(functools.partial(middle_stage, n), out_shape=(shape((rows...  75.6 us
    pallas_call x1, Pallas kernels, shards(): pl.pallas_call(functools.partial(hidden_weights_out, n), out_shape=(shape...  63.1 us
    reduce_scatter x3, waiting for transfers between devices, reduce_rows(): lax.psum_scatter(grad.reshape(n, width // n, columns), 'fsdp', scatter_di...  53.2 us
    dot_general x5, matrix products, dot_tn(): lax.dot_general(a, b, (((0,), (0,)), ((), ())), preferred_element_type=F32)  44.1 us
    pallas_call x1, Pallas kernels, shards(): pl.pallas_call(functools.partial(input_stage, n), out_shape=(shape((rows,...  40.3 us
    pallas_call x1, Pallas kernels, shards(): pl.pallas_call(functools.partial(out_stage, n), out_shape=shape((rows, wi...  39.8 us
    pallas_call x2, Pallas kernels, swap(): pl.pallas_call(functools.partial(exchange, n, count), out_shape=tuple((sh...  37.4 us
  transfers between devices with their start and end apart: 8, of which 2 were waited for; matrix products, arithmetic and copies ran while one was open for 13% of the time, Pallas kernels for 51%

profile of v1, /device:TPU:0, one launch (start us, length us, event | category | flops | bytes accessed | tf_op | source)
XLA Modules:
  0.0 731.6 jit_solution(16553012286474678392)
XLA Ops:
  11.0 14.1 %shard_map.256 = (bf16[4,64,1024]{2,1,0:T(8,128)(2,1)}, f32[8,4,8,128]{3,2,1,0:T(8,128)}) custom-call(bf16[64,2048]{1,0:T(8,128)(2,1)} %wq.1, bf16[64,1024]{1,0:T(8,128)(2,1)} %wk.1, bf16[64,1024]{1,0:T(8,128)(2,1)} %wv.1, f32[8,128]{1,0:T(8,128)} %copy-done.7), custom_call_target="tpu_custom_call" | custom-call | tf_op jit(solution)/shard_map/pallas_call | solution.py:592
  25.9 63.1 %shard_map.255 = (bf16[4,256,2048]{2,1,0:T(8,128)(2,1)}, bf16[4,64,3072]{2,1,0:T(8,128)(2,1)}, bf16[4,64,1536]{2,1,0:T(8,128)(2,1)}) custom-call(bf16[256,2048]{1,0:T(8,128)(2,1)} %x.16, bf16[64,6144]{1,0:T(8,128)(2,1)} %wg.1, bf16[64,6144]{1,0:T(8,128)(2,1)} %wu.1, bf16[64,6144]{1,0:T(8,128)(2,1)} %bitcast.117), custom_call_target="tpu_custom_call" | custom-call | tf_op jit(solution)/shard_map/pallas_call | solution.py:615
  95.1 1.9 fusion.5
  97.0 1.3 pad_maximum_fusion.1
  99.0 12.2 %shard_map.257 = (bf16[1024,2048]{1,0:T(8,128)(2,1)}, f32[1024,512]{1,0:T(8,128)}, f32[1024,256]{1,0:T(8,128)}, bf16[1024,512]{1,0:T(8,128)(2,1)}, bf16[1024,256...) custom-call(bf16[1024,2048]{1,0:T(8,128)(2,1)} %bitcast.113, ...), custom_call_target="tpu_custom_call" | custom-call | tf_op jit(solution)/shard_map/pallas_call | solution.py:665
  112.4 17.3 %shard_map.258 = (bf16[1024,512]{1,0:T(8,128)(2,1)}, f32[8,1024]{1,0:T(8,128)}, bf16[1024,2048]{1,0:T(8,128)(2,1)}) custom-call(bf16[1024,512]{1,0:T(8,128)(2,1)} %get-tuple-element.100.q_ref, bf16[1024,256]{1,0:T(8,128)(2,1)} %get-tuple-element.101.k_ref, bf16[256,1024]{1,0:T(8,128)(2,1)} %get-tuple-element.102.vt_ref, ...), custom_call_target="tpu_custom_call" | custom-call | tf_op jit(solution)/shard_map/pallas_call | solution.py:700
  129.7 75.6 %shard_map.259 = (f32[256,2048]{1,0:T(8,128)}, bf16[4,256,2048]{2,1,0:T(8,128)(2,1)}) custom-call(bf16[4,256,2048]{2,1,0:T(8,128)(2,1)} %bitcast.111, bf16[256,2048]{1,0:T(8,128)(2,1)} %x.16, f32[1,2048]{1,0:T(1,128)} %reshape_squeeze.27.gain), custom_call_target="tpu_custom_call" | custom-call | tf_op jit(solution)/shard_map/pallas_call | solution.py:728
  205.3 34.6 %shard_map.263 = bf16[4,256,2048]{2,1,0:T(8,128)(2,1)} custom-call(bf16[256,2048]{1,0:T(8,128)(2,1)} %cot.1), custom_call_target="tpu_custom_call" | custom-call | tf_op jit(solution)/shard_map/pallas_call | solution.py:739
  240.0 19.4 %shard_map.260 = (f32[1024,1536]{1,0:T(8,128)}, f32[1024,1536]{1,0:T(8,128)}, bf16[1024,1536]{1,0:T(8,128)(2,1)}) custom-call(bf16[1024,2048]{1,0:T(8,128)(2,1)} %bitcast.106, bf16[2048,3072]{1,0:T(8,128)(2,1)} %bitcast.91, bf16[2048,3072]{1,0:T(8,128)(2,1)} %bitcast.92), custom_call_target="tpu_custom_call" | custom-call | tf_op jit(solution)/shard_map/pallas_call | solution.py:750
  259.4 23.2 %all-gather.11.cloned.1.call-done = bf16[4,512,1536]{2,1,0:T(8,128)(2,1)} async-done(((bf16[4,64,1536]{2,1,0:T(8,128)(2,1)}), bf16[4,512,1536]{2,1,0:T(8,128)(2,1)}) %all-gather.11.cloned.1.call-update) | async-done | bytes 6291472 | tf_op jit(solution)/shard_map/all_gather | solution.py:634
  282.6 15.1 %shard_map.264 = (bf16[1024,1536]{1,0:T(8,128)(2,1)}, bf16[1024,1536]{1,0:T(8,128)(2,1)}) custom-call(bf16[1024,2048]{1,0:T(8,128)(2,1)} %bitcast.103, bf16[2048,1536]{1,0:T(8,128)(2,1)} %bitcast.96, f32[1024,1536]{1,0:T(8,128)} %get-tuple-element.114.gate_ref, f32[1024,1536]{1,0:T(8,128)} %get-tuple-element.115.up_ref), custom_call_target="tpu_custom_call" | custom-call | tf_op jit(solution)/shard_map/pallas_call | solution.py:774
  297.8 19.9 %shard_map.265 = bf16[1024,2048]{1,0:T(8,128)(2,1)} custom-call(bf16[1024,1536]{1,0:T(8,128)(2,1)} %get-tuple-element.116.a_ref, bf16[1024,1536]{1,0:T(8,128)(2,1)} %get-tuple-element.117.b_ref, bf16[2048,3072]{1,0:T(8,128)(2,1)} %bitcast.93, bf16[2048,3072]{1,0:T(8,128)(2,1)} %bitcast.94), custom_call_target="tpu_custom_call" | custom-call | tf_op jit(solution)/shard_map/pallas_call | solution.py:791
  317.7 79.1 %shard_map.266 = (f32[256,2048]{1,0:T(8,128)}, bf16[4,256,2048]{2,1,0:T(8,128)(2,1)}, f32[8,2048]{1,0:T(8,128)}) custom-call(bf16[4,256,2048]{2,1,0:T(8,128)(2,1)} %bitcast.98, f32[256,2048]{1,0:T(8,128)} %get-tuple-element.108.x2, bf16[256,2048]{1,0:T(8,128)(2,1)} %cot.1, f32[1,2048]{1,0:T(1,128)} %reshape_squeeze.27.gain), custom_call_target="tpu_custom_call" | custom-call | tf_op jit(solution)/shard_map/pallas_call | solution.py:805
  396.8 5.9 convolution_convert_fusion.4
  402.8 27.4 %shard_map.267 = (bf16[1024,512]{1,0:T(8,128)(2,1)}, bf16[1024,256]{1,0:T(8,128)(2,1)}, bf16[1024,256]{1,0:T(8,128)(2,1)}, f32[8,128]{1,0:T(8,128)}, f32[8,128]{1,0:T(8,128)}) custom-call(bf16[1024,512]{1,0:T(8,128)(2,1)} %get-tuple-element.100.q_ref, f32[1024,512]{1,0:T(8,128)} %get-tuple-element.109.qraw_ref, bf16[1024,256]{1,0:T(8,128)(2,1)} %get-tuple-element.101.k_ref, ...), custom_call_target="tpu_custom_call" | custom-call | tf_op jit(solution)/shard_map/pallas_call | solution.py:837
  430.2 9.4 %convolution_convert_fusion.3 = bf16[2048,1024]{1,0:T(8,128)(2,1)} fusion(bf16[1024,2048]{1,0:T(8,128)(2,1)} %get-tuple-element.129, bf16[1024,256]{1,0:T(8,128)(2,1)} %get-tuple-element.122.dv_ref, bf16[1024,256]{1,0:T(8,128)(2,1)} %get-tuple-element.121.dk_ref, bf16[1024,512]{1,0:T(8,128)(2,1)} %get-tuple-element.120.dq_ref), kind=kOutput, calls=%fused_computation.4 | convolution fusion | flops 4303355904 | bytes 10485760 | tf_op jit(solution)/shard_map/dot_general | solution.py:32
  439.7 1.8 copy-done.3
  441.5 11.2 %convolution_convert_fusion = bf16[2048,1536]{1,0:T(8,128)(2,1)} fusion(bf16[1024,2048]{1,0:T(8,128)(2,1)} %bitcast.104, bf16[1024,1536]{1,0:T(8,128)(2,1)S(1)} %copy-done.3), kind=kOutput, calls=%fused_computation.1 | convolution fusion | flops 6445596672 | bytes 13631488 | tf_op jit(solution)/shard_map/dot_general | solution.py:32
  452.8 10.1 %convolution_convert_fusion.1 = bf16[2048,1536]{0,1:T(8,128)(2,1)S(1)} fusion(bf16[1024,2048]{1,0:T(8,128)(2,1)} %bitcast.107, bf16[1024,1536]{1,0:T(8,128)(2,1)} %get-tuple-element.117.b_ref), kind=kOutput, calls=%fused_computation.2 | convolution fusion | flops 6445596672 | bytes 13631488 | tf_op jit(solution)/shard_map/dot_general | solution.py:32
  462.9 7.5 %convolution_convert_fusion.2 = bf16[2048,1536]{0,1:T(8,128)(2,1)S(1)} fusion(bf16[1024,2048]{1,0:T(8,128)(2,1)S(1)} %bitcast.108, bf16[1024,1536]{1,0:T(8,128)(2,1)S(1)} %copy-done.2), kind=kOutput, calls=%fused_computation.3 | convolution fusion | flops 6445596672 | bytes 13631488 | tf_op jit(solution)/shard_map/dot_general | solution.py:32
  470.4 14.9 %pad_maximum_fusion = bf16[2048,3072]{0,1:T(8,128)(2,1)} fusion(bf16[2048,1536]{0,1:T(8,128)(2,1)S(1)} %convolution_convert_fusion.1, bf16[2048,1536]{0,1:T(8,128)(2,1)S(1)} %convolution_convert_fusion.2), kind=kLoop, calls=%fused_computation | loop fusion | flops 25165824 | bytes 25165824 | tf_op jit(solution)/shard_map/concatenate | solution.py:788
  485.3 16.5 %copy.62 = bf16[2048,3072]{1,0:T(8,128)(2,1)} copy(bf16[2048,3072]{0,1:T(8,128)(2,1)} %pad_maximum_fusion) | data formatting | bytes 25165824 | tf_op jit(solution)/shard_map/concatenate | solution.py:788
  501.8 11.4 %shard_map.261 = bf16[1024,2048]{1,0:T(8,128)(2,1)} custom-call(bf16[1024,1536]{1,0:T(8,128)(2,1)} %get-tuple-element.106.a_ref, bf16[2048,1536]{1,0:T(8,128)(2,1)} %bitcast.97), custom_call_target="tpu_custom_call" | custom-call | tf_op jit(solution)/shard_map/pallas_call | solution.py:819
  513.2 8.9 %shard_map.268 = bf16[1024,2048]{1,0:T(8,128)(2,1)} custom-call(bf16[1024,512]{1,0:T(8,128)(2,1)} %get-tuple-element.120.dq_ref, bf16[1024,256]{1,0:T(8,128)(2,1)} %get-tuple-element.121.dk_ref, bf16[1024,256]{1,0:T(8,128)(2,1)} %get-tuple-element.122.dv_ref, bf16[2048,1024]{1,0:T(8,128)(2,1)} %bitcast.101), custom_call_target="tpu_custom_call" | custom-call | tf_op jit(solution)/shard_map/pallas_call | solution.py:883
  522.1 39.8 %shard_map.262 = bf16[256,2048]{1,0:T(8,128)(2,1)} custom-call(bf16[4,256,2048]{2,1,0:T(8,128)(2,1)} %bitcast.99, f32[256,2048]{1,0:T(8,128)} %get-tuple-element.108.x2), custom_call_target="tpu_custom_call" | custom-call | tf_op jit(solution)/shard_map/pallas_call | solution.py:827
  561.9 40.3 %shard_map.269 = (bf16[256,2048]{1,0:T(8,128)(2,1)}, f32[8,2048]{1,0:T(8,128)}) custom-call(bf16[4,256,2048]{2,1,0:T(8,128)(2,1)} %bitcast.102, bf16[256,2048]{1,0:T(8,128)(2,1)} %x.16, f32[256,2048]{1,0:T(8,128)} %get-tuple-element.123.dx2, f32[1,2048]{1,0:T(1,128)} %reshape_squeeze.24.gain_ref.gain), custom_call_target="tpu_custom_call" | custom-call | tf_op jit(solution)/shard_map/pallas_call | solution.py:896
  602.2 0.9 slice_reduce_fusion.1
  603.2 0.9 slice_reduce_fusion
  604.2 0.7 slice_reduce_fusion.2
  605.9 0.8 concatenate.25
  606.7 11.0 %shard_map.270 = f32[8,128]{1,0:T(8,128)} custom-call(f32[8,4,8,128]{3,2,1,0:T(8,128)} %bitcast.119), custom_call_target="tpu_custom_call" | custom-call | tf_op jit(solution)/shard_map/pallas_call | solution.py:919
  617.7 1.3 slice_bitcast_fusion.1
  618.9 1.3 slice_bitcast_fusion
  620.2 1.8 convert_element_type.99
  622.0 10.4 %shard_map.271 = bf16[4,64,1024]{2,1,0:T(8,128)(2,1)} custom-call(bf16[4,64,1024]{2,1,0:T(8,128)(2,1)} %reduce-scatter.5.cloned.1.call-done.refs_0_), custom_call_target="tpu_custom_call" | custom-call | tf_op jit(solution)/shard_map/pallas_call | solution.py:937
  632.4 1.0 convert_bitcast_fusion.3
  633.4 0.8 copy.66
  634.2 1.0 convert_bitcast_fusion.4
  635.3 0.7 copy.68
  636.0 0.7 copy.67
  636.7 53.2 %reduce-scatter.9.cloned.1.call-done.refs_0_ = bf16[4,64,3072]{2,1,0:T(8,128)(2,1)} async-done(((bf16[4,512,3072]{2,1,0:T(8,128)(2,1)}), bf16[4,64,3072]{2,1,0:T(8,128)(2,1)}) %reduce-scatter.9.cloned.1.call-update) | async-done | bytes 1572880 | tf_op jit(solution)/shard_map/reduce_scatter | solution.py:768
  689.9 27.0 %shard_map.272 = (bf16[4,64,3072]{2,1,0:T(8,128)(2,1)}, bf16[4,64,1536]{2,1,0:T(8,128)(2,1)}) custom-call(bf16[4,64,3072]{2,1,0:T(8,128)(2,1)} %reduce-scatter.9.cloned.1.call-done.refs_0_, bf16[4,64,1536]{2,1,0:T(8,128)(2,1)} %reduce-scatter.11.cloned.1.call-done.refs_1_), custom_call_target="tpu_custom_call" | custom-call | tf_op jit(solution)/shard_map/pallas_call | solution.py:937
  716.9 1.4 convert_bitcast_fusion
  718.4 1.3 copy.71
  720.1 1.3 copy.70
  721.3 1.3 copy.69
  722.6 1.0 copy.77
  723.6 1.0 copy.78
  (85 shorter events, 12.9 us)
Async XLA Ops:
  7.2 85.2 %copy-start.8 = (s32[1,3]{1,0:T(1,128)S(1)}, s32[1,3]{1,0:T(1,128)}, u32[]{:S(2)}) copy-start(s32[1,3]{1,0:T(1,128)} %param.25) | copy-start | bytes 40
  7.2 87.8 %copy-start.9 = (s32[1,2]{1,0:T(1,128)S(1)}, s32[1,2]{1,0:T(1,128)}, u32[]{:S(2)}) copy-start(s32[1,2]{1,0:T(1,128)} %param.26) | copy-start | bytes 28
  7.2 87.8 %copy-start.11 = (s32[1,2]{1,0:T(1,128)S(1)}, s32[1,2]{1,0:T(1,128)}, u32[]{:S(2)}) copy-start(s32[1,2]{1,0:T(1,128)} %param.27) | copy-start | bytes 28
  7.2 91.7 %all-gather.5.cloned.1.call-start = ((), (), s32[]{:S(2)}) async-start(), calls=%async_computation.4 | async-start | bytes 4718592 | tf_op jit(solution)/shard_map/all_gather | solution.py:607
  10.4 0.6 copy-start.7
  25.1 64.6 %copy-start.6 = (f32[8,4,8,128]{3,2,1,0:T(8,128)S(1)}, f32[8,4,8,128]{3,2,1,0:T(8,128)}, u32[]{:S(2)}) copy-start(f32[8,4,8,128]{3,2,1,0:T(8,128)} %get-tuple-element.98) | copy-start | bytes 393220
  25.1 86.1 %all-gather.7.cloned.1.call-start = ((), (), s32[]{:S(2)}) async-start(), calls=%async_computation.5 | async-start | bytes 2359296 | tf_op jit(solution)/shard_map/all_gather | solution.py:591
  25.9 214.1 %all-gather.9.cloned.1.call-start = ((), (), s32[]{:S(2)}) async-start(), calls=%async_computation.6 | async-start | bytes 14155776 | tf_op jit(solution)/shard_map/all_gather | solution.py:633
  89.1 193.6 %all-gather.11.cloned.1.call-start = ((), (), s32[]{:S(2)}) async-start(), calls=%async_computation.7 | async-start | bytes 7077888 | tf_op jit(solution)/shard_map/all_gather | solution.py:634
  89.6 530.5 %reduce-scatter.7.cloned.1.call-start = ((), (), s32[]{:S(2)}) async-start(), calls=%async_computation.9 | async-start | bytes 2359296 | tf_op jit(solution)/shard_map/reduce_scatter | solution.py:877
  317.7 79.2 %copy-start.10 = (bf16[1024,512]{1,0:T(8,128)(2,1)S(1)}, bf16[1024,512]{1,0:T(8,128)(2,1)}, u32[]{:S(2)}) copy-start(bf16[1024,512]{1,0:T(8,128)(2,1)} %get-tuple-element.130) | copy-start | bytes 3145732
  402.7 219.2 %reduce-scatter.5.cloned.1.call-start = ((), (), s32[]{:S(2)}) async-start(), calls=%async_computation.8 | async-start | bytes 4718592 | tf_op jit(solution)/shard_map/reduce_scatter | solution.py:768
  439.6 1.9 copy-start.3
  439.6 197.1 %reduce-scatter.11.cloned.1.call-start = ((), (), s32[]{:S(2)}) async-start(), calls=%async_computation.11 | async-start | bytes 7077888 | tf_op jit(solution)/shard_map/reduce_scatter | solution.py:768
  452.7 10.1 %copy-start.2 = (bf16[1024,1536]{1,0:T(8,128)(2,1)S(1)}, bf16[1024,1536]{1,0:T(8,128)(2,1)}, u32[]{:S(2)}) copy-start(bf16[1024,1536]{1,0:T(8,128)(2,1)} %get-tuple-element.116.a_ref) | copy-start | bytes 9437188
  452.8 237.2 %reduce-scatter.9.cloned.1.call-start = ((), (), s32[]{:S(2)}) async-start(), calls=%async_computation.10 | async-start | bytes 14155776 | tf_op jit(solution)/shard_map/reduce_scatter | solution.py:768
  452.8 10.1 %copy-start = (bf16[4,256,2048]{2,1,0:T(8,128)(2,1)S(1)}, bf16[4,256,2048]{2,1,0:T(8,128)(2,1)}, u32[]{:S(2)}) copy-start(bf16[4,256,2048]{2,1,0:T(8,128)(2,1)} %get-tuple-element.104) | copy-start | bytes 12582916
  716.9 2.7 copy-start.4
  720.0 2.6 copy-start.1
  720.0 3.5 copy-start.5
Sparse Core Ops, SparseCore 0:
  25.3 45.5 all-gather.4
  72.5 27.8 all-gather.6
  102.0 116.2 all-gather.8
  219.7 62.8 all-gather.10
  402.8 33.6 reduce-scatter.6
  439.8 47.7 reduce-scatter.4
  489.9 67.9 reduce-scatter.10
  560.2 129.6 reduce-scatter.8

commit v2 on v1

--- a/solution.py
+++ b/solution.py
@@ -85,116 +85,127 @@
     return 6 if n == 4 else n - 1
 
 
-def gather(n, own, out, send, recv, local):
+def gather_parts(n, own, out, send, recv, local):
     me = lax.axis_index("seq")
     keep = pltpu.make_async_copy(own, out.at[me], local)
-    keep.start()
+    half = own.shape[0] // 2
+    low, high = pl.ds(0, half), pl.ds(half, half)
     if n == 4:
         across, along, _ = square(me)
-        half = own.shape[0] // 2
-        low, high = pl.ds(0, half), pl.ds(half, half)
-
-        def piece(number, rows, to):
-            return remote(
-                own.at[rows], out.at[me, rows], send.at[number], recv.at[number], "seq", to
-            )
-
-        first = [
-            piece(0, low, across),
-            piece(1, high, along),
-            piece(2, high, across),
-            piece(3, low, along),
+        moves = [
+            (own.at[low], out.at[me, low], across),
+            (own.at[high], out.at[me, high], along),
+            (own.at[high], out.at[me, high], across),
+            (own.at[low], out.at[me, low], along),
+            (out.at[across, low], out.at[across, low], along),
+            (out.at[along, high], out.at[along, high], across),
         ]
-        for copy in first:
+    else:
+        moves = [(own, out.at[me], lax.rem(me + j, n)) for j in range(1, n)]
+    copies = [
+        remote(src, dst, send.at[i], recv.at[i], "seq", to)
+        for i, (src, dst, to) in enumerate(moves)
+    ]
+
+    def start():
+        for copy in copies[:4]:
             copy.start()
-        first[0].wait_recv()
-        on_a = remote(
-            out.at[across, low], out.at[across, low], send.at[4], recv.at[4], "seq", along
-        )
-        on_a.start()
-        first[1].wait_recv()
-        on_b = remote(
-            out.at[along, high], out.at[along, high], send.at[5], recv.at[5], "seq", across
-        )
-        on_b.start()
-        first[2].wait_recv()
-        first[3].wait_recv()
-        on_a.wait_recv()
-        on_b.wait_recv()
-        for copy in first + [on_a, on_b]:
+        if n != 4:
+            for copy in copies[4:]:
+                copy.start()
+        keep.start()
+
+    def relay():
+        if n == 4:
+            copies[0].wait_recv()
+            copies[4].start()
+            copies[1].wait_recv()
+            copies[5].start()
+
+    def finish():
+        for copy in copies[2:] if n == 4 else copies:
+            copy.wait_recv()
+        for copy in copies:
             copy.wait_send()
+        keep.wait()
+
+    return start, relay, finish
+
+
+def gather(n, own, out, send, recv, local):
+    for part in gather_parts(n, own, out, send, recv, local):
+        part()
+
+
+def scatter_slots(n):
+    return 4 if n == 4 else n - 1
+
+
+def scatter_sum(n, part, slots, stage, send, recv, finish):
+    start, relay, total = scatter_parts(n, part, slots, stage, send, recv, finish)
+    start()
+    relay()
+    total()
+
+
+def scatter_parts(n, part, slots, stage, send, recv, finish):
+    me = lax.axis_index("seq")
+    rows = part.shape[1]
+    half = rows // 2
+    low, high = pl.ds(0, half), pl.ds(half, half)
+    if n == 4:
+        across, along, corner = square(me)
+        moves = [
+            (part.at[corner, low], slots.at[2, low], along),
+            (part.at[corner, high], slots.at[2, high], across),
+            (part.at[across, high], slots.at[0, high], across),
+            (part.at[along, low], slots.at[1, low], along),
+            (stage.at[low], slots.at[0, low], across),
+            (stage.at[high], slots.at[1, high], along),
+        ]
+        count = 2
     else:
-        copies = []
+        moves = []
         for j in range(1, n):
             to = lax.rem(me + j, n)
-            copies.append(
-                remote(own, out.at[me], send.at[j - 1], recv.at[j - 1], "seq", to)
-            )
+            moves.append((part.at[to], slots.at[j - 1], to))
+        count = n - 1
+    copies = [
+        remote(src, dst, send.at[i], recv.at[i], "seq", to)
+        for i, (src, dst, to) in enumerate(moves)
+    ]
+
+    def start(begin=0, end=4):
+        for copy in copies[begin:end] if n == 4 else copies:
+            copy.start()
+
+    def relay():
+        if n == 4:
+            copies[0].wait_recv()
+            stage[low] = (part[across, low].astype(F32) + slots[2, low].astype(F32)).astype(BF)
+            copies[4].start()
+            copies[1].wait_recv()
+            stage[high] = (part[along, high].astype(F32) + slots[2, high].astype(F32)).astype(BF)
+            copies[5].start()
+
+    def total():
+        for copy in copies[2:] if n == 4 else copies:
+            copy.wait_recv()
+        step = 32
+
+        def chunk(number, carry):
+            at = pl.ds(pl.multiple_of(number * step, step), step)
+            value = part[me, at].astype(F32)
+            for slot in range(count):
+                value += slots[slot, at].astype(F32)
+            finish(at, value)
+            return carry
+
+        lax.fori_loop(0, rows // step, chunk, 0)
         for copy in copies:
-            copy.start()
-        for copy in copies:
-            copy.wait()
-    keep.wait()
-
-
-def scatter_slots(n):
-    return 4 if n == 4 else n - 1
-
-
-def scatter_sum(n, part, slots, stage, send, recv, finish):
-    me = lax.axis_index("seq")
-    rows = part.shape[1]
-    if n == 4:
-        across, along, corner = square(me)
-        half = rows // 2
-        low, high = pl.ds(0, half), pl.ds(half, half)
-        c0 = remote(part.at[corner, low], slots.at[2, low], send.at[0], recv.at[0], "seq", along)
-        c1 = remote(part.at[corner, high], slots.at[2, high], send.at[1], recv.at[1], "seq", across)
-        c2 = remote(part.at[across, high], slots.at[0, high], send.at[2], recv.at[2], "seq", across)
-        c3 = remote(part.at[along, low], slots.at[1, low], send.at[3], recv.at[3], "seq", along)
-        c4 = remote(stage.at[low], slots.at[0, low], send.at[4], recv.at[4], "seq", across)
-        c5 = remote(stage.at[high], slots.at[1, high], send.at[5], recv.at[5], "seq", along)
-        for copy in (c0, c1, c2, c3):
-            copy.start()
-        c0.wait_recv()
-        stage[low] = (
-            part[across, low].astype(F32) + slots[2, low].astype(F32)
-        ).astype(BF)
-        c4.start()
-        c1.wait_recv()
-        stage[high] = (
-            part[along, high].astype(F32) + slots[2, high].astype(F32)
-        ).astype(BF)
-        c5.start()
-        for copy in (c2, c3, c4, c5):
-            copy.wait_recv()
-        copies = (c0, c1, c2, c3, c4, c5)
-        count = 2
-    else:
-        copies = []
-        for j in range(1, n):
-            to = lax.rem(me + j, n)
-            copies.append(
-                remote(part.at[to], slots.at[j - 1], send.at[j - 1], recv.at[j - 1], "seq", to)
-            )
-        for copy in copies:
-            copy.start()
-        for copy in copies:
-            copy.wait_recv()
-        count = n - 1
-    step = 32
-
-    def chunk(number, carry):
-        at = pl.ds(pl.multiple_of(number * step, step), step)
-        total = part[me, at].astype(F32)
-        for slot in range(count):
-            total += slots[slot, at].astype(F32)
-        finish(at, total)
-        return carry
-
-    lax.fori_loop(0, rows // step, chunk, 0)
-    for copy in copies:
-        copy.wait_send()
+            copy.wait_send()
+
+    return start, relay, total
 
 
 def inverse_rms(values):
@@ -210,18 +221,14 @@
     return back, jnp.sum(grad * values * inverse, axis=0, keepdims=True)
 
 
-def attention_weights_out(n, nf, wq, wk, wv, gains, out, all_gains, seen, send, recv, gsend, grecv, local):
-    me, spot = lax.axis_index("seq"), lax.axis_index("fsdp")
-    greet(others("seq", n) + others("fsdp", nf))
+def attention_weights_out(n, wq, wk, wv, out, send, recv, local):
+    me = lax.axis_index("seq")
+    greet(others("seq", n))
     widths = [wq.shape[1] // n, wk.shape[1] // n, wv.shape[1] // n]
     begins = [0, widths[0], widths[0] + widths[1]]
     copies = []
-    small = []
     for j in range(1, n):
         to = lax.rem(me + j, n)
-        copy = remote(gains, seen.at[me], gsend.at[j - 1], grecv.at[j - 1], "seq", to)
-        copy.start()
-        small.append(copy)
         for i, ref in enumerate((wq, wk, wv)):
             columns = pl.ds(pl.multiple_of(to * widths[i], 128), widths[i])
             copies.append(
@@ -234,44 +241,23 @@
                     to,
                 )
             )
-    for copy in copies:
-        copy.start()
-    keeps = []
     for i, ref in enumerate((wq, wk, wv)):
         columns = pl.ds(pl.multiple_of(me * widths[i], 128), widths[i])
-        keeps.append(
+        copies.append(
             pltpu.make_async_copy(
                 ref.at[:, columns], out.at[me, :, pl.ds(begins[i], widths[i])], local.at[i]
             )
         )
-    keeps.append(pltpu.make_async_copy(gains, seen.at[me], local.at[3]))
-    for keep in keeps:
-        keep.start()
-    keeps[3].wait()
-    for copy in small:
+    for copy in copies:
+        copy.start()
+    for copy in copies:
         copy.wait()
-    last = pltpu.make_async_copy(seen, all_gains.at[spot], local.at[4])
-    last.start()
-    wide = []
-    for j in range(1, nf):
-        to = lax.rem(spot + j, nf)
-        copy = remote(
-            seen, all_gains.at[spot], gsend.at[n + j - 2], grecv.at[n + j - 2], "fsdp", to
-        )
-        copy.start()
-        wide.append(copy)
-    for copy in copies + wide:
-        copy.wait()
-    for keep in keeps[:3] + [last]:
-        keep.wait()
-
-
-def hidden_weights_out(n, x, wg, wu, wd, xg, gu, dn, send, recv, asend, arecv, local):
+
+
+def start_columns(n, views, send, recv, local):
     me = lax.axis_index("seq")
-    greet(others("seq", n))
-    width = wg.shape[1] // n
+    width = views[0][0].shape[1] // n
     copies, keeps = [], []
-    views = [(wg, gu, 0), (wu, gu, 1), (wd, dn, 0)]
     for i, (ref, out, place) in enumerate(views):
         for j in range(1, n):
             to = lax.rem(me + j, n)
@@ -293,23 +279,199 @@
                 ref.at[:, columns], out.at[me, :, pl.ds(place * width, width)], local.at[i]
             )
         )
-    for copy in copies:
+    for copy in copies + keeps:
         copy.start()
-    for keep in keeps:
+    return copies + keeps
+
+
+def gate_up_out(n, nf, wg, wu, gains, gu, all_gains, seen, send, recv, local, gsend, grecv, glocal):
+    me, spot = lax.axis_index("seq"), lax.axis_index("fsdp")
+    greet(others("seq", n) + others("fsdp", nf))
+    small = []
+    for j in range(1, n):
+        to = lax.rem(me + j, n)
+        small.append(
+            remote(gains, seen.at[me], gsend.at[j - 1], grecv.at[j - 1], "seq", to)
+        )
+    keep = pltpu.make_async_copy(gains, seen.at[me], glocal.at[0])
+    for copy in small + [keep]:
+        copy.start()
+    copies = start_columns(n, [(wg, gu, 0), (wu, gu, 1)], send, recv, local)
+    for copy in small + [keep]:
+        copy.wait()
+    wide = [pltpu.make_async_copy(seen, all_gains.at[spot], glocal.at[1])]
+    for j in range(1, nf):
+        to = lax.rem(spot + j, nf)
+        k = n + j - 2
+        wide.append(
+            remote(seen, all_gains.at[spot], gsend.at[k], grecv.at[k], "fsdp", to)
+        )
+    for copy in wide:
+        copy.start()
+    for copy in copies + wide:
+        copy.wait()
+
+
+def line_gather(own, out, send, recv, local):
+    spot = lax.axis_index("fsdp")
+    z = lax.div(spot, 2)
+    twin = spot + 1 - 2 * lax.rem(spot, 2)
+    keep = pltpu.make_async_copy(own, out.at[spot], local)
+    keep.start()
+
+    def up(k):
+        block = spot - 2 * k
+        return remote(
+            own if k == 0 else out.at[block], out.at[block], send.at[k], recv.at[k], "fsdp", spot + 2
+        )
+
+    def down(k):
+        block = spot + 2 * k
+        return remote(
+            own if k == 0 else out.at[block],
+            out.at[block],
+            send.at[3 + k],
+            recv.at[3 + k],
+            "fsdp",
+            spot - 2,
+        )
+
+    def over(offset):
+        block = spot + 2 * offset
+        return remote(
+            own if offset == 0 else out.at[block],
+            out.at[block],
+            send.at[6 + lax.div(block, 2)],
+            recv.at[6 + lax.div(block, 2)],
+            "fsdp",
+            twin,
+        )
+
+    def from_twin(offset):
+        block = twin + 2 * offset
+        return remote(
+            own, out.at[block], send.at[6 + lax.div(block, 2)], recv.at[6 + lax.div(block, 2)], "fsdp", twin
+        )
+
+    @pl.when(z < 3)
+    def _():
+        up(0).start()
+
+    @pl.when(z > 0)
+    def _():
+        down(0).start()
+
+    over(0).start()
+    for k in range(1, 4):
+
+        @pl.when(z >= k)
+        def _():
+            up(k - 1).wait_recv()
+            if k < 3:
+
+                @pl.when(z < 3)
+                def _():
+                    up(k).start()
+
+            over(-k).start()
+
+        @pl.when(z + k <= 3)
+        def _():
+            down(k - 1).wait_recv()
+            if k < 3:
+
+                @pl.when(z > 0)
+                def _():
+                    down(k).start()
+
+            over(k).start()
+
+    from_twin(0).wait_recv()
+    over(0).wait_send()
+    for k in range(1, 4):
+
+        @pl.when(z >= k)
+        def _():
+            from_twin(-k).wait_recv()
+            over(-k).wait_send()
+
+        @pl.when(z + k <= 3)
+        def _():
+            from_twin(k).wait_recv()
+            over(k).wait_send()
+
+    for k in range(3):
+
+        @pl.when((z >= k) & (z < 3))
+        def _():
+            up(k).wait_send()
+
+        @pl.when((z + k <= 3) & (z > 0))
+        def _():
+            down(k).wait_send()
+
+    keep.wait()
+
+
+def greet_line(places):
+    spot = lax.axis_index("fsdp")
+    z = lax.div(spot, 2)
+    twin = spot + 1 - 2 * lax.rem(spot, 2)
+    barrier = pltpu.get_barrier_semaphore()
+    for axis, index in places + [("fsdp", twin)]:
+        pl.semaphore_signal(barrier, inc=1, device_id={axis: index}, device_id_type=MESH)
+
+    @pl.when(z < 3)
+    def _():
+        pl.semaphore_signal(barrier, inc=1, device_id={"fsdp": spot + 2}, device_id_type=MESH)
+
+    @pl.when(z > 0)
+    def _():
+        pl.semaphore_signal(barrier, inc=1, device_id={"fsdp": spot - 2}, device_id_type=MESH)
+
+    inner = (z < 3).astype(jnp.int32) + (z > 0).astype(jnp.int32)
+    pl.semaphore_wait(barrier, len(places) + 1 + inner)
+
+
+def entry_stage(n, nf, line, x, wd, w_out, xg, dn, wo, send, recv, local, wsend, wrecv, wlocal, lsend, lrecv, llocal):
+    if line:
+        greet_line(others("seq", n))
+    else:
+        greet(others("seq", n))
+    start, relay, finish = gather_parts(n, x, xg, send, recv, local)
+    start()
+    copies = start_columns(n, [(wd, dn, 0)], wsend, wrecv, wlocal)
+    if line:
+        line_gather(w_out, wo, lsend, lrecv, llocal)
+    else:
+        keep = pltpu.make_async_copy(w_out, wo.at[0], llocal)
         keep.start()
-    gather(n, x, xg, asend, arecv, local.at[3])
+        keep.wait()
+    relay()
+    finish()
     for copy in copies:
         copy.wait()
-    for keep in keeps:
-        keep.wait()
-
-
-def gather_alone(n, x, out, send, recv, local):
-    greet(ring_places(n))
-    gather(n, x, out, send, recv, local)
-
-
-def project(x_ref, gain_ref, w_ref, gq_ref, gk_ref, cos_ref, sin_ref, n1_ref, qraw_ref, kraw_ref, q_ref, k_ref, v_ref, kt_ref, vt_ref):
+
+
+def half_gather(n, begin, cot, cg, send, recv, local):
+    at = pl.ds(begin, cot.shape[0] // 2)
+    start, relay, finish = gather_parts(n, cot.at[at], cg.at[:, at], send, recv, local)
+    step, steps = pl.program_id(0), pl.num_programs(0)
+
+    @pl.when(step == 0)
+    def _():
+        greet(ring_places(n))
+        start()
+
+    @pl.when(step == steps - 1)
+    def _():
+        relay()
+
+    return finish
+
+
+def project(n, x_ref, gain_ref, w_ref, gq_ref, gk_ref, cos_ref, sin_ref, cot, n1_ref, qraw_ref, kraw_ref, q_ref, k_ref, v_ref, kt_ref, vt_ref, cg, send, recv, local):
+    finish_half = half_gather(n, 0, cot, cg, send, recv, local)
     x = x_ref[...].astype(F32)
     normed = (x * inverse_rms(x) * gain_ref[...]).astype(BF)
     n1_ref[...] = normed
@@ -335,6 +497,10 @@
         k_ref[:, h * 128 : h * 128 + 128] = turned.astype(BF)
         kt_ref[h * 128 : h * 128 + 128, :] = turned.T.astype(BF)
 
+    @pl.when(pl.program_id(0) == pl.num_programs(0) - 1)
+    def _():
+        finish_half()
+
 
 def bias_of(low_ref, high_ref, keys):
     key = lax.broadcasted_iota(jnp.int32, (keys, low_ref.shape[1]), 0)
@@ -342,7 +508,8 @@
     return jnp.where(fine, 0.0, masked_score)
 
 
-def attend(q_ref, k_ref, vt_ref, wo_ref, low_ref, high_ref, attn_ref, lse_ref, part_ref, bias):
+def attend(n, q_ref, k_ref, vt_ref, wo_ref, low_ref, high_ref, cot, cg_half, attn_ref, lse_ref, part_ref, cg, bias, send, recv, local):
+    finish_half = half_gather(n, cot.shape[0] // 2, cot, cg, send, recv, local)
     keys = k_ref.shape[0]
     bias[...] = bias_of(low_ref, high_ref, keys)
     heads = q_ref.shape[1] // 128
@@ -362,6 +529,10 @@
         attn_ref[:, h * 128 : h * 128 + 128] = (mixed / total).T.astype(BF)
     part_ref[...] = dot(attn_ref[...], wo_ref[...]).astype(BF)
 
+    @pl.when(pl.program_id(0) == pl.num_programs(0) - 1)
+    def _():
+        finish_half()
+
 
 def middle_stage(n, part, x, gain, x2, n2, slots, stage, own, send, recv, asend, arecv, local):
     greet(ring_places(n))
@@ -414,37 +585,41 @@
     gather(n, own, dz, asend, arecv, local)
 
 
-def out_stage(n, part, x2, out, slots, stage, send, recv):
-    greet(ring_places(n))
-
-    def finish(at, total):
-        out[at] = (x2[at] + total).astype(BF)
-
-    scatter_sum(n, part, slots, stage, send, recv, finish)
-
-
-def input_stage(n, part, x, dx2, gain, out, dgain, slots, stage, send, recv):
+def input_stage(n, part, x, gain, out, dgain, slots, stage, send, recv):
     greet(ring_places(n))
     dgain[...] = jnp.zeros_like(dgain)
 
     def finish(at, total):
         back, dg = norm_back(x[at].astype(F32), gain[...], total)
-        out[at] = (dx2[at] + back).astype(BF)
+        out[at] = back
         dgain[0:1] += dg
 
     scatter_sum(n, part, slots, stage, send, recv, finish)
 
 
-def attend_back(q_ref, qraw_ref, k_ref, kt_ref, v_ref, kraw_ref, dz_ref, wo_ref, lse_ref, low_ref, high_ref, cq_ref, sq_ref, ck_ref, sk_ref, gq_ref, gk_ref, dq_ref, dk_ref, dv_ref, dgq_ref, dgk_ref, dk_sum, dv_sum):
+def attend_back(n, q_ref, qraw_ref, k_ref, kt_ref, v_ref, kraw_ref, dz_ref, wo_ref, lse_ref, low_ref, high_ref, cq_ref, sq_ref, ck_ref, sk_ref, gq_ref, gk_ref, part, dq_ref, dk_ref, dv_ref, dgq_ref, dgk_ref, out, dk_sum, dv_sum, slots, stage, send, recv):
     kv, block = pl.program_id(0), pl.program_id(1)
     keys = k_ref.shape[0]
     ratio = q_ref.shape[1] // 128
     scale = 128 ** (-0.5)
 
-    @pl.when((kv == 0) & (block == 0))
-    def _():
+    def finish(at, total):
+        out[at] = total
+
+    start, relay, total = scatter_parts(n, part, slots, stage, send, recv, finish)
+    steps = pl.num_programs(0) * pl.num_programs(1)
+    step = kv * pl.num_programs(1) + block
+
+    @pl.when(step == 0)
+    def _():
+        greet(ring_places(n))
+        start()
         dgq_ref[...] = jnp.zeros_like(dgq_ref)
         dgk_ref[...] = jnp.zeros_like(dgk_ref)
+
+    @pl.when(step == steps // 2)
+    def _():
+        relay()
 
     @pl.when(block == 0)
     def _():
@@ -482,6 +657,34 @@
         )
         dk_ref[...] = back.astype(BF)
         dgk_ref[0:1] += dg
+
+    @pl.when(step == steps - 1)
+    def _():
+        total()
+
+
+def gradient(counts, kept, *refs):
+    a_ref, bs, out_ref, turned = refs[0], refs[1 : 1 + len(counts)], refs[-2], refs[-1]
+    spot = pl.program_id(0)
+
+    @pl.when(spot == 0)
+    def _():
+        turned[...] = a_ref[...].T
+
+    depth = out_ref.shape[1]
+    step = min(512, depth)
+    begin = 0
+    for b_ref, count in zip(bs, counts):
+
+        @pl.when((spot >= begin) & (spot < begin + count))
+        def _(b_ref=b_ref):
+            for at in range(0, turned.shape[0], step):
+                inner = at % depth
+                out_ref[at // depth, inner : inner + step, :] = dot(
+                    turned[at : at + step, :], b_ref[...]
+                ).astype(BF)
+
+        begin += count
 
 
 def qkv_back(dq_ref, dk_ref, dv_ref, w_ref, out_ref):
@@ -511,6 +714,12 @@
         copy.start()
     for copy in copies + keeps:
         copy.wait()
+
+
+def widen(pieces, *refs):
+    ins, outs = refs[: -len(pieces)], refs[-len(pieces) :]
+    for out, (i, begin, count) in zip(outs, pieces):
+        out[...] = ins[i][0, :, begin : begin + count].astype(F32)
 
 
 def gains_back(n, nf, part, out, wide, mid, seen, send, recv, local):
@@ -547,6 +756,10 @@
         copy.wait_send()
 
 
+def after(value, done):
+    return lax.optimization_barrier((value, done))[0]
+
+
 def dma(count):
     return pltpu.SemaphoreType.DMA((count,))
 
@@ -588,23 +801,30 @@
     packed = packed.at[1, :own_gain].set(norm2_gain.astype(F32))
     packed = packed.at[2, :own_head].set(q_gain.astype(F32))
     packed = packed.at[3, :own_head].set(k_gain.astype(F32))
-    wo = lax.all_gather(w_out, "fsdp", axis=0, tiled=True)
-    w_att, all_gains = pl.pallas_call(
-        functools.partial(attention_weights_out, n, nf),
-        out_shape=(shape((n, depth, cw), BF), shape((nf, n, 8, 128), F32)),
-        in_specs=[ANY] * 4,
+    w_att = pl.pallas_call(
+        functools.partial(attention_weights_out, n),
+        out_shape=shape((n, depth, cw), BF),
+        in_specs=[ANY] * 3,
+        out_specs=ANY,
+        scratch_shapes=[dma(3 * (n - 1)), dma(3 * (n - 1)), dma(3)],
+        compiler_params=comm_params(0),
+    )(w_query, w_key, w_value)
+    gu, all_gains = pl.pallas_call(
+        functools.partial(gate_up_out, n, nf),
+        out_shape=(shape((n, depth, 2 * fw), BF), shape((nf, n, 8, 128), F32)),
+        in_specs=[ANY] * 3,
         out_specs=(ANY, ANY),
         scratch_shapes=[
             pltpu.VMEM((n, 8, 128), F32),
-            dma(3 * (n - 1)),
-            dma(3 * (n - 1)),
+            dma(2 * (n - 1)),
+            dma(2 * (n - 1)),
+            dma(2),
             dma(n + nf - 2),
             dma(n + nf - 2),
-            dma(5),
+            dma(2),
         ],
-        compiler_params=comm_params(0),
-    )(w_query, w_key, w_value, packed)
-    w_att = lax.all_gather(w_att, "fsdp", axis=1, tiled=True).reshape(width, cw)
+        compiler_params=comm_params(8),
+    )(after(w_gate, w_att), w_up, packed)
     ordered = all_gains.transpose(1, 0, 2, 3)
     gain_one = ordered[:, :, 0, :own_gain].reshape(1, width)
     gain_two = ordered[:, :, 1, :own_gain].reshape(1, width)
@@ -612,24 +832,25 @@
     gain_k = ordered[:, :, 3, :own_head].reshape(1, head)
 
     wdt = w_down.T
-    xg, gu, dn = pl.pallas_call(
-        functools.partial(hidden_weights_out, n),
+    gather_sems = [dma(gather_copies(n)), dma(gather_copies(n)), pltpu.SemaphoreType.DMA]
+    line = nf == 8
+    w_att = lax.all_gather(w_att, "fsdp", axis=1, tiled=True).reshape(width, cw)
+    xg, dn, wo = pl.pallas_call(
+        functools.partial(entry_stage, n, nf, line),
         out_shape=(
             shape((n, rows, width), BF),
-            shape((n, depth, 2 * fw), BF),
             shape((n, depth, fw), BF),
+            shape((nf if line else 1, depth, width), BF),
         ),
-        in_specs=[ANY] * 4,
+        in_specs=[ANY] * 3,
         out_specs=(ANY,) * 3,
-        scratch_shapes=[
-            dma(3 * (n - 1)),
-            dma(3 * (n - 1)),
-            dma(gather_copies(n)),
-            dma(gather_copies(n)),
-            dma(4),
-        ],
+        scratch_shapes=gather_sems
+        + [dma(n - 1), dma(n - 1), dma(1), dma(10), dma(10), pltpu.SemaphoreType.DMA],
         compiler_params=comm_params(1),
-    )(tokens, w_gate, w_up, wdt)
+    )(after(tokens, gu), wdt, w_out)
+    wo = wo.reshape(-1, width)
+    if not line:
+        wo = lax.all_gather(wo, "fsdp", axis=0, tiled=True)
     gu = lax.all_gather(gu, "fsdp", axis=1, tiled=True).reshape(width, 2 * fw)
     dn = lax.all_gather(dn, "fsdp", axis=1, tiled=True).reshape(width, fw)
 
@@ -662,8 +883,8 @@
         return pl.BlockSpec((count, columns), lambda i: (0, i))
 
     blocks = group // 256
-    n1, qraw, kraw, q, k, v, kt, vt = pl.pallas_call(
-        project,
+    n1, qraw, kraw, q, k, v, kt, vt, cg = pl.pallas_call(
+        functools.partial(project, n),
         grid=(blocks,),
         out_shape=(
             shape((group, width), BF),
@@ -674,6 +895,7 @@
             shape((group, kw), BF),
             shape((kw, group), BF),
             shape((kw, group), BF),
+            shape((n, rows, width), BF),
         ),
         in_specs=[
             by_rows(256, width),
@@ -683,6 +905,7 @@
             whole((1, head)),
             by_rows(256, head),
             by_rows(256, head),
+            ANY,
         ],
         out_specs=(
             by_rows(256, width),
@@ -693,17 +916,20 @@
             by_rows(256, kw),
             by_cols(kw, 256),
             by_cols(kw, 256),
+            ANY,
         ),
-        compiler_params=plain_params(),
-    )(xg.reshape(group, width), gain_one, w_att, gain_q, gain_k, cos, sin)
-
-    attn, lse, part_out = pl.pallas_call(
-        attend,
+        scratch_shapes=gather_sems,
+        compiler_params=comm_params(11),
+    )(xg.reshape(group, width), gain_one, w_att, gain_q, gain_k, cos, sin, cotangent)
+
+    attn, lse, part_out, cg = pl.pallas_call(
+        functools.partial(attend, n),
         grid=(blocks,),
         out_shape=(
             shape((group, qw), BF),
             shape((8, group), F32),
             shape((group, width), BF),
+            shape((n, rows, width), BF),
         ),
         in_specs=[
             by_rows(256, qw),
@@ -712,18 +938,21 @@
             whole((qw, width)),
             by_cols(8, 256),
             by_cols(8, 256),
+            ANY,
+            ANY,
         ],
-        out_specs=(by_rows(256, qw), by_cols(8, 256), by_rows(256, width)),
-        scratch_shapes=[pltpu.VMEM((group, 256), F32)],
-        compiler_params=plain_params(),
-    )(q, k, vt, wo, low, high)
+        out_specs=(by_rows(256, qw), by_cols(8, 256), by_rows(256, width), ANY),
+        scratch_shapes=[pltpu.VMEM((group, 256), F32)] + gather_sems,
+        input_output_aliases={7: 3},
+        compiler_params=comm_params(3),
+    )(q, k, vt, wo, low, high, cotangent, cg)
+    cg = cg.reshape(group, width)
 
     slots = [
         pltpu.VMEM((scatter_slots(n), rows, width), BF),
         pltpu.VMEM((rows, width), BF),
     ]
     sems = [dma(max(6, n - 1)), dma(max(6, n - 1))]
-    gather_sems = [dma(gather_copies(n)), dma(gather_copies(n)), pltpu.SemaphoreType.DMA]
 
     x2, n2 = pl.pallas_call(
         functools.partial(middle_stage, n),
@@ -734,16 +963,6 @@
         compiler_params=comm_params(2),
     )(part_out.reshape(n, rows, width), tokens, gain_two)
     n2 = n2.reshape(group, width)
-
-    (cotangent_late,) = lax.optimization_barrier((cotangent, n2))[:1]
-    cg = pl.pallas_call(
-        functools.partial(gather_alone, n),
-        out_shape=shape((n, rows, width), BF),
-        in_specs=[ANY],
-        out_specs=ANY,
-        scratch_shapes=gather_sems,
-        compiler_params=comm_params(3),
-    )(cotangent_late).reshape(group, width)
 
     tile = 256
     tiles = fw // tile
@@ -764,12 +983,47 @@
         compiler_params=plain_params(),
     )(n2, gu, gu)
 
+    def product(a, *bs, into=None, dims=None, spot=None):
+        tile = 512
+        while any(b.shape[1] % tile for b in bs):
+            tile //= 2
+        counts = [b.shape[1] // tile for b in bs]
+        begins = [sum(counts[:i]) for i in range(len(bs))]
+
+        def spec(begin, count):
+            return pl.BlockSpec(
+                (group, tile), lambda i: (0, jnp.clip(i - begin, 0, count - 1))
+            )
+
+        if dims is None:
+            dims = (1, a.shape[1], sum(counts) * tile)
+        lead = a.shape[1] // dims[1]
+        across = dims[2] // tile
+        first = 0 if spot is None else spot
+        kept = [] if into is None else [into]
+        return pl.pallas_call(
+            functools.partial(gradient, counts, len(kept)),
+            grid=(sum(counts),),
+            out_shape=shape(dims, BF),
+            in_specs=[whole(a.shape)]
+            + [spec(b, c) for b, c in zip(begins, counts)]
+            + [ANY] * len(kept),
+            out_specs=pl.BlockSpec(
+                (lead, dims[1], tile),
+                lambda i: (first + lax.div(i, across), 0, lax.rem(i, across)),
+            ),
+            scratch_shapes=[pltpu.VMEM((a.shape[1], group), BF)],
+            input_output_aliases={} if into is None else {1 + len(bs): 0},
+            compiler_params=plain_params(),
+        )(a, *bs, *kept)
+
     def reduce_rows(grad, columns):
         return lax.psum_scatter(
             grad.reshape(n, width // n, columns), "fsdp", scatter_dimension=1, tiled=True
         )
 
-    dn_share = reduce_rows(dot_tn(cg, hidden).astype(BF), fw)
+    dn_grad = product(cg, hidden)
+    dn_share = reduce_rows(dn_grad, fw)
 
     dgate, dup = pl.pallas_call(
         ffn_back,
@@ -783,11 +1037,9 @@
         ],
         out_specs=(by_cols(group, tile),) * 2,
         compiler_params=plain_params(),
-    )(cg, dn, gate, up)
-
-    dgu = jnp.concatenate([dot_tn(n2, dgate).astype(BF), dot_tn(n2, dup).astype(BF)], axis=1)
-    gu_share = reduce_rows(dgu, 2 * fw)
-
+    )(cg, after(dn, dn_grad), gate, up)
+
+    gu_grad = product(n2, dgate, dup)
     part_n2 = pl.pallas_call(
         two_nt,
         grid=(blocks,),
@@ -800,7 +1052,16 @@
         ],
         out_specs=by_rows(256, width),
         compiler_params=plain_params(),
-    )(dgate, dup, gu, gu)
+    )(after(dgate, gu_grad), dup, gu, gu)
+    part_y = pl.pallas_call(
+        one_nt,
+        grid=(blocks,),
+        out_shape=shape((group, width), BF),
+        in_specs=[by_rows(256, fw), whole((width, fw))],
+        out_specs=by_rows(256, width),
+        compiler_params=plain_params(),
+    )(after(hidden, part_n2), dn)
+    gu_share = reduce_rows(after(gu_grad, (dn_share, part_y)), 2 * fw)
 
     dx2, dz, dgain_two = pl.pallas_call(
         functools.partial(back_stage, n),
@@ -813,29 +1074,16 @@
         out_specs=(VMEM, ANY, VMEM),
         scratch_shapes=slots + [pltpu.VMEM((rows, width), BF)] + sems + gather_sems,
         compiler_params=comm_params(4),
-    )(part_n2.reshape(n, rows, width), x2, cotangent, gain_two)
+    )(
+        after(part_n2, (part_y, dn_share)).reshape(n, rows, width), x2, cotangent, gain_two,
+    )
     dz = dz.reshape(group, width)
 
-    part_y = pl.pallas_call(
-        one_nt,
-        grid=(blocks,),
-        out_shape=shape((group, width), BF),
-        in_specs=[by_rows(256, fw), whole((width, fw))],
-        out_specs=by_rows(256, width),
-        compiler_params=plain_params(),
-    )(hidden, dn)
-    output = pl.pallas_call(
-        functools.partial(out_stage, n),
-        out_shape=shape((rows, width), BF),
-        in_specs=[VMEM] * 2,
-        out_specs=VMEM,
-        scratch_shapes=slots + sems,
-        compiler_params=comm_params(5),
-    )(part_y.reshape(n, rows, width), x2)
+    wo_grad = product(attn, dz, dims=(n + width // cw, qw, cw), spot=n)
 
     wide = ratio * head
-    dq, dk, dv, dgain_q, dgain_k = pl.pallas_call(
-        attend_back,
+    dq, dk, dv, dgain_q, dgain_k, branch = pl.pallas_call(
+        functools.partial(attend_back, n),
         grid=(kheads, blocks),
         out_shape=(
             shape((group, qw), BF),
@@ -843,6 +1091,7 @@
             shape((group, kw), BF),
             shape((8, head), F32),
             shape((8, head), F32),
+            shape((rows, width), F32),
         ),
         in_specs=[
             pl.BlockSpec((256, wide), lambda h, b: (b, h)),
@@ -862,6 +1111,7 @@
             whole((group, head)),
             whole((1, head)),
             whole((1, head)),
+            VMEM,
         ],
         out_specs=(
             pl.BlockSpec((256, wide), lambda h, b: (b, h)),
@@ -869,16 +1119,22 @@
             pl.BlockSpec((group, head), lambda h, b: (0, h)),
             whole((8, head)),
             whole((8, head)),
+            VMEM,
         ),
-        scratch_shapes=[pltpu.VMEM((group, head), F32), pltpu.VMEM((group, head), F32)],
-        compiler_params=plain_params(),
-    )(q, qraw, k, kt, v, kraw, dz, wo, lse, low, high, cos, sin, cos, sin, gain_q, gain_k)
-
-    wo_share = lax.psum_scatter(
-        dot_tn(attn, dz).astype(BF), "fsdp", scatter_dimension=0, tiled=True
+        scratch_shapes=[pltpu.VMEM((group, head), F32), pltpu.VMEM((group, head), F32)]
+        + slots
+        + sems,
+        compiler_params=comm_params(5),
+    )(
+        q, qraw, k, kt, v, kraw, dz, wo, lse, low, high, cos, sin, cos, sin, gain_q, gain_k,
+        part_y.reshape(n, rows, width),
     )
-    dqkv = jnp.concatenate([dq, dk, dv], axis=1)
-    att_share = reduce_rows(dot_tn(n1, dqkv).astype(BF), cw)
+    output = (x2 + branch).astype(BF)
+
+    att_grad = product(n1, dq, dk, dv, into=wo_grad, dims=wo_grad.shape)
+    att_share = lax.psum_scatter(
+        after(att_grad, gu_share), "fsdp", scatter_dimension=1, tiled=True
+    )
 
     part_n1 = pl.pallas_call(
         qkv_back,
@@ -892,15 +1148,16 @@
         ],
         out_specs=by_rows(256, width),
         compiler_params=plain_params(),
-    )(dq, dk, dv, w_att)
-    input_grad, dgain_one = pl.pallas_call(
+    )(after(dq, att_grad), dk, dv, w_att)
+    back_one, dgain_one = pl.pallas_call(
         functools.partial(input_stage, n),
-        out_shape=(shape((rows, width), BF), shape((8, width), F32)),
-        in_specs=[VMEM] * 4,
+        out_shape=(shape((rows, width), F32), shape((8, width), F32)),
+        in_specs=[VMEM] * 3,
         out_specs=(VMEM, VMEM),
         scratch_shapes=slots + sems,
-        compiler_params=comm_params(6),
-    )(part_n1.reshape(n, rows, width), tokens, dx2, gain_one)
+        compiler_params=comm_params(10),
+    )(part_n1.reshape(n, rows, width), tokens, gain_one)
+    input_grad = (dx2 + back_one).astype(BF)
 
     def owned(row, count):
         cut = row.reshape(n, nf, 1, count)
@@ -936,34 +1193,49 @@
         count = len(arrays)
         return pl.pallas_call(
             functools.partial(exchange, n, count),
-            out_shape=tuple(shape(a.shape, a.dtype) for a in arrays),
+            out_shape=tuple(shape((n,) + a.shape[1:], BF) for a in arrays),
             in_specs=[ANY] * count,
             out_specs=(ANY,) * count,
             scratch_shapes=[dma(count * (n - 1)), dma(count * (n - 1)), dma(count)],
             compiler_params=comm_params(number),
         )(*arrays)
 
-    gu_mine, dn_mine = swap(8, gu_share, dn_share)
-    (att_mine,) = swap(9, att_share)
-
-    def assemble(array, begin, count):
-        return array[:, :, begin : begin + count].transpose(1, 0, 2).reshape(depth, -1).astype(F32)
+    def spread(arrays, pieces):
+        ins = [pl.BlockSpec((1, depth, a.shape[2]), lambda i: (i, 0, 0)) for a in arrays]
+        outs = [by_cols(depth, count) for _, _, count in pieces]
+        shapes = [shape((depth, n * count), F32) for _, _, count in pieces]
+        return pl.pallas_call(
+            functools.partial(widen, pieces),
+            grid=(n,),
+            out_shape=tuple(shapes),
+            in_specs=ins,
+            out_specs=tuple(outs),
+            compiler_params=plain_params(),
+        )(*arrays)
+
+    gu_mine, dn_mine = swap(6, gu_share, after(dn_share, gains))
+    gate_grad, up_grad, down_grad = spread(
+        [gu_mine, dn_mine], [(0, 0, fw), (0, fw, fw), (1, 0, fw)]
+    )
+    wide_grads = (gate_grad, up_grad, down_grad.T)
+    wo_out = att_share[n:].transpose(1, 0, 2).reshape(depth, width).astype(F32)
+    (att_mine,) = swap(9, after(att_share, (gains, wide_grads, input_grad, output)))
+    wq_grad, wk_grad, wv_grad = spread(
+        [att_mine], [(0, 0, qw), (0, qw, kw), (0, qw + kw, kw)]
+    )
 
     return (
         output,
         input_grad,
         gains[0, :own_gain],
-        assemble(att_mine, 0, qw),
-        assemble(att_mine, qw, kw),
-        assemble(att_mine, qw + kw, kw),
+        wq_grad,
+        wk_grad,
+        wv_grad,
         gains[2, :own_head],
         gains[3, :own_head],
-        wo_share.astype(F32),
+        wo_out,
         gains[1, :own_gain],
-        assemble(gu_mine, 0, fw),
-        assemble(gu_mine, fw, fw),
-        assemble(dn_mine, 0, fw).T,
-    )
+    ) + wide_grads
 
 
 def solution(mesh):

time: 737 us -> 599 us (0.81)
  waiting for transfers between devices: 77.8 us -> 1.08 us
  matrix products: 44.1 us -> 0 us
  Pallas kernels: 527 us -> 555 us
  local copies, waits for them, and re-layouts: 38.8 us -> 13.2 us
  other arithmetic: 27.8 us -> 12.3 us
    reduce_scatter x3 -> x2, waiting for transfers between devices: 53.2 us -> 0.92 us  [reduce_rows(): lax.psum_scatter(grad.reshape(n, width // n, columns), 'fsdp', scatter_di...]
    dot_general x5 -> x0, matrix products: 44.1 us -> none  [dot_tn(): lax.dot_general(a, b, (((0,), (0,)), ((), ())), preferred_element_type=F32)]
    pallas_call x7 -> x12, Pallas kernels: 208 us -> 236 us  [the longest x1 61.9 us: shards(): pl.pallas_call(functools.partial(entry_stage, n, nf, line), out_shape=(sh...]
    all_gather x1, waiting for transfers between devices: 23.2 us -> 0.02 us  [shards(): dn = lax.all_gather(dn, 'fsdp', axis=1, tiled=True).reshape(width, fw)]
    concatenate x1 -> x0, local copies, waits for them, and re-layouts: 16.5 us -> none  [shards(): jnp.concatenate([dot_tn(n2, dgate).astype(BF), dot_tn(n2, dup).astype(BF)...]
    concatenate x1 -> x0, other arithmetic: 14.9 us -> none  [shards(): jnp.concatenate([dot_tn(n2, dgate).astype(BF), dot_tn(n2, dup).astype(BF)...]
  transfers between devices with their start and end apart: 8 -> 6, of which waited for: 2 -> 2; matrix products, arithmetic and copies ran while one was open for 13% -> 4% of each run, Pallas kernels for 51% -> 89%
where the time goes in v2:
time: 599 us; the launch traced here: 598 us
  Pallas kernels  555 us (93%)
  between operations  15.8 us (3%)
  local copies, waits for them, and re-layouts  13.2 us (2%)
  other arithmetic  12.3 us (2%)
    pallas_call x1, Pallas kernels, shards(): pl.pallas_call(functools.partial(back_stage, n), out_shape=(shape((rows,...  73.6 us
    pallas_call x1, Pallas kernels, shards(): pl.pallas_call(functools.partial(middle_stage, n), out_shape=(shape((rows...  72.4 us
    pallas_call x1, Pallas kernels, shards(): pl.pallas_call(functools.partial(entry_stage, n, nf, line), out_shape=(sh...  61.9 us
    pallas_call x4, Pallas kernels, product(): pl.pallas_call(functools.partial(gradient, counts, len(kept)), grid=(sum(...  49.1 us
    pallas_call x1, Pallas kernels, shards(): pl.pallas_call(functools.partial(input_stage, n), out_shape=(shape((rows,...  40.6 us
    pallas_call x2, Pallas kernels, swap(): pl.pallas_call(functools.partial(exchange, n, count), out_shape=tuple((sh...  39.4 us
    pallas_call x1, Pallas kernels, shards(): pl.pallas_call(functools.partial(attend_back, n), grid=(kheads, blocks),...  38.6 us
    pallas_call x1, Pallas kernels, shards(): pl.pallas_call(functools.partial(gate_up_out, n, nf), out_shape=(shape((n...  23.8 us
  transfers between devices with their start and end apart: 6, of which 2 were waited for; matrix products, arithmetic and copies ran while one was open for 4% of the time, Pallas kernels for 89%

profile of v2, /device:TPU:0, one launch (start us, length us, event | category | flops | bytes accessed | tf_op | source)
XLA Modules:
  0.0 597.9 jit_solution(7931279919276619858)
XLA Ops:
  7.2 11.1 %shard_map.255 = bf16[4,64,1024]{2,1,0:T(8,128)(2,1)} custom-call(bf16[64,2048]{1,0:T(8,128)(2,1)} %wq.1, bf16[64,1024]{1,0:T(8,128)(2,1)} %wk.1, bf16[64,1024]{1,0:T(8,128)(2,1)} %wv.1), custom_call_target="tpu_custom_call" | custom-call | tf_op jit(solution)/shard_map/pallas_call | solution.py:804
  18.4 0.7 pad_convert_fusion
  19.1 0.7 bitcast_convert_fusion.2
  19.8 0.7 bitcast_convert_fusion.1
  20.6 0.7 bitcast_convert_fusion
  21.9 23.8 %shard_map.256 = (bf16[4,64,3072]{2,1,0:T(8,128)(2,1)}, f32[8,4,8,128]{3,2,1,0:T(8,128)}) custom-call(bf16[64,6144]{1,0:T(8,128)(2,1)} %wg, bf16[64,6144]{1,0:T(8,128)(2,1)} %wu.1, f32[8,128]{1,0:T(8,128)} %copy-done.4), custom_call_target="tpu_custom_call" | custom-call | tf_op jit(solution)/shard_map/pallas_call | solution.py:812
  45.8 61.9 %shard_map.257 = (bf16[4,256,2048]{2,1,0:T(8,128)(2,1)}, bf16[4,64,1536]{2,1,0:T(8,128)(2,1)}, bf16[8,64,2048]{2,1,0:T(8,128)(2,1)}) custom-call(bf16[256,2048]{1,0:T(8,128)(2,1)} %x.14, bf16[64,6144]{1,0:T(8,128)(2,1)} %bitcast.84, bf16[64,2048]{1,0:T(8,128)(2,1)} %w_out.1), custom_call_target="tpu_custom_call" | custom-call | tf_op jit(solution)/shard_map/pallas_call | solution.py:838
  107.9 0.7 reshape_squeeze.24.gain_ref.gain
  108.6 0.6 reshape_squeeze.25.gq_ref
  109.2 0.6 reshape_squeeze.26.gk_ref
  109.8 0.7 reshape_squeeze.27.gain
  112.4 0.7 subtract_convert_fusion
  113.2 1.9 fusion
  115.1 1.3 pad_maximum_fusion
  116.4 0.7 add_maximum_fusion
  117.1 23.1 %shard_map.258 = (bf16[1024,2048]{1,0:T(8,128)(2,1)}, f32[1024,512]{1,0:T(8,128)}, f32[1024,256]{1,0:T(8,128)}, bf16[1024,512]{1,0:T(8,128)(2,1)}, bf16[1024,256...) custom-call(bf16[1024,2048]{1,0:T(8,128)(2,1)} %bitcast.83, ...), custom_call_target="tpu_custom_call" | custom-call | tf_op jit(solution)/shard_map/pallas_call | solution.py:886
  140.2 0.6 broadcast_in_dim.33.low_ref
  141.5 20.8 %shard_map.259 = (bf16[1024,512]{1,0:T(8,128)(2,1)}, f32[8,1024]{1,0:T(8,128)}, bf16[1024,2048]{1,0:T(8,128)(2,1)}, bf16[4,256,2048]{2,1,0:T(8,128)(2,1)}) custom-call(bf16[1024,512]{1,0:T(8,128)(2,1)} %get-tuple-element.121.q_ref, bf16[1024,256]{1,0:T(8,128)(2,1)} %get-tuple-element.122.k_ref, ...), custom_call_target="tpu_custom_call", output_to_operand_aliasing={{3}: (7, {})} | custom-call | tf_op jit(solution)/shard_map/pallas_call | solution.py:925
  162.3 72.4 %shard_map.260 = (f32[256,2048]{1,0:T(8,128)}, bf16[4,256,2048]{2,1,0:T(8,128)(2,1)}) custom-call(bf16[4,256,2048]{2,1,0:T(8,128)(2,1)} %bitcast.82, bf16[256,2048]{1,0:T(8,128)(2,1)} %x.14, f32[1,2048]{1,0:T(1,128)} %reshape_squeeze.27.gain), custom_call_target="tpu_custom_call" | custom-call | tf_op jit(solution)/shard_map/pallas_call | solution.py:957
  234.7 19.3 %shard_map.261 = (f32[1024,1536]{1,0:T(8,128)}, f32[1024,1536]{1,0:T(8,128)}, bf16[1024,1536]{1,0:T(8,128)(2,1)}) custom-call(bf16[1024,2048]{1,0:T(8,128)(2,1)} %bitcast.75, bf16[2048,3072]{1,0:T(8,128)(2,1)} %bitcast.61, bf16[2048,3072]{1,0:T(8,128)(2,1)} %bitcast.62), custom_call_target="tpu_custom_call" | custom-call | tf_op jit(solution)/shard_map/pallas_call | solution.py:969
  254.0 12.3 %shard_map.262 = bf16[1,2048,1536]{2,1,0:T(8,128)(2,1)} custom-call(bf16[1024,2048]{1,0:T(8,128)(2,1)} %bitcast.66, bf16[1024,1536]{1,0:T(8,128)(2,1)} %get-tuple-element.142.refs_1_.a_ref), custom_call_target="tpu_custom_call" | custom-call | tf_op jit(solution)/shard_map/pallas_call | solution.py:1004
  266.4 15.6 %shard_map.263 = (bf16[1024,1536]{1,0:T(8,128)(2,1)}, bf16[1024,1536]{1,0:T(8,128)(2,1)}) custom-call(bf16[1024,2048]{1,0:T(8,128)(2,1)} %bitcast.67, bf16[2048,1536]{1,0:T(8,128)(2,1)} %bitcast.69, f32[1024,1536]{1,0:T(8,128)} %get-tuple-element.137.gate_ref, f32[1024,1536]{1,0:T(8,128)} %get-tuple-element.138.up_ref), custom_call_target="tpu_custom_call" | custom-call | tf_op jit(solution)/shard_map/pallas_call | solution.py:1028
  282.0 20.0 %shard_map.264 = bf16[1,2048,3072]{2,1,0:T(8,128)(2,1)} custom-call(bf16[1024,2048]{1,0:T(8,128)(2,1)} %bitcast.76, bf16[1024,1536]{1,0:T(8,128)(2,1)} %get-tuple-element.141.refs_1_.a_ref, bf16[1024,1536]{1,0:T(8,128)(2,1)} %get-tuple-element.140.refs_2_.b_ref), custom_call_target="tpu_custom_call" | custom-call | tf_op jit(solution)/shard_map/pallas_call | solution.py:1004
  302.0 20.0 %shard_map.265 = bf16[1024,2048]{1,0:T(8,128)(2,1)} custom-call(bf16[1024,1536]{1,0:T(8,128)(2,1)} %get-tuple-element.141.refs_1_.a_ref, bf16[1024,1536]{1,0:T(8,128)(2,1)} %get-tuple-element.140.refs_2_.b_ref, bf16[2048,3072]{1,0:T(8,128)(2,1)} %bitcast.63, bf16[2048,3072]{1,0:T(8,128)(2,1)} %bitcast.64), custom_call_target="tpu_custom_call" | custom-call | tf_op jit(solution)/shard_map/pallas_call | solution.py:1043
  322.0 11.5 %shard_map.266 = bf16[1024,2048]{1,0:T(8,128)(2,1)} custom-call(bf16[1024,1536]{1,0:T(8,128)(2,1)} %get-tuple-element.142.refs_1_.a_ref, bf16[2048,1536]{1,0:T(8,128)(2,1)} %bitcast.70), custom_call_target="tpu_custom_call" | custom-call | tf_op jit(solution)/shard_map/pallas_call | solution.py:1056
  333.8 73.6 %shard_map.267 = (f32[256,2048]{1,0:T(8,128)}, bf16[4,256,2048]{2,1,0:T(8,128)(2,1)}, f32[8,2048]{1,0:T(8,128)}) custom-call(bf16[4,256,2048]{2,1,0:T(8,128)(2,1)} %bitcast.71, f32[256,2048]{1,0:T(8,128)} %get-tuple-element.127.x2, bf16[256,2048]{1,0:T(8,128)(2,1)} %cot.5, f32[1,2048]{1,0:T(1,128)} %reshape_squeeze.27.gain), custom_call_target="tpu_custom_call" | custom-call | tf_op jit(solution)/shard_map/pallas_call | solution.py:1066
  407.4 6.5 %shard_map.269.refs_4_ = bf16[6,512,1024]{2,1,0:T(8,128)(2,1)} custom-call(bf16[1024,512]{1,0:T(8,128)(2,1)} %get-tuple-element.152.refs_0_, bf16[1024,2048]{1,0:T(8,128)(2,1)} %bitcast.78), custom_call_target="tpu_custom_call" | custom-call | tf_op jit(solution)/shard_map/pallas_call | solution.py:1004
  413.9 38.6 %shard_map.268 = (bf16[1024,512]{1,0:T(8,128)(2,1)}, bf16[1024,256]{1,0:T(8,128)(2,1)}, bf16[1024,256]{1,0:T(8,128)(2,1)}, f32[8,128]{1,0:T(8,128)}, f32[8,128]{1,0:T(8,128)}, /*index=5*/f32[256,2048]{1,0:T(8,128)}) custom-call(bf16[1024,512]{1,0:T(8,128)(2,1)} %get-tuple-element.121.q_ref, f32[1024,512]{1,0:T(8,128)} %get-tuple-element.128.qraw_ref, ...), custom_call_target="tpu_custom_call" | custom-call | tf_op jit(solution)/shard_map/pallas_call | solution.py:1085
  452.6 10.3 %shard_map.270 = bf16[6,512,1024]{2,1,0:T(8,128)(2,1)} custom-call(bf16[1024,2048]{1,0:T(8,128)(2,1)} %get-tuple-element.149.refs_0_, bf16[1024,512]{1,0:T(8,128)(2,1)} %get-tuple-element.153.refs_1_.dq_ref, bf16[1024,256]{1,0:T(8,128)(2,1)} %get-tuple-element.150.refs_2_.dk_ref, ...), custom_call_target="tpu_custom_call", output_to_operand_aliasing={{}: (4, {})} | custom-call | tf_op jit(solution)/shard_map/pallas_call | solution.py:1004
  462.9 0.6 reduce-scatter.6.cloned.1.call-done.refs_0_
  463.5 8.8 %shard_map.271 = bf16[1024,2048]{1,0:T(8,128)(2,1)} custom-call(bf16[1024,512]{1,0:T(8,128)(2,1)} %get-tuple-element.153.refs_1_.dq_ref, bf16[1024,256]{1,0:T(8,128)(2,1)} %get-tuple-element.150.refs_2_.dk_ref, bf16[1024,256]{1,0:T(8,128)(2,1)} %get-tuple-element.151.refs_3_.dv_ref, bf16[2048,1024]{1,0:T(8,128)(2,1)} %bitcast.74), custom_call_target="tpu_custom_call" | custom-call | tf_op jit(solution)/shard_map/pallas_call | solution.py:1139
  472.3 40.6 %shard_map.272 = (f32[256,2048]{1,0:T(8,128)}, f32[8,2048]{1,0:T(8,128)}) custom-call(bf16[4,256,2048]{2,1,0:T(8,128)(2,1)} %bitcast.72, bf16[256,2048]{1,0:T(8,128)(2,1)} %x.14, f32[1,2048]{1,0:T(1,128)} %reshape_squeeze.24.gain_ref.gain), custom_call_target="tpu_custom_call" | custom-call | tf_op jit(solution)/shard_map/pallas_call | solution.py:1152
  513.0 0.9 slice_reduce_fusion.1
  513.9 0.9 slice_reduce_fusion
  514.9 0.7 slice_reduce_fusion.3
  515.8 0.7 slice_reduce_fusion.2
  516.7 0.8 concatenate.19
  517.4 18.1 %shard_map.273 = f32[8,128]{1,0:T(8,128)} custom-call(f32[8,4,8,128]{3,2,1,0:T(8,128)} %bitcast.86), custom_call_target="tpu_custom_call" | custom-call | tf_op jit(solution)/shard_map/pallas_call | solution.py:1176
  535.6 1.4 slice_bitcast_fusion
  537.0 1.3 slice_bitcast_fusion.1
  538.2 2.8 add_convert_fusion.1
  541.1 1.2 add_convert_fusion
  542.3 30.0 %shard_map.274 = (bf16[4,64,3072]{2,1,0:T(8,128)(2,1)}, bf16[4,64,1536]{2,1,0:T(8,128)(2,1)}) custom-call(bf16[4,64,3072]{2,1,0:T(8,128)(2,1)} %reduce-scatter.6.cloned.1.call-done.refs_0_, bf16[4,64,1536]{2,1,0:T(8,128)(2,1)} %reduce-scatter.4.cloned.1.call-done.refs_1_), custom_call_target="tpu_custom_call" | custom-call | tf_op jit(solution)/shard_map/pallas_call | solution.py:1194
  572.3 4.3 shard_map.275
  576.6 9.4 %shard_map.276.refs_0_ = bf16[4,64,1024]{2,1,0:T(8,128)(2,1)} custom-call(bf16[6,64,1024]{2,1,0:T(8,128)(2,1)} %reduce-scatter.8.cloned.1.call-done.refs_0_), custom_call_target="tpu_custom_call" | custom-call | tf_op jit(solution)/shard_map/pallas_call | solution.py:1194
  586.0 3.2 shard_map.277
  589.2 1.0 convert_bitcast_fusion
  590.2 0.8 copy.55
  (60 shorter events, 3.4 us)
Async XLA Ops:
  7.2 109.9 %all-gather.4.cloned.1.call-start = ((), (), s32[]{:S(2)}) async-start(), calls=%async_computation.3 | async-start | bytes 4718592 | tf_op jit(solution)/shard_map/all_gather | solution.py:837
  18.3 216.3 %all-gather.8.cloned.1.call-start = ((), (), s32[]{:S(2)}) async-start(), calls=%async_computation.5 | async-start | bytes 14155776 | tf_op jit(solution)/shard_map/all_gather | solution.py:854
  21.3 0.6 copy-start.4
  21.9 88.6 %copy-start.5 = (s32[1,3]{1,0:T(1,128)S(1)}, s32[1,3]{1,0:T(1,128)}, u32[]{:S(2)}) copy-start(s32[1,3]{1,0:T(1,128)} %param.25) | copy-start | bytes 40
  21.9 91.2 %copy-start.6 = (s32[1,2]{1,0:T(1,128)S(1)}, s32[1,2]{1,0:T(1,128)}, u32[]{:S(2)}) copy-start(s32[1,2]{1,0:T(1,128)} %param.26) | copy-start | bytes 28
  21.9 91.2 %copy-start.7 = (s32[1,2]{1,0:T(1,128)S(1)}, s32[1,2]{1,0:T(1,128)}, u32[]{:S(2)}) copy-start(s32[1,2]{1,0:T(1,128)} %param.27) | copy-start | bytes 28
  45.7 62.1 %copy-start.3 = (f32[8,4,8,128]{3,2,1,0:T(8,128)S(1)}, f32[8,4,8,128]{3,2,1,0:T(8,128)}, u32[]{:S(2)}) copy-start(f32[8,4,8,128]{3,2,1,0:T(8,128)} %get-tuple-element.120) | copy-start | bytes 393220
  45.7 220.7 %all-gather.6.cloned.1.call-start = ((), (), s32[]{:S(2)}) async-start(), calls=%async_computation.4 | async-start | bytes 7077888 | tf_op jit(solution)/shard_map/all_gather | solution.py:855
  107.8 226.0 %reduce-scatter.4.cloned.1.call-start = ((), (), s32[]{:S(2)}) async-start(), calls=%async_computation.6 | async-start | bytes 7077888 | tf_op jit(solution)/shard_map/reduce_scatter | solution.py:1021
  266.4 197.1 %reduce-scatter.6.cloned.1.call-start = ((), (), s32[]{:S(2)}) async-start(), calls=%async_computation.7 | async-start | bytes 14155776 | tf_op jit(solution)/shard_map/reduce_scatter | solution.py:1021
  333.8 242.8 %reduce-scatter.8.cloned.1.call-start = ((), (), s32[]{:S(2)}) async-start(), calls=%async_computation.8 | async-start | bytes 7077888 | tf_op jit(solution)/shard_map/reduce_scatter | solution.py:1135
  472.3 65.9 %copy-start = (f32[256,2048]{1,0:T(8,128)S(1)}, f32[256,2048]{1,0:T(8,128)}, u32[]{:S(2)}) copy-start(f32[256,2048]{1,0:T(8,128)} %get-tuple-element.127.x2) | copy-start | bytes 6291460
  535.6 5.5 copy-start.1
  535.6 5.5 copy-start.2
Sparse Core Ops, SparseCore 0:
  18.5 58.0 all-gather.3
  78.2 117.2 all-gather.7
  197.1 62.9 all-gather.5
  266.5 67.2 reduce-scatter.3
  335.9 127.5 reduce-scatter.5
  465.7 74.9 reduce-scatter.7

commit v3 on v2

--- a/solution.py
+++ b/solution.py
@@ -2,6 +2,7 @@
 
 import jax
 import jax.numpy as jnp
+import numpy as np
 from jax import lax
 from jax.experimental import pallas as pl
 from jax.experimental.pallas import tpu as pltpu
@@ -312,7 +313,7 @@
         copy.wait()
 
 
-def line_gather(own, out, send, recv, local):
+def line_gather(own, out, send, recv, local, between):
     spot = lax.axis_index("fsdp")
     z = lax.div(spot, 2)
     twin = spot + 1 - 2 * lax.rem(spot, 2)
@@ -362,6 +363,7 @@
         down(0).start()
 
     over(0).start()
+    between()
     for k in range(1, 4):
 
         @pl.when(z >= k)
@@ -433,7 +435,7 @@
     pl.semaphore_wait(barrier, len(places) + 1 + inner)
 
 
-def entry_stage(n, nf, line, x, wd, w_out, xg, dn, wo, send, recv, local, wsend, wrecv, wlocal, lsend, lrecv, llocal):
+def entry_stage(n, nf, line, own_gain, x, wd, w_out, gains, lengths, starts, sizes, freq, xg, dn, wo, gain_one, gain_two, gain_q, gain_k, cos, sin, low, high, send, recv, local, wsend, wrecv, wlocal, lsend, lrecv, llocal):
     if line:
         greet_line(others("seq", n))
     else:
@@ -441,13 +443,65 @@
     start, relay, finish = gather_parts(n, x, xg, send, recv, local)
     start()
     copies = start_columns(n, [(wd, dn, 0)], wsend, wrecv, wlocal)
+
+    def tables():
+        per = 128 // own_gain
+        for row in range(n * nf // per):
+            seq, first = row * per // nf, row * per % nf
+            one = gains[first, seq, 0:1, :]
+            two = gains[first, seq, 1:2, :]
+            for f in range(first + 1, first + per):
+                one += gains[f, seq, 0:1, :]
+                two += gains[f, seq, 1:2, :]
+            gain_one[:, row * 128 : row * 128 + 128] = one
+            gain_two[:, row * 128 : row * 128 + 128] = two
+        total = jnp.zeros((8, 128), F32)
+        for f in range(nf):
+            for seq in range(n):
+                total += gains[f, seq]
+        gain_q[...] = total[2:3, :]
+        gain_k[...] = total[3:4, :]
+
+        group = cos.shape[0]
+        border_one = lengths[0, 0]
+        border_two = border_one + lengths[0, 1]
+
+        def begin_of(places):
+            later = jnp.where(places >= border_one, border_one, 0)
+            return jnp.where(places >= border_two, border_two, later)
+
+        step = 128
+        lane = lax.broadcasted_iota(jnp.int32, (step, 128), 1)
+
+        def turn(number, carry):
+            at = pl.ds(pl.multiple_of(number * step, step), step)
+            places = lax.broadcasted_iota(jnp.int32, (step, 128), 0) + number * step
+            angle = (places - begin_of(places)).astype(F32) * freq[...]
+            cos[at, :] = jnp.cos(angle)
+            sine = jnp.sin(angle)
+            sin[at, :] = jnp.where(lane < 64, -sine, sine)
+            return carry
+
+        lax.fori_loop(0, group // step, turn, 0)
+        places = lax.broadcasted_iota(jnp.int32, (8, group), 1)
+        end = jnp.where(places >= border_one, border_two, border_one)
+        end = jnp.where(places >= border_two, group, end)
+        picture = jnp.zeros_like(places)
+        for i in range(starts.shape[1]):
+            first, count = starts[0, i], sizes[0, i]
+            inside = (places >= first) & (places < first + count)
+            picture = jnp.where(inside, jnp.maximum(picture, first + count), picture)
+        low[...] = begin_of(places)
+        high[...] = jnp.maximum(places, jnp.minimum(picture, end) - 1)
+
     if line:
-        line_gather(w_out, wo, lsend, lrecv, llocal)
+        line_gather(w_out, wo, lsend, lrecv, llocal, relay)
     else:
         keep = pltpu.make_async_copy(w_out, wo.at[0], llocal)
         keep.start()
+        relay()
         keep.wait()
-    relay()
+    tables()
     finish()
     for copy in copies:
         copy.wait()
@@ -566,35 +620,98 @@
     out_ref[...] = (dot_nt(a_ref[...], wa_ref[...]) + dot_nt(b_ref[...], wb_ref[...])).astype(BF)
 
 
-def one_nt(a_ref, w_ref, out_ref):
-    out_ref[...] = dot_nt(a_ref[...], w_ref[...]).astype(BF)
-
-
-def back_stage(n, part, x2, cot, gain, dx2, dz, dgain, slots, stage, own, send, recv, asend, arecv, local):
+def spread_rows(row, out):
+    for i in range(out.shape[0]):
+        out[i : i + 1, :] = row[:, i * 128 : i * 128 + 128]
+
+
+def back_stage(n, part, x2, cot, gain, hidden_far, dn_far, dx2, dz, dgain, part_y, slots, stage, own, send, recv, asend, arecv, local, row, hidden, dn, load):
     greet(ring_places(n))
-    dgain[...] = jnp.zeros_like(dgain)
+    loads = [
+        pltpu.make_async_copy(hidden_far, hidden, load.at[0]),
+        pltpu.make_async_copy(dn_far, dn, load.at[1]),
+    ]
+    for copy in loads:
+        copy.start()
+    row[...] = jnp.zeros_like(row)
+    rows, width = x2.shape
+    step = 512
+
+    def forward(to, carry):
+        at = pl.ds(pl.multiple_of(to * rows, rows), rows)
+
+        def columns(number, carry):
+            span = pl.ds(pl.multiple_of(number * step, step), step)
+            part_y[to, :, span] = dot_nt(hidden[at, :], dn[span, :]).astype(BF)
+            return carry
+
+        return lax.fori_loop(0, width // step, columns, carry)
 
     def finish(at, total):
         back, dg = norm_back(x2[at], gain[...], total)
         value = cot[at].astype(F32) + back
         dx2[at] = value
         own[at] = value.astype(BF)
-        dgain[0:1] += dg
-
-    scatter_sum(n, part, slots, stage, send, recv, finish)
-    gather(n, own, dz, asend, arecv, local)
-
-
-def input_stage(n, part, x, gain, out, dgain, slots, stage, send, recv):
+        row[...] += dg
+
+    start, relay, total = scatter_parts(n, part, slots, stage, send, recv, finish)
+    start()
+    for copy in loads:
+        copy.wait()
+    relay()
+    lax.fori_loop(0, n // 2, forward, 0)
+    total()
+    start, relay, end = gather_parts(n, own, dz, asend, arecv, local)
+    start()
+    spread_rows(row[...], dgain)
+    relay()
+    lax.fori_loop(n // 2, n, forward, 0)
+    end()
+
+
+def input_stage(n, dq, dk, dv, w, x, gain, out, dgain, part, slots, stage, send, recv, row):
     greet(ring_places(n))
-    dgain[...] = jnp.zeros_like(dgain)
+    row[...] = jnp.zeros_like(row)
+    me = lax.axis_index("seq")
+    rows, width = x.shape
+    qw, kw = dq.shape[1], dk.shape[1]
+    step = 512
+
+    def block(to):
+        at = pl.ds(pl.multiple_of(to * rows, rows), rows)
+
+        def columns(number, carry):
+            span = pl.ds(pl.multiple_of(number * step, step), step)
+            value = dot_nt(dq[at, :], w[span, pl.ds(0, qw)])
+            value += dot_nt(dk[at, :], w[span, pl.ds(qw, kw)])
+            value += dot_nt(dv[at, :], w[span, pl.ds(qw + kw, kw)])
+            part[to, :, span] = value.astype(BF)
+            return carry
+
+        lax.fori_loop(0, width // step, columns, 0)
 
     def finish(at, total):
         back, dg = norm_back(x[at].astype(F32), gain[...], total)
         out[at] = back
-        dgain[0:1] += dg
-
-    scatter_sum(n, part, slots, stage, send, recv, finish)
+        row[...] += dg
+
+    start, relay, total = scatter_parts(n, part, slots, stage, send, recv, finish)
+    if n == 4:
+        across, along, corner = square(me)
+        block(corner)
+        start(0, 2)
+        block(across)
+        start(2, 3)
+        block(along)
+        start(3, 4)
+        block(me)
+    else:
+        for j in range(n):
+            block(lax.rem(me + j, n))
+        start()
+    relay()
+    total()
+    spread_rows(row[...], dgain)
 
 
 def attend_back(n, q_ref, qraw_ref, k_ref, kt_ref, v_ref, kraw_ref, dz_ref, wo_ref, lse_ref, low_ref, high_ref, cq_ref, sq_ref, ck_ref, sk_ref, gq_ref, gk_ref, part, dq_ref, dk_ref, dv_ref, dgq_ref, dgk_ref, out, dk_sum, dv_sum, slots, stage, send, recv):
@@ -664,55 +781,83 @@
 
 
 def gradient(counts, kept, *refs):
-    a_ref, bs, out_ref, turned = refs[0], refs[1 : 1 + len(counts)], refs[-2], refs[-1]
-    spot = pl.program_id(0)
-
-    @pl.when(spot == 0)
-    def _():
+    a_ref, bs = refs[0], refs[1 : 1 + len(counts)]
+    out_ref, turned, both, got, send, recv = refs[1 + len(counts) + kept :]
+    step = pl.program_id(0)
+    tiles = sum(counts)
+    core = lax.rem(lax.axis_index("fsdp"), 2)
+    twin = lax.axis_index("fsdp") + 1 - 2 * core
+    blocks, depth, tile = both.shape[1], both.shape[3], both.shape[4]
+    piece = min(512, turned.shape[0])
+    part = piece // (2 * depth)
+
+    def move(number):
+        slot = lax.rem(number, 2)
+        return remote(
+            both.at[slot, :, 1 - core], got.at[number], send.at[number], recv.at[number], "fsdp", twin
+        )
+
+    @pl.when(step == 0)
+    def _():
+        greet([("fsdp", twin)])
         turned[...] = a_ref[...].T
 
-    depth = out_ref.shape[1]
-    step = min(512, depth)
     begin = 0
     for b_ref, count in zip(bs, counts):
 
-        @pl.when((spot >= begin) & (spot < begin + count))
+        @pl.when((step >= begin) & (step < begin + count))
         def _(b_ref=b_ref):
-            for at in range(0, turned.shape[0], step):
-                inner = at % depth
-                out_ref[at // depth, inner : inner + step, :] = dot(
-                    turned[at : at + step, :], b_ref[...]
-                ).astype(BF)
+            slot = lax.rem(step, 2)
+
+            @pl.when(step >= 2)
+            def _():
+                move(step - 2).wait_send()
+
+            for i in range(turned.shape[0] // piece):
+                rows = dot(turned[i * piece : i * piece + piece, :], b_ref[...]).astype(BF)
+                both[slot, i * part : i * part + part] = rows.reshape(part, 2, depth, tile)
+            move(step).start()
 
         begin += count
 
-
-def qkv_back(dq_ref, dk_ref, dv_ref, w_ref, out_ref):
-    qw, kw = dq_ref.shape[1], dk_ref.shape[1]
-    out_ref[...] = (
-        dot_nt(dq_ref[...], w_ref[:, :qw])
-        + dot_nt(dk_ref[...], w_ref[:, qw : qw + kw])
-        + dot_nt(dv_ref[...], w_ref[:, qw + kw :])
-    ).astype(BF)
-
-
-def exchange(n, count, *refs):
-    ins, outs = refs[:count], refs[count : 2 * count]
-    send, recv, local = refs[2 * count :]
+    @pl.when(step >= 1)
+    def _():
+        last = step - 1
+        move(last).wait_recv()
+        lead = out_ref.shape[0]
+        inner = blocks // lead
+        for i in range(lead):
+            own = both[lax.rem(last, 2), i * inner : i * inner + inner, core]
+            other = got[last, i * inner : i * inner + inner]
+            total = (own.astype(F32) + other.astype(F32)).astype(BF)
+            out_ref[i] = total.reshape(inner * depth, tile)
+
+    @pl.when(step == tiles)
+    def _():
+        if tiles >= 2:
+            move(tiles - 2).wait_send()
+        move(tiles - 1).wait_send()
+
+
+def exchange_copies(n, ins, outs, send, recv, local):
     me = lax.axis_index("seq")
-    greet(others("seq", n))
-    copies, keeps = [], []
-    for i in range(count):
+    copies = []
+    for i, (source, out) in enumerate(zip(ins, outs)):
         for j in range(1, n):
             to = lax.rem(me + j, n)
             k = i * (n - 1) + j - 1
             copies.append(
-                remote(ins[i].at[to], outs[i].at[me], send.at[k], recv.at[k], "seq", to)
+                remote(source.at[to], out.at[me], send.at[k], recv.at[k], "seq", to)
             )
-        keeps.append(pltpu.make_async_copy(ins[i].at[me], outs[i].at[me], local.at[i]))
-    for copy in copies + keeps:
+        copies.append(pltpu.make_async_copy(source.at[me], out.at[me], local.at[i]))
+    for copy in copies:
         copy.start()
-    for copy in copies + keeps:
+    return copies
+
+
+def exchange(n, source, out, send, recv, local):
+    greet(others("seq", n))
+    for copy in exchange_copies(n, [source], [out], send, recv, local):
         copy.wait()
 
 
@@ -722,18 +867,29 @@
         out[...] = ins[i][0, :, begin : begin + count].astype(F32)
 
 
-def gains_back(n, nf, part, out, wide, mid, seen, send, recv, local):
+def exchange_gains(n, nf, gu, dn, one, two, gq, gk, gu_out, dn_out, out, part, wide, mid, seen, send, recv, local, gsend, grecv):
     me, spot = lax.axis_index("seq"), lax.axis_index("fsdp")
     greet(others("seq", n) + others("fsdp", nf))
-    copies = []
+    part[...] = jnp.zeros_like(part)
+    count = one.shape[0]
+    per = n * nf // count
+    for f in range(nf):
+        for seq in range(n):
+            row = (seq * nf + f) // per
+            part[f, seq, 0:1] = one[row : row + 1]
+            part[f, seq, 1:2] = two[row : row + 1]
+            part[f, seq, 2:3] = gq[0:1]
+            part[f, seq, 3:4] = gk[0:1]
+    far = []
     for j in range(1, nf):
         to = lax.rem(spot + j, nf)
-        copies.append(
-            remote(part.at[to], wide.at[j - 1], send.at[j - 1], recv.at[j - 1], "fsdp", to)
+        far.append(
+            remote(part.at[to], wide.at[j - 1], gsend.at[j - 1], grecv.at[j - 1], "fsdp", to)
         )
-    for copy in copies:
+    for copy in far:
         copy.start()
-    for copy in copies:
+    copies = exchange_copies(n, [gu, dn], [gu_out, dn_out], send, recv, local)
+    for copy in far:
         copy.wait_recv()
     total = part[spot]
     for j in range(nf - 1):
@@ -743,7 +899,7 @@
     for j in range(1, n):
         to = lax.rem(me + j, n)
         k = nf + j - 2
-        near.append(remote(mid.at[to], seen.at[j - 1], send.at[k], recv.at[k], "seq", to))
+        near.append(remote(mid.at[to], seen.at[j - 1], gsend.at[k], grecv.at[k], "seq", to))
     for copy in near:
         copy.start()
     for copy in near:
@@ -752,8 +908,10 @@
     for j in range(n - 1):
         result += seen[j]
     out[...] = result
-    for copy in copies + near:
+    for copy in far + near:
         copy.wait_send()
+    for copy in copies:
+        copy.wait()
 
 
 def after(value, done):
@@ -796,11 +954,26 @@
     own_gain = norm1_gain.shape[0]
     own_head = q_gain.shape[0]
 
-    packed = jnp.zeros((8, 128), F32)
-    packed = packed.at[0, :own_gain].set(norm1_gain.astype(F32))
-    packed = packed.at[1, :own_gain].set(norm2_gain.astype(F32))
-    packed = packed.at[2, :own_head].set(q_gain.astype(F32))
-    packed = packed.at[3, :own_head].set(k_gain.astype(F32))
+    spot = lax.axis_index("fsdp")
+    owner = lax.axis_index("seq") * nf + spot
+    lanes = jnp.arange(128, dtype=jnp.int32)[None, :]
+
+    def placed(gain, mine):
+        count = gain.shape[0]
+        wide = jnp.tile(gain.astype(F32), 128 // count)[None, :]
+        return jnp.where(lax.div(lanes, count) == mine, wide, 0.0)
+
+    sharing = 128 // own_gain
+    packed = jnp.concatenate(
+        [
+            placed(norm1_gain, lax.rem(spot, sharing)),
+            placed(norm2_gain, lax.rem(spot, sharing)),
+            placed(q_gain, owner),
+            placed(k_gain, owner),
+            jnp.zeros((4, 128), F32),
+        ],
+        axis=0,
+    )
     w_att = pl.pallas_call(
         functools.partial(attention_weights_out, n),
         out_shape=shape((n, depth, cw), BF),
@@ -825,53 +998,39 @@
         ],
         compiler_params=comm_params(8),
     )(after(w_gate, w_att), w_up, packed)
-    ordered = all_gains.transpose(1, 0, 2, 3)
-    gain_one = ordered[:, :, 0, :own_gain].reshape(1, width)
-    gain_two = ordered[:, :, 1, :own_gain].reshape(1, width)
-    gain_q = ordered[:, :, 2, :own_head].reshape(1, head)
-    gain_k = ordered[:, :, 3, :own_head].reshape(1, head)
-
-    wdt = w_down.T
     gather_sems = [dma(gather_copies(n)), dma(gather_copies(n)), pltpu.SemaphoreType.DMA]
     line = nf == 8
     w_att = lax.all_gather(w_att, "fsdp", axis=1, tiled=True).reshape(width, cw)
-    xg, dn, wo = pl.pallas_call(
-        functools.partial(entry_stage, n, nf, line),
+    half = head // 2
+    powers = -(np.arange(half, dtype=np.float32) * np.float32(2.0) / np.float32(head))
+    freq = np.tile((np.float32(theta) ** powers).astype(np.float32), 2)[None, :]
+    small = pl.BlockSpec(memory_space=pltpu.SMEM)
+    xg, dn, wo, gain_one, gain_two, gain_q, gain_k, cos, sin, low, high = pl.pallas_call(
+        functools.partial(entry_stage, n, nf, line, own_gain),
         out_shape=(
             shape((n, rows, width), BF),
             shape((n, depth, fw), BF),
             shape((nf if line else 1, depth, width), BF),
+            shape((1, width), F32),
+            shape((1, width), F32),
+            shape((1, head), F32),
+            shape((1, head), F32),
+            shape((group, head), F32),
+            shape((group, head), F32),
+            shape((8, group), jnp.int32),
+            shape((8, group), jnp.int32),
         ),
-        in_specs=[ANY] * 3,
-        out_specs=(ANY,) * 3,
+        in_specs=[ANY] * 3 + [VMEM] + [small] * 3 + [VMEM],
+        out_specs=(ANY,) * 3 + (VMEM,) * 8,
         scratch_shapes=gather_sems
         + [dma(n - 1), dma(n - 1), dma(1), dma(10), dma(10), pltpu.SemaphoreType.DMA],
         compiler_params=comm_params(1),
-    )(after(tokens, gu), wdt, w_out)
+    )(after(tokens, gu), w_down.T, w_out, all_gains, seq_lengths, pic_starts, pic_lengths, jnp.asarray(freq))
     wo = wo.reshape(-1, width)
     if not line:
         wo = lax.all_gather(wo, "fsdp", axis=0, tiled=True)
     gu = lax.all_gather(gu, "fsdp", axis=1, tiled=True).reshape(width, 2 * fw)
     dn = lax.all_gather(dn, "fsdp", axis=1, tiled=True).reshape(width, fw)
-
-    places = jnp.arange(group, dtype=jnp.int32)
-    lengths = seq_lengths[0]
-    border_one = lengths[0]
-    border_two = border_one + lengths[1]
-    begins = jnp.where(places >= border_two, border_two, jnp.where(places >= border_one, border_one, 0))
-    ends = jnp.where(places >= border_two, group, jnp.where(places >= border_one, border_two, border_one))
-    starts, sizes = pic_starts[0], pic_lengths[0]
-    inside = (places[:, None] >= starts[None, :]) & (places[:, None] < (starts + sizes)[None, :])
-    pic_end = jnp.max(jnp.where(inside, (starts + sizes)[None, :], 0), axis=1)
-    last = jnp.maximum(places, jnp.minimum(pic_end, ends) - 1)
-    low = jnp.broadcast_to(begins[None, :], (8, group))
-    high = jnp.broadcast_to(last[None, :], (8, group))
-    half = head // 2
-    frequency = F32(theta) ** (-(jnp.arange(half, dtype=F32) * 2.0 / head))
-    angles = (places - begins).astype(F32)[:, None] * frequency[None, :]
-    cosine, sine = jnp.cos(angles), jnp.sin(angles)
-    cos = jnp.concatenate([cosine, cosine], axis=1)
-    sin = jnp.concatenate([-sine, sine], axis=1)
 
     def whole(dims):
         return pl.BlockSpec(dims, lambda *ids: (0,) * len(dims))
@@ -983,12 +1142,13 @@
         compiler_params=plain_params(),
     )(n2, gu, gu)
 
-    def product(a, *bs, into=None, dims=None, spot=None):
+    def product(number, a, *bs, into=None, dims=None, spot=0):
         tile = 512
         while any(b.shape[1] % tile for b in bs):
             tile //= 2
         counts = [b.shape[1] // tile for b in bs]
         begins = [sum(counts[:i]) for i in range(len(bs))]
+        tiles = sum(counts)
 
         def spec(begin, count):
             return pl.BlockSpec(
@@ -996,34 +1156,44 @@
             )
 
         if dims is None:
-            dims = (1, a.shape[1], sum(counts) * tile)
-        lead = a.shape[1] // dims[1]
+            dims = (n, width // n // 2, tiles * tile)
+        lead = a.shape[1] // 2 // dims[1]
         across = dims[2] // tile
-        first = 0 if spot is None else spot
         kept = [] if into is None else [into]
+        blocks = a.shape[1] // (2 * depth)
+
+        def place(i):
+            last = jnp.maximum(i - 1, 0)
+            return (spot + lax.div(last, across), 0, lax.rem(last, across))
+
         return pl.pallas_call(
             functools.partial(gradient, counts, len(kept)),
-            grid=(sum(counts),),
+            grid=(tiles + 1,),
             out_shape=shape(dims, BF),
             in_specs=[whole(a.shape)]
             + [spec(b, c) for b, c in zip(begins, counts)]
             + [ANY] * len(kept),
-            out_specs=pl.BlockSpec(
-                (lead, dims[1], tile),
-                lambda i: (first + lax.div(i, across), 0, lax.rem(i, across)),
-            ),
-            scratch_shapes=[pltpu.VMEM((a.shape[1], group), BF)],
+            out_specs=pl.BlockSpec((lead, dims[1], tile), place),
+            scratch_shapes=[
+                pltpu.VMEM((a.shape[1], group), BF),
+                pltpu.VMEM((2, blocks, 2, depth, tile), BF),
+                pltpu.VMEM((tiles, blocks, depth, tile), BF),
+                dma(tiles),
+                dma(tiles),
+            ],
             input_output_aliases={} if into is None else {1 + len(bs): 0},
-            compiler_params=plain_params(),
+            compiler_params=comm_params(number),
         )(a, *bs, *kept)
 
-    def reduce_rows(grad, columns):
+    same_core = [[core + 2 * i for i in range(nf // 2)] for core in range(2)]
+
+    def reduce_rows(grad):
         return lax.psum_scatter(
-            grad.reshape(n, width // n, columns), "fsdp", scatter_dimension=1, tiled=True
+            grad, "fsdp", scatter_dimension=1, tiled=True, axis_index_groups=same_core
         )
 
-    dn_grad = product(cg, hidden)
-    dn_share = reduce_rows(dn_grad, fw)
+    dn_grad = product(12, cg, hidden)
+    dn_share = reduce_rows(dn_grad)
 
     dgate, dup = pl.pallas_call(
         ffn_back,
@@ -1039,7 +1209,7 @@
         compiler_params=plain_params(),
     )(cg, after(dn, dn_grad), gate, up)
 
-    gu_grad = product(n2, dgate, dup)
+    gu_grad = product(13, n2, dgate, dup)
     part_n2 = pl.pallas_call(
         two_nt,
         grid=(blocks,),
@@ -1053,33 +1223,35 @@
         out_specs=by_rows(256, width),
         compiler_params=plain_params(),
     )(after(dgate, gu_grad), dup, gu, gu)
-    part_y = pl.pallas_call(
-        one_nt,
-        grid=(blocks,),
-        out_shape=shape((group, width), BF),
-        in_specs=[by_rows(256, fw), whole((width, fw))],
-        out_specs=by_rows(256, width),
-        compiler_params=plain_params(),
-    )(after(hidden, part_n2), dn)
-    gu_share = reduce_rows(after(gu_grad, (dn_share, part_y)), 2 * fw)
-
-    dx2, dz, dgain_two = pl.pallas_call(
+    gu_share = reduce_rows(after(gu_grad, (dn_share, part_n2)))
+
+    dx2, dz, dgain_two, part_y = pl.pallas_call(
         functools.partial(back_stage, n),
         out_shape=(
             shape((rows, width), F32),
             shape((n, rows, width), BF),
-            shape((8, width), F32),
+            shape((width // 128, 128), F32),
+            shape((n, rows, width), BF),
         ),
-        in_specs=[VMEM] * 4,
-        out_specs=(VMEM, ANY, VMEM),
-        scratch_shapes=slots + [pltpu.VMEM((rows, width), BF)] + sems + gather_sems,
+        in_specs=[VMEM] * 4 + [ANY] * 2,
+        out_specs=(VMEM, ANY, VMEM, VMEM),
+        scratch_shapes=slots
+        + [pltpu.VMEM((rows, width), BF)]
+        + sems
+        + gather_sems
+        + [
+            pltpu.VMEM((1, width), F32),
+            pltpu.VMEM((group, fw), BF),
+            pltpu.VMEM((width, fw), BF),
+            dma(2),
+        ],
         compiler_params=comm_params(4),
     )(
-        after(part_n2, (part_y, dn_share)).reshape(n, rows, width), x2, cotangent, gain_two,
+        after(part_n2, dn_share).reshape(n, rows, width), x2, cotangent, gain_two, hidden, dn,
     )
     dz = dz.reshape(group, width)
 
-    wo_grad = product(attn, dz, dims=(n + width // cw, qw, cw), spot=n)
+    wo_grad = product(14, attn, dz, dims=(n + width // cw, qw // 2, cw), spot=n)
 
     wide = ratio * head
     dq, dk, dv, dgain_q, dgain_k, branch = pl.pallas_call(
@@ -1127,78 +1299,58 @@
         compiler_params=comm_params(5),
     )(
         q, qraw, k, kt, v, kraw, dz, wo, lse, low, high, cos, sin, cos, sin, gain_q, gain_k,
-        part_y.reshape(n, rows, width),
+        part_y,
     )
     output = (x2 + branch).astype(BF)
 
-    att_grad = product(n1, dq, dk, dv, into=wo_grad, dims=wo_grad.shape)
-    att_share = lax.psum_scatter(
-        after(att_grad, gu_share), "fsdp", scatter_dimension=1, tiled=True
-    )
-
-    part_n1 = pl.pallas_call(
-        qkv_back,
-        grid=(blocks,),
-        out_shape=shape((group, width), BF),
-        in_specs=[
-            by_rows(256, qw),
-            by_rows(256, kw),
-            by_rows(256, kw),
-            whole((width, cw)),
-        ],
-        out_specs=by_rows(256, width),
-        compiler_params=plain_params(),
-    )(after(dq, att_grad), dk, dv, w_att)
+    att_grad = product(15, n1, dq, dk, dv, into=wo_grad, dims=wo_grad.shape)
+    att_share = reduce_rows(after(att_grad, gu_share))
+
     back_one, dgain_one = pl.pallas_call(
         functools.partial(input_stage, n),
-        out_shape=(shape((rows, width), F32), shape((8, width), F32)),
-        in_specs=[VMEM] * 3,
+        out_shape=(shape((rows, width), F32), shape((width // 128, 128), F32)),
+        in_specs=[VMEM] * 6,
         out_specs=(VMEM, VMEM),
-        scratch_shapes=slots + sems,
+        scratch_shapes=[pltpu.VMEM((n, rows, width), BF)]
+        + slots
+        + sems
+        + [pltpu.VMEM((1, width), F32)],
         compiler_params=comm_params(10),
-    )(part_n1.reshape(n, rows, width), tokens, gain_one)
+    )(after(dq, att_grad), dk, dv, w_att, tokens, gain_one)
     input_grad = (dx2 + back_one).astype(BF)
 
-    def owned(row, count):
-        cut = row.reshape(n, nf, 1, count)
-        return jnp.pad(cut, ((0, 0), (0, 0), (0, 0), (0, 128 - count)))
-
-    blocks_of = jnp.concatenate(
-        [
-            owned(dgain_one[0], own_gain),
-            owned(dgain_two[0], own_gain),
-            owned(dgain_q[0], own_head),
-            owned(dgain_k[0], own_head),
-            jnp.zeros((n, nf, 4, 128), F32),
-        ],
-        axis=2,
-    ).transpose(1, 0, 2, 3)
-    gains = pl.pallas_call(
-        functools.partial(gains_back, n, nf),
-        out_shape=shape((8, 128), F32),
-        in_specs=[VMEM],
-        out_specs=VMEM,
+    gu_mine, dn_mine, gains = pl.pallas_call(
+        functools.partial(exchange_gains, n, nf),
+        out_shape=(
+            shape(gu_share.shape, BF),
+            shape(dn_share.shape, BF),
+            shape((8, 128), F32),
+        ),
+        in_specs=[ANY] * 2 + [VMEM] * 4,
+        out_specs=(ANY, ANY, VMEM),
         scratch_shapes=[
+            pltpu.VMEM((nf, n, 8, 128), F32),
             pltpu.VMEM((nf - 1, n, 8, 128), F32),
             pltpu.VMEM((n, 8, 128), F32),
             pltpu.VMEM((n - 1, 8, 128), F32),
+            dma(2 * (n - 1)),
+            dma(2 * (n - 1)),
+            dma(2),
             dma(n + nf - 2),
             dma(n + nf - 2),
-            pltpu.SemaphoreType.DMA,
         ],
         compiler_params=comm_params(7),
-    )(blocks_of)
-
-    def swap(number, *arrays):
-        count = len(arrays)
-        return pl.pallas_call(
-            functools.partial(exchange, n, count),
-            out_shape=tuple(shape((n,) + a.shape[1:], BF) for a in arrays),
-            in_specs=[ANY] * count,
-            out_specs=(ANY,) * count,
-            scratch_shapes=[dma(count * (n - 1)), dma(count * (n - 1)), dma(count)],
-            compiler_params=comm_params(number),
-        )(*arrays)
+    )(gu_share, dn_share, dgain_one, dgain_two, dgain_q, dgain_k)
+
+    def owned(row, count, mine):
+        return lax.dynamic_slice_in_dim(row, mine * count, count, 0)
+
+    gain_grads = (
+        owned(gains[0], own_gain, lax.rem(spot, sharing)),
+        owned(gains[1], own_gain, lax.rem(spot, sharing)),
+        owned(gains[2], own_head, owner),
+        owned(gains[3], own_head, owner),
+    )
 
     def spread(arrays, pieces):
         ins = [pl.BlockSpec((1, depth, a.shape[2]), lambda i: (i, 0, 0)) for a in arrays]
@@ -1213,13 +1365,19 @@
             compiler_params=plain_params(),
         )(*arrays)
 
-    gu_mine, dn_mine = swap(6, gu_share, after(dn_share, gains))
     gate_grad, up_grad, down_grad = spread(
         [gu_mine, dn_mine], [(0, 0, fw), (0, fw, fw), (1, 0, fw)]
     )
     wide_grads = (gate_grad, up_grad, down_grad.T)
     wo_out = att_share[n:].transpose(1, 0, 2).reshape(depth, width).astype(F32)
-    (att_mine,) = swap(9, after(att_share, (gains, wide_grads, input_grad, output)))
+    att_mine = pl.pallas_call(
+        functools.partial(exchange, n),
+        out_shape=shape((n, depth, cw), BF),
+        in_specs=[ANY],
+        out_specs=ANY,
+        scratch_shapes=[dma(n - 1), dma(n - 1), dma(1)],
+        compiler_params=comm_params(9),
+    )(after(att_share, (gain_grads, wide_grads, input_grad, output)))
     wq_grad, wk_grad, wv_grad = spread(
         [att_mine], [(0, 0, qw), (0, qw, kw), (0, qw + kw, kw)]
     )
@@ -1227,14 +1385,14 @@
     return (
         output,
         input_grad,
-        gains[0, :own_gain],
+        gain_grads[0],
         wq_grad,
         wk_grad,
         wv_grad,
-        gains[2, :own_head],
-        gains[3, :own_head],
+        gain_grads[2],
+        gain_grads[3],
         wo_out,
-        gains[1, :own_gain],
+        gain_grads[1],
     ) + wide_grads
 
 

time: 599 us -> 575 us (0.960)
  Pallas kernels: 555 us -> 537 us
  waiting for transfers between devices: 1.08 us -> 9.64 us
  other arithmetic: 12.3 us -> 5.22 us
    pallas_call x10 -> x7, Pallas kernels: 189 us -> 155 us  [the longest x4 59.7 us: product(): pl.pallas_call(functools.partial(gradient, counts, len(kept)), grid=(tile...]
    all_gather x1, waiting for transfers between devices: 0.02 us -> 7.57 us  [shards(): dn = lax.all_gather(dn, 'fsdp', axis=1, tiled=True).reshape(width, fw)]
  transfers between devices with their start and end apart: 6 -> 6, of which waited for: 2 -> 2; matrix products, arithmetic and copies ran while one was open for 4% -> 2% of each run, Pallas kernels for 89% -> 89%
where the time goes in v3:
time: 575 us; the launch traced here: 574 us
  Pallas kernels  537 us (93%)
  between operations  14.4 us (3%)
  waiting for transfers between devices  9.64 us (2%)
  local copies, waits for them, and re-layouts  7.61 us (1%)
    pallas_call x1, Pallas kernels, shards(): pl.pallas_call(functools.partial(back_stage, n), out_shape=(shape((rows,...  78.9 us
    pallas_call x1, Pallas kernels, shards(): pl.pallas_call(functools.partial(middle_stage, n), out_shape=(shape((rows...  73 us
    pallas_call x4, Pallas kernels, product(): pl.pallas_call(functools.partial(gradient, counts, len(kept)), grid=(tile...  59.7 us
    pallas_call x1, Pallas kernels, shards(): pl.pallas_call(functools.partial(entry_stage, n, nf, line, own_gain), out...  52.9 us
    pallas_call x1, Pallas kernels, shards(): pl.pallas_call(functools.partial(input_stage, n), out_shape=(shape((rows,...  45 us
    pallas_call x1, Pallas kernels, shards(): pl.pallas_call(functools.partial(attend_back, n), grid=(kheads, blocks),...  42.8 us
    pallas_call x1, Pallas kernels, shards(): pl.pallas_call(functools.partial(exchange_gains, n, nf), out_shape=(shape...  32.8 us
    pallas_call x1, Pallas kernels, shards(): pl.pallas_call(functools.partial(gate_up_out, n, nf), out_shape=(shape((n...  23.8 us
  transfers between devices with their start and end apart: 6, of which 2 were waited for; matrix products, arithmetic and copies ran while one was open for 2% of the time, Pallas kernels for 89%

profile of v3, /device:TPU:0, one launch (start us, length us, event | category | flops | bytes accessed | tf_op | source)
XLA Modules:
  0.0 574.2 jit_solution(17970708797561471359)
XLA Ops:
  7.2 0.0 all-gather.4.cloned.1.call-start
  7.2 11.1 %shard_map.264 = bf16[4,64,1024]{2,1,0:T(8,128)(2,1)} custom-call(bf16[64,2048]{1,0:T(8,128)(2,1)} %wq.1, bf16[64,1024]{1,0:T(8,128)(2,1)} %wk.1, bf16[64,1024]{1,0:T(8,128)(2,1)} %wv.1), custom_call_target="tpu_custom_call" | custom-call | tf_op jit(solution)/shard_map/pallas_call | solution.py:977
  18.3 0.0 all-gather.8.cloned.1.call-start
  18.4 0.7 tile.8
  19.1 0.1 broadcast_in_dim_tile.12
  19.1 0.7 tile.9
  19.8 0.1 broadcast_in_dim_tile.13
  19.9 0.7 tile.10
  20.5 0.1 broadcast_in_dim_tile.14
  20.6 0.7 tile.11
  21.3 0.1 broadcast_in_dim_tile.15
  21.5 0.6 concatenate.3.gains
  22.1 23.8 %shard_map.265 = (bf16[4,64,3072]{2,1,0:T(8,128)(2,1)}, f32[8,4,8,128]{3,2,1,0:T(8,128)}) custom-call(bf16[64,6144]{1,0:T(8,128)(2,1)} %wg, bf16[64,6144]{1,0:T(8,128)(2,1)} %wu.1, f32[8,128]{1,0:T(8,128)} %concatenate.3.gains), custom_call_target="tpu_custom_call" | custom-call | tf_op jit(solution)/shard_map/pallas_call | solution.py:985
  45.9 0.0 all-gather.6.cloned.1.call-start
  45.9 52.9 %shard_map.266 = (bf16[4,256,2048]{2,1,0:T(8,128)(2,1)}, bf16[4,64,1536]{2,1,0:T(8,128)(2,1)}, bf16[8,64,2048]{2,1,0:T(8,128)(2,1)}, f32[1,2048]{1,0:T(1,128)}, ...) custom-call(bf16[256,2048]{1,0:T(8,128)(2,1)} %x.4, ...), custom_call_target="tpu_custom_call" | custom-call | tf_op jit(solution)/shard_map/pallas_call | solution.py:1008
  98.9 0.0 reduce-scatter.4.cloned.1.call-start
  98.9 23.5 %shard_map.267 = (bf16[1024,2048]{1,0:T(8,128)(2,1)}, f32[1024,512]{1,0:T(8,128)}, f32[1024,256]{1,0:T(8,128)}, bf16[1024,512]{1,0:T(8,128)(2,1)}, bf16[1024,256...) custom-call(bf16[1024,2048]{1,0:T(8,128)(2,1)} %bitcast.42, ...), custom_call_target="tpu_custom_call" | custom-call | tf_op jit(solution)/shard_map/pallas_call | solution.py:1045
  122.4 21.7 %shard_map.268 = (bf16[1024,512]{1,0:T(8,128)(2,1)}, f32[8,1024]{1,0:T(8,128)}, bf16[1024,2048]{1,0:T(8,128)(2,1)}, bf16[4,256,2048]{2,1,0:T(8,128)(2,1)}) custom-call(bf16[1024,512]{1,0:T(8,128)(2,1)} %get-tuple-element.86.q_ref, bf16[1024,256]{1,0:T(8,128)(2,1)} %get-tuple-element.87.k_ref, ...), custom_call_target="tpu_custom_call", output_to_operand_aliasing={{3}: (7, {})} | custom-call | tf_op jit(solution)/shard_map/pallas_call | solution.py:1084
  144.1 73.0 %shard_map.269 = (f32[256,2048]{1,0:T(8,128)}, bf16[4,256,2048]{2,1,0:T(8,128)(2,1)}) custom-call(bf16[4,256,2048]{2,1,0:T(8,128)(2,1)} %bitcast.41, bf16[256,2048]{1,0:T(8,128)(2,1)} %x.4, f32[1,2048]{1,0:T(1,128)} %get-tuple-element.94.gain), custom_call_target="tpu_custom_call" | custom-call | tf_op jit(solution)/shard_map/pallas_call | solution.py:1116
  217.1 0.0 all-gather.8.cloned.1.call-done
  217.2 19.3 %shard_map.270 = (f32[1024,1536]{1,0:T(8,128)}, f32[1024,1536]{1,0:T(8,128)}, bf16[1024,1536]{1,0:T(8,128)(2,1)}) custom-call(bf16[1024,2048]{1,0:T(8,128)(2,1)} %bitcast.34, bf16[2048,3072]{1,0:T(8,128)(2,1)} %bitcast.24, bf16[2048,3072]{1,0:T(8,128)(2,1)} %bitcast.25), custom_call_target="tpu_custom_call" | custom-call | tf_op jit(solution)/shard_map/pallas_call | solution.py:1128
  236.5 15.3 %shard_map.271 = bf16[4,256,1536]{2,1,0:T(8,128)(2,1)} custom-call(bf16[1024,2048]{1,0:T(8,128)(2,1)} %bitcast.28, bf16[1024,1536]{1,0:T(8,128)(2,1)} %get-tuple-element.103.refs_1_.hidden_far), custom_call_target="tpu_custom_call" | custom-call | tf_op jit(solution)/shard_map/pallas_call | solution.py:1169
  251.8 0.2 reduce-scatter.6.cloned.1.call-start
  252.0 7.6 %all-gather.6.cloned.1.call-done = bf16[4,512,1536]{2,1,0:T(8,128)(2,1)} async-done(((bf16[4,64,1536]{2,1,0:T(8,128)(2,1)}), bf16[4,512,1536]{2,1,0:T(8,128)(2,1)}) %all-gather.6.cloned.1.call-update) | async-done | bytes 6291472 | tf_op jit(solution)/shard_map/all_gather | solution.py:1033
  259.6 15.6 %shard_map.272 = (bf16[1024,1536]{1,0:T(8,128)(2,1)}, bf16[1024,1536]{1,0:T(8,128)(2,1)}) custom-call(bf16[1024,2048]{1,0:T(8,128)(2,1)} %bitcast.29, bf16[2048,1536]{1,0:T(8,128)(2,1)} %bitcast.30, f32[1024,1536]{1,0:T(8,128)} %get-tuple-element.105.gate_ref, f32[1024,1536]{1,0:T(8,128)} %get-tuple-element.106.up_ref), custom_call_target="tpu_custom_call" | custom-call | tf_op jit(solution)/shard_map/pallas_call | solution.py:1198
  275.2 23.6 %shard_map.273 = bf16[4,256,3072]{2,1,0:T(8,128)(2,1)} custom-call(bf16[1024,2048]{1,0:T(8,128)(2,1)} %bitcast.35, bf16[1024,1536]{1,0:T(8,128)(2,1)} %get-tuple-element.109.refs_1_.a_ref, bf16[1024,1536]{1,0:T(8,128)(2,1)} %get-tuple-element.108.refs_2_.b_ref), custom_call_target="tpu_custom_call" | custom-call | tf_op jit(solution)/shard_map/pallas_call | solution.py:1169
  298.8 20.0 %shard_map.274 = bf16[1024,2048]{1,0:T(8,128)(2,1)} custom-call(bf16[1024,1536]{1,0:T(8,128)(2,1)} %get-tuple-element.109.refs_1_.a_ref, bf16[1024,1536]{1,0:T(8,128)(2,1)} %get-tuple-element.108.refs_2_.b_ref, bf16[2048,3072]{1,0:T(8,128)(2,1)} %bitcast.26, bf16[2048,3072]{1,0:T(8,128)(2,1)} %bitcast.27), custom_call_target="tpu_custom_call" | custom-call | tf_op jit(solution)/shard_map/pallas_call | solution.py:1213
  318.8 1.9 reduce-scatter.4.cloned.1.call-done.dn
  320.7 0.3 reduce-scatter.8.cloned.1.call-start
  321.0 78.9 %shard_map.275 = (f32[256,2048]{1,0:T(8,128)}, bf16[4,256,2048]{2,1,0:T(8,128)(2,1)}, f32[16,128]{1,0:T(8,128)}, bf16[4,256,2048]{2,1,0:T(8,128)(2,1)}) custom-call(bf16[4,256,2048]{2,1,0:T(8,128)(2,1)} %bitcast.36, f32[256,2048]{1,0:T(8,128)} %get-tuple-element.95.x2, bf16[256,2048]{1,0:T(8,128)(2,1)} %cot.5, f32[1,2048]{1,0:T(1,128)} %get-tuple-element.94.gain, ...), custom_call_target="tpu_custom_call" | custom-call | tf_op jit(solution)/shard_map/pallas_call | solution.py:1228
  399.9 8.2 %shard_map.277.refs_4_ = bf16[6,256,1024]{2,1,0:T(8,128)(2,1)} custom-call(bf16[1024,512]{1,0:T(8,128)(2,1)} %get-tuple-element.120.refs_0_, bf16[1024,2048]{1,0:T(8,128)(2,1)} %bitcast.37), custom_call_target="tpu_custom_call" | custom-call | tf_op jit(solution)/shard_map/pallas_call | solution.py:1169
  408.2 42.8 %shard_map.276 = (bf16[1024,512]{1,0:T(8,128)(2,1)}, bf16[1024,256]{1,0:T(8,128)(2,1)}, bf16[1024,256]{1,0:T(8,128)(2,1)}, f32[8,128]{1,0:T(8,128)}, f32[8,128]{1,0:T(8,128)}, /*index=5*/f32[256,2048]{1,0:T(8,128)}) custom-call(bf16[1024,512]{1,0:T(8,128)(2,1)} %get-tuple-element.86.q_ref, f32[1024,512]{1,0:T(8,128)} %get-tuple-element.96.qraw_ref, ...), custom_call_target="tpu_custom_call" | custom-call | tf_op jit(solution)/shard_map/pallas_call | solution.py:1257
  451.0 12.5 %shard_map.278 = bf16[6,256,1024]{2,1,0:T(8,128)(2,1)} custom-call(bf16[1024,2048]{1,0:T(8,128)(2,1)} %get-tuple-element.117.refs_0_, bf16[1024,512]{1,0:T(8,128)(2,1)} %get-tuple-element.121.refs_1_.dq, bf16[1024,256]{1,0:T(8,128)(2,1)} %get-tuple-element.118.refs_2_.dk, ...), custom_call_target="tpu_custom_call", output_to_operand_aliasing={{}: (4, {})} | custom-call | tf_op jit(solution)/shard_map/pallas_call | solution.py:1169
  463.5 0.0 reduce-scatter.6.cloned.1.call-done.gu
  463.6 45.0 %shard_map.279 = (f32[256,2048]{1,0:T(8,128)}, f32[16,128]{1,0:T(8,128)}) custom-call(bf16[1024,512]{1,0:T(8,128)(2,1)} %get-tuple-element.121.refs_1_.dq, bf16[1024,256]{1,0:T(8,128)(2,1)} %get-tuple-element.118.refs_2_.dk, bf16[1024,256]{1,0:T(8,128)(2,1)} %get-tuple-element.119.refs_3_.dv, bf16[2048,1024]{1,0:T(8,128)(2,1)} %bitcast.33, ...), custom_call_target="tpu_custom_call" | custom-call | tf_op jit(solution)/shard_map/pallas_call | solution.py:1309
  508.6 3.0 add_convert_fusion.1
  511.6 1.2 add_convert_fusion
  512.9 32.8 %shard_map.280 = (bf16[4,64,3072]{2,1,0:T(8,128)(2,1)}, bf16[4,64,1536]{2,1,0:T(8,128)(2,1)}, f32[8,128]{1,0:T(8,128)}) custom-call(bf16[4,64,3072]{2,1,0:T(8,128)(2,1)} %reduce-scatter.6.cloned.1.call-done.gu, bf16[4,64,1536]{2,1,0:T(8,128)(2,1)} %reduce-scatter.4.cloned.1.call-done.dn, f32[16,128]{1,0:T(8,128)} %get-tuple-element.124.one, ...), custom_call_target="tpu_custom_call" | custom-call | tf_op jit(solution)/shard_map/pallas_call | solution.py:1322
  545.7 4.3 shard_map.281
  550.0 0.8 fusion.4
  550.8 0.6 fusion.3
  551.4 0.6 fusion.2
  551.9 0.6 fusion.1
  552.5 0.6 fusion
  553.1 1.0 convert_bitcast_fusion
  554.1 0.8 copy.33
  554.9 9.2 %shard_map.282.refs_0_ = bf16[4,64,1024]{2,1,0:T(8,128)(2,1)} custom-call(bf16[6,64,1024]{2,1,0:T(8,128)(2,1)} %reduce-scatter.8.cloned.1.call-done.source), custom_call_target="tpu_custom_call" | custom-call | tf_op jit(solution)/shard_map/pallas_call | solution.py:1373
  564.1 3.2 shard_map.283
  (17 shorter events, 0.2 us)
Async XLA Ops:
  7.2 91.8 %all-gather.4.cloned.1.call-start = ((), (), s32[]{:S(2)}) async-start(), calls=%async_computation.3 | async-start | bytes 4718592 | tf_op jit(solution)/shard_map/all_gather | solution.py:1003
  18.3 198.8 %all-gather.8.cloned.1.call-start = ((), (), s32[]{:S(2)}) async-start(), calls=%async_computation.5 | async-start | bytes 14155776 | tf_op jit(solution)/shard_map/all_gather | solution.py:1032
  45.9 213.7 %all-gather.6.cloned.1.call-start = ((), (), s32[]{:S(2)}) async-start(), calls=%async_computation.4 | async-start | bytes 7077888 | tf_op jit(solution)/shard_map/all_gather | solution.py:1033
  98.9 221.9 %reduce-scatter.4.cloned.1.call-start = ((), (), s32[]{:S(2)}) async-start(), calls=%async_computation.6 | async-start | bytes 3932160 | tf_op jit(solution)/shard_map/reduce_scatter | solution.py:1191
  251.8 211.8 %reduce-scatter.6.cloned.1.call-start = ((), (), s32[]{:S(2)}) async-start(), calls=%async_computation.7 | async-start | bytes 7864320 | tf_op jit(solution)/shard_map/reduce_scatter | solution.py:1191
  320.7 232.4 %reduce-scatter.8.cloned.1.call-start = ((), (), s32[]{:S(2)}) async-start(), calls=%async_computation.8 | async-start | bytes 3932160 | tf_op jit(solution)/shard_map/reduce_scatter | solution.py:1191
  463.6 45.1 %copy-start = (f32[256,2048]{1,0:T(8,128)S(1)}, f32[256,2048]{1,0:T(8,128)}, u32[]{:S(2)}) copy-start(f32[256,2048]{1,0:T(8,128)} %get-tuple-element.95.x2) | copy-start | bytes 6291460
  508.6 3.0 copy-start.1
  508.6 3.0 copy-start.2
Sparse Core Ops, SparseCore 0:
  18.5 58.1 all-gather.3
  78.2 116.7 all-gather.7
  196.6 62.8 all-gather.5
  261.7 58.9 reduce-scatter.3
  322.9 110.7 reduce-scatter.5
  463.7 61.9 reduce-scatter.7

commit v4 on v3

--- a/solution.py
+++ b/solution.py
@@ -108,13 +108,15 @@
         for i, (src, dst, to) in enumerate(moves)
     ]
 
-    def start():
-        for copy in copies[:4]:
-            copy.start()
-        if n != 4:
-            for copy in copies[4:]:
-                copy.start()
-        keep.start()
+    def start(part=None):
+        chosen = range(len(copies))
+        if n == 4:
+            chosen = {None: (0, 1, 2, 3), 0: (0, 3), 1: (1, 2)}[part]
+        if n == 4 or part != 0:
+            for i in chosen:
+                copies[i].start()
+        if part != 0:
+            keep.start()
 
     def relay():
         if n == 4:
@@ -143,10 +145,11 @@
 
 
 def scatter_sum(n, part, slots, stage, send, recv, finish):
-    start, relay, total = scatter_parts(n, part, slots, stage, send, recv, finish)
+    start, relay, lower, upper = scatter_parts(n, part, slots, stage, send, recv, finish)
     start()
     relay()
-    total()
+    lower()
+    upper()
 
 
 def scatter_parts(n, part, slots, stage, send, recv, finish):
@@ -189,24 +192,30 @@
             stage[high] = (part[along, high].astype(F32) + slots[2, high].astype(F32)).astype(BF)
             copies[5].start()
 
-    def total():
-        for copy in copies[2:] if n == 4 else copies:
+    step = 32
+
+    def chunk(number, carry):
+        at = pl.ds(pl.multiple_of(number * step, step), step)
+        value = part[me, at].astype(F32)
+        for slot in range(count):
+            value += slots[slot, at].astype(F32)
+        finish(at, value)
+        return carry
+
+    def lower():
+        for copy in copies[3:5] if n == 4 else copies:
             copy.wait_recv()
-        step = 32
-
-        def chunk(number, carry):
-            at = pl.ds(pl.multiple_of(number * step, step), step)
-            value = part[me, at].astype(F32)
-            for slot in range(count):
-                value += slots[slot, at].astype(F32)
-            finish(at, value)
-            return carry
-
-        lax.fori_loop(0, rows // step, chunk, 0)
+        lax.fori_loop(0, half // step, chunk, 0)
+
+    def upper():
+        if n == 4:
+            copies[2].wait_recv()
+            copies[5].wait_recv()
+        lax.fori_loop(half // step, rows // step, chunk, 0)
         for copy in copies:
             copy.wait_send()
 
-    return start, relay, total
+    return start, relay, lower, upper
 
 
 def inverse_rms(values):
@@ -528,7 +537,7 @@
     finish_half = half_gather(n, 0, cot, cg, send, recv, local)
     x = x_ref[...].astype(F32)
     normed = (x * inverse_rms(x) * gain_ref[...]).astype(BF)
-    n1_ref[...] = normed
+    n1_ref[...] = normed.T
     full = dot(normed, w_ref[...])
     qw, kw = q_ref.shape[1], k_ref.shape[1]
     cos, sin = cos_ref[...], sin_ref[...]
@@ -596,11 +605,26 @@
         x2[at] = value
         own[at] = (value * inverse_rms(value) * gain[...]).astype(BF)
 
-    scatter_sum(n, part, slots, stage, send, recv, finish)
-    gather(n, own, n2, asend, arecv, local)
-
-
-def ffn_forward(n2_ref, wg_ref, wu_ref, gate_ref, up_ref, hidden_ref):
+    start, relay, lower, upper = scatter_parts(n, part, slots, stage, send, recv, finish)
+    send_on, pass_on, end = gather_parts(n, own, n2, asend, arecv, local)
+    start()
+    relay()
+    lower()
+    send_on(0)
+    upper()
+    send_on(1)
+    pass_on()
+    end()
+
+
+def ffn_forward(cuts, n2_ref, wg_ref, wu_ref, gate_ref, up_ref, hidden_ref, turned_ref):
+    count = n2_ref.shape[1] // cuts
+    step = pl.program_id(0)
+
+    @pl.when(step < cuts)
+    def _():
+        turned_ref[...] = n2_ref[:, pl.ds(pl.multiple_of(step * count, 128), count)].T
+
     gate = dot(n2_ref[...], wg_ref[...])
     up = dot(n2_ref[...], wu_ref[...])
     gate_ref[...] = gate
@@ -616,17 +640,40 @@
     dup_ref[...] = (dh * (gate * s)).astype(BF)
 
 
-def two_nt(a_ref, b_ref, wa_ref, wb_ref, out_ref):
-    out_ref[...] = (dot_nt(a_ref[...], wa_ref[...]) + dot_nt(b_ref[...], wb_ref[...])).astype(BF)
-
-
 def spread_rows(row, out):
     for i in range(out.shape[0]):
         out[i : i + 1, :] = row[:, i * 128 : i * 128 + 128]
 
 
-def back_stage(n, part, x2, cot, gain, hidden_far, dn_far, dx2, dz, dgain, part_y, slots, stage, own, send, recv, asend, arecv, local, row, hidden, dn, load):
+def back_stage(n, dgate_far, dup_far, gu_far, x2, cot, gain, hidden_far, dn_far, dx2, dz, dgain, part_y, part, slots, stage, own, send, recv, asend, arecv, local, row, hidden, dn, load, dgate, dup, gu, rload, wload):
     greet(ring_places(n))
+    me = lax.axis_index("seq")
+    rows, width = x2.shape
+    units = dup.shape[1]
+    step = 512
+
+    def row_loads(to):
+        at = pl.ds(pl.multiple_of(to * rows, rows), rows)
+        return [
+            pltpu.make_async_copy(dgate_far.at[at], dgate.at[at], rload.at[0, to]),
+            pltpu.make_async_copy(dup_far.at[at], dup.at[at], rload.at[1, to]),
+        ]
+
+    def weight_load(number):
+        at = pl.ds(pl.multiple_of(number * step, step), step)
+        return pltpu.make_async_copy(gu_far.at[at], gu.at[at], wload.at[number])
+
+    order = [lax.rem(me + j, n) for j in range(1, n)] + [me]
+    if n == 4:
+        across, along, corner = square(me)
+        order = [corner, across, along, me]
+    for copy in row_loads(order[0]):
+        copy.start()
+    for number in range(width // step):
+        weight_load(number).start()
+    for to in order[1:]:
+        for copy in row_loads(to):
+            copy.start()
     loads = [
         pltpu.make_async_copy(hidden_far, hidden, load.at[0]),
         pltpu.make_async_copy(dn_far, dn, load.at[1]),
@@ -634,8 +681,22 @@
     for copy in loads:
         copy.start()
     row[...] = jnp.zeros_like(row)
-    rows, width = x2.shape
-    step = 512
+
+    def block(to, first=False):
+        at = pl.ds(pl.multiple_of(to * rows, rows), rows)
+        for copy in row_loads(to):
+            copy.wait()
+
+        def columns(number, carry):
+            if first:
+                weight_load(number).wait()
+            span = pl.ds(pl.multiple_of(number * step, step), step)
+            value = dot_nt(dgate[at, :], gu[span, pl.ds(0, units)])
+            value += dot_nt(dup[at, :], gu[span, pl.ds(units, units)])
+            part[to, :, span] = value.astype(BF)
+            return carry
+
+        lax.fori_loop(0, width // step, columns, 0)
 
     def forward(to, carry):
         at = pl.ds(pl.multiple_of(to * rows, rows), rows)
@@ -654,67 +715,36 @@
         own[at] = value.astype(BF)
         row[...] += dg
 
-    start, relay, total = scatter_parts(n, part, slots, stage, send, recv, finish)
-    start()
-    for copy in loads:
-        copy.wait()
-    relay()
-    lax.fori_loop(0, n // 2, forward, 0)
-    total()
-    start, relay, end = gather_parts(n, own, dz, asend, arecv, local)
-    start()
-    spread_rows(row[...], dgain)
-    relay()
-    lax.fori_loop(n // 2, n, forward, 0)
-    end()
-
-
-def input_stage(n, dq, dk, dv, w, x, gain, out, dgain, part, slots, stage, send, recv, row):
-    greet(ring_places(n))
-    row[...] = jnp.zeros_like(row)
-    me = lax.axis_index("seq")
-    rows, width = x.shape
-    qw, kw = dq.shape[1], dk.shape[1]
-    step = 512
-
-    def block(to):
-        at = pl.ds(pl.multiple_of(to * rows, rows), rows)
-
-        def columns(number, carry):
-            span = pl.ds(pl.multiple_of(number * step, step), step)
-            value = dot_nt(dq[at, :], w[span, pl.ds(0, qw)])
-            value += dot_nt(dk[at, :], w[span, pl.ds(qw, kw)])
-            value += dot_nt(dv[at, :], w[span, pl.ds(qw + kw, kw)])
-            part[to, :, span] = value.astype(BF)
-            return carry
-
-        lax.fori_loop(0, width // step, columns, 0)
-
-    def finish(at, total):
-        back, dg = norm_back(x[at].astype(F32), gain[...], total)
-        out[at] = back
-        row[...] += dg
-
-    start, relay, total = scatter_parts(n, part, slots, stage, send, recv, finish)
+    start, relay, lower, upper = scatter_parts(n, part, slots, stage, send, recv, finish)
+    send_on, pass_on, end = gather_parts(n, own, dz, asend, arecv, local)
     if n == 4:
-        across, along, corner = square(me)
-        block(corner)
+        block(corner, True)
         start(0, 2)
         block(across)
         start(2, 3)
         block(along)
         start(3, 4)
+        relay()
         block(me)
     else:
-        for j in range(n):
-            block(lax.rem(me + j, n))
+        block(order[0], True)
+        for to in order[1:]:
+            block(to)
         start()
-    relay()
-    total()
+    for copy in loads:
+        copy.wait()
+    lax.fori_loop(0, n // 4, forward, 0)
+    lower()
+    send_on(0)
+    upper()
+    send_on(1)
     spread_rows(row[...], dgain)
-
-
-def attend_back(n, q_ref, qraw_ref, k_ref, kt_ref, v_ref, kraw_ref, dz_ref, wo_ref, lse_ref, low_ref, high_ref, cq_ref, sq_ref, ck_ref, sk_ref, gq_ref, gk_ref, part, dq_ref, dk_ref, dv_ref, dgq_ref, dgk_ref, out, dk_sum, dv_sum, slots, stage, send, recv):
+    pass_on()
+    lax.fori_loop(n // 4, n, forward, 0)
+    end()
+
+
+def attend_back(n, q_ref, qraw_ref, k_ref, kt_ref, v_ref, kraw_ref, dz_ref, wo_ref, lse_ref, low_ref, high_ref, cq_ref, sq_ref, ck_ref, sk_ref, gq_ref, gk_ref, attn_ref, part, dq_ref, dk_ref, dv_ref, dgq_ref, dgk_ref, out, grads, dk_sum, dv_sum, slots, stage, send, recv, wo_sum, both, got, done, tsend, trecv, put):
     kv, block = pl.program_id(0), pl.program_id(1)
     keys = k_ref.shape[0]
     ratio = q_ref.shape[1] // 128
@@ -723,13 +753,22 @@
     def finish(at, total):
         out[at] = total
 
-    start, relay, total = scatter_parts(n, part, slots, stage, send, recv, finish)
+    start, relay, lower, upper = scatter_parts(n, part, slots, stage, send, recv, finish)
+    core = lax.rem(lax.axis_index("fsdp"), 2)
+    twin = lax.axis_index("fsdp") + 1 - 2 * core
+    kheads, pieces, depth = both.shape[0], both.shape[1], both.shape[3]
+
+    def move(number):
+        return remote(
+            both.at[number, :, 1 - core], got.at[number], tsend.at[number], trecv.at[number], "fsdp", twin
+        )
+
     steps = pl.num_programs(0) * pl.num_programs(1)
     step = kv * pl.num_programs(1) + block
 
     @pl.when(step == 0)
     def _():
-        greet(ring_places(n))
+        greet(ring_places(n) + [("fsdp", twin)])
         start()
         dgq_ref[...] = jnp.zeros_like(dgq_ref)
         dgk_ref[...] = jnp.zeros_like(dgk_ref)
@@ -742,6 +781,7 @@
     def _():
         dk_sum[...] = jnp.zeros_like(dk_sum)
         dv_sum[...] = jnp.zeros_like(dv_sum)
+        wo_sum[...] = jnp.zeros_like(wo_sum)
 
     bias = bias_of(low_ref, high_ref, keys)
     dattn = dot_nt(dz_ref[...], wo_ref[...]).astype(BF)
@@ -766,8 +806,12 @@
         dq_ref[:, span] = back.astype(BF)
         dgq_ref[0:1] += dg
 
+    wo_sum[...] += dot_tn(attn_ref[...], dz_ref[...])
+
     @pl.when(block == pl.num_programs(1) - 1)
     def _():
+        both[kv] = wo_sum[...].astype(BF).reshape(both.shape[1:])
+        move(kv).start()
         dv_ref[...] = dv_sum[...].astype(BF)
         back, dg = prep_back(
             dk_sum[...] * scale, kraw_ref[...], gk_ref[...], ck_ref[...], sk_ref[...]
@@ -777,18 +821,47 @@
 
     @pl.when(step == steps - 1)
     def _():
-        total()
-
-
-def gradient(counts, kept, *refs):
+        cw = grads.shape[2]
+        writes = []
+        for number in range(kheads):
+            move(number).wait_recv()
+            value = both[number, :, core].astype(F32) + got[number].astype(F32)
+            done[number] = value.astype(BF).reshape(done.shape[1:])
+            for i in range(done.shape[2] // cw):
+                rows = pl.ds(number * pieces * depth, pieces * depth)
+                writes.append(
+                    pltpu.make_async_copy(
+                        done.at[number, :, pl.ds(i * cw, cw)],
+                        grads.at[n + i, rows],
+                        put.at[number, i],
+                    )
+                )
+        for copy in writes:
+            copy.start()
+        lower()
+        upper()
+        for copy in writes:
+            copy.wait()
+        for number in range(kheads):
+            move(number).wait_send()
+
+
+def gradient(n, counts, kept, flipped, beside, *refs):
     a_ref, bs = refs[0], refs[1 : 1 + len(counts)]
-    out_ref, turned, both, got, send, recv = refs[1 + len(counts) + kept :]
+    refs = refs[1 + len(counts) + kept :]
+    if beside:
+        given, out_ref, taken, both, got, send, recv, esend, erecv, local = refs[:10]
+        refs = refs[10:]
+    else:
+        out_ref, both, got, send, recv = refs[:5]
+        refs = refs[5:]
+    turned = a_ref if flipped else refs[0]
     step = pl.program_id(0)
     tiles = sum(counts)
     core = lax.rem(lax.axis_index("fsdp"), 2)
     twin = lax.axis_index("fsdp") + 1 - 2 * core
     blocks, depth, tile = both.shape[1], both.shape[3], both.shape[4]
-    piece = min(512, turned.shape[0])
+    piece = min(1024, turned.shape[0])
     part = piece // (2 * depth)
 
     def move(number):
@@ -799,8 +872,12 @@
 
     @pl.when(step == 0)
     def _():
-        greet([("fsdp", twin)])
-        turned[...] = a_ref[...].T
+        greet([("fsdp", twin)] + (others("seq", n) if beside else []))
+        if beside:
+            for copy in exchange_copies(n, [given], [taken], esend, erecv, local):
+                copy.start()
+        if not flipped:
+            turned[...] = a_ref[...].T
 
     begin = 0
     for b_ref, count in zip(bs, counts):
@@ -837,6 +914,9 @@
         if tiles >= 2:
             move(tiles - 2).wait_send()
         move(tiles - 1).wait_send()
+        if beside:
+            for copy in exchange_copies(n, [given], [taken], esend, erecv, local):
+                copy.wait()
 
 
 def exchange_copies(n, ins, outs, send, recv, local):
@@ -850,14 +930,15 @@
                 remote(source.at[to], out.at[me], send.at[k], recv.at[k], "seq", to)
             )
         copies.append(pltpu.make_async_copy(source.at[me], out.at[me], local.at[i]))
+    return copies
+
+
+def exchange(n, source, out, send, recv, local):
+    greet(others("seq", n))
+    copies = exchange_copies(n, [source], [out], send, recv, local)
     for copy in copies:
         copy.start()
-    return copies
-
-
-def exchange(n, source, out, send, recv, local):
-    greet(others("seq", n))
-    for copy in exchange_copies(n, [source], [out], send, recv, local):
+    for copy in copies:
         copy.wait()
 
 
@@ -867,31 +948,75 @@
         out[...] = ins[i][0, :, begin : begin + count].astype(F32)
 
 
-def exchange_gains(n, nf, gu, dn, one, two, gq, gk, gu_out, dn_out, out, part, wide, mid, seen, send, recv, local, gsend, grecv):
+def last_stage(n, nf, dq, dk, dv, w, x, gain, gu, two, gq, gk, out, gu_out, gains, part, slots, stage, send, recv, row, small, wide, mid, seen, esend, erecv, local, gsend, grecv):
     me, spot = lax.axis_index("seq"), lax.axis_index("fsdp")
     greet(others("seq", n) + others("fsdp", nf))
-    part[...] = jnp.zeros_like(part)
-    count = one.shape[0]
-    per = n * nf // count
+    row[...] = jnp.zeros_like(row)
+    rows, width = x.shape
+    qw, kw = dq.shape[1], dk.shape[1]
+    step = 512
+
+    def block(to):
+        at = pl.ds(pl.multiple_of(to * rows, rows), rows)
+
+        def columns(number, carry):
+            span = pl.ds(pl.multiple_of(number * step, step), step)
+            value = dot_nt(dq[at, :], w[span, pl.ds(0, qw)])
+            value += dot_nt(dk[at, :], w[span, pl.ds(qw, kw)])
+            value += dot_nt(dv[at, :], w[span, pl.ds(qw + kw, kw)])
+            part[to, :, span] = value.astype(BF)
+            return carry
+
+        lax.fori_loop(0, width // step, columns, 0)
+
+    def finish(at, total):
+        back, dg = norm_back(x[at].astype(F32), gain[...], total)
+        out[at] = back
+        row[...] += dg
+
+    start, relay, lower, upper = scatter_parts(n, part, slots, stage, send, recv, finish)
+    exchanges = exchange_copies(n, [gu], [gu_out], esend, erecv, local)
+    if n == 4:
+        across, along, corner = square(me)
+        block(corner)
+        start(0, 2)
+        block(across)
+        start(2, 3)
+        block(along)
+        start(3, 4)
+        relay()
+        for copy in exchanges:
+            copy.start()
+        block(me)
+    else:
+        for j in range(n):
+            block(lax.rem(me + j, n))
+        start()
+        for copy in exchanges:
+            copy.start()
+    lower()
+    upper()
+    small[...] = jnp.zeros_like(small)
+    per = 128 * n * nf // width
+    one = row[...]
     for f in range(nf):
         for seq in range(n):
-            row = (seq * nf + f) // per
-            part[f, seq, 0:1] = one[row : row + 1]
-            part[f, seq, 1:2] = two[row : row + 1]
-            part[f, seq, 2:3] = gq[0:1]
-            part[f, seq, 3:4] = gk[0:1]
+            line = (seq * nf + f) // per
+            small[f, seq, 0:1] = one[:, line * 128 : line * 128 + 128]
+            small[f, seq, 1:2] = two[line : line + 1]
+            small[f, seq, 2:3] = gq[0:1]
+            small[f, seq, 3:4] = gk[0:1]
     far = []
     for j in range(1, nf):
         to = lax.rem(spot + j, nf)
         far.append(
-            remote(part.at[to], wide.at[j - 1], gsend.at[j - 1], grecv.at[j - 1], "fsdp", to)
+            remote(small.at[to], wide.at[j - 1], gsend.at[j - 1], grecv.at[j - 1], "fsdp", to)
         )
     for copy in far:
         copy.start()
-    copies = exchange_copies(n, [gu, dn], [gu_out, dn_out], send, recv, local)
     for copy in far:
         copy.wait_recv()
-    total = part[spot]
+    total = small[spot]
     for j in range(nf - 1):
         total += wide[j]
     mid[...] = total
@@ -907,10 +1032,10 @@
     result = mid[me]
     for j in range(n - 1):
         result += seen[j]
-    out[...] = result
+    gains[...] = result
     for copy in far + near:
         copy.wait_send()
-    for copy in copies:
+    for copy in exchanges:
         copy.wait()
 
 
@@ -1046,7 +1171,7 @@
         functools.partial(project, n),
         grid=(blocks,),
         out_shape=(
-            shape((group, width), BF),
+            shape((width, group), BF),
             shape((group, qw), F32),
             shape((group, kw), F32),
             shape((group, qw), BF),
@@ -1067,7 +1192,7 @@
             ANY,
         ],
         out_specs=(
-            by_rows(256, width),
+            by_cols(width, 256),
             by_rows(256, qw),
             by_rows(256, kw),
             by_rows(256, qw),
@@ -1125,24 +1250,29 @@
 
     tile = 256
     tiles = fw // tile
-    gate, up, hidden = pl.pallas_call(
-        ffn_forward,
+    cuts = 1
+    while 2 * cuts <= tiles:
+        cuts *= 2
+    gate, up, hidden, n2_turned = pl.pallas_call(
+        functools.partial(ffn_forward, cuts),
         grid=(tiles,),
         out_shape=(
             shape((group, fw), F32),
             shape((group, fw), F32),
             shape((group, fw), BF),
+            shape((width, group), BF),
         ),
         in_specs=[
             whole((group, width)),
             by_cols(width, tile),
             pl.BlockSpec((width, tile), lambda i: (0, i + tiles)),
         ],
-        out_specs=(by_cols(group, tile),) * 3,
+        out_specs=(by_cols(group, tile),) * 3
+        + (pl.BlockSpec((width // cuts, group), lambda i: (jnp.minimum(i, cuts - 1), 0)),),
         compiler_params=plain_params(),
     )(n2, gu, gu)
 
-    def product(number, a, *bs, into=None, dims=None, spot=0):
+    def product(number, a, *bs, into=None, flipped=False, given=None):
         tile = 512
         while any(b.shape[1] % tile for b in bs):
             tile //= 2
@@ -1155,35 +1285,32 @@
                 (group, tile), lambda i: (0, jnp.clip(i - begin, 0, count - 1))
             )
 
-        if dims is None:
-            dims = (n, width // n // 2, tiles * tile)
-        lead = a.shape[1] // 2 // dims[1]
-        across = dims[2] // tile
+        dims = (n, width // n // 2, tiles * tile) if into is None else into.shape
         kept = [] if into is None else [into]
-        blocks = a.shape[1] // (2 * depth)
-
-        def place(i):
-            last = jnp.maximum(i - 1, 0)
-            return (spot + lax.div(last, across), 0, lax.rem(last, across))
-
-        return pl.pallas_call(
-            functools.partial(gradient, counts, len(kept)),
+        side = [] if given is None else [given]
+        blocks = width // (2 * depth)
+        outs = [pl.BlockSpec((n, dims[1], tile), lambda i: (0, 0, jnp.maximum(i - 1, 0)))]
+        extra = [dma(n - 1), dma(n - 1), dma(1)] if side else []
+        result = pl.pallas_call(
+            functools.partial(gradient, n, counts, len(kept), flipped, len(side)),
             grid=(tiles + 1,),
-            out_shape=shape(dims, BF),
+            out_shape=(shape(dims, BF),) + tuple(shape(g.shape, BF) for g in side),
             in_specs=[whole(a.shape)]
             + [spec(b, c) for b, c in zip(begins, counts)]
-            + [ANY] * len(kept),
-            out_specs=pl.BlockSpec((lead, dims[1], tile), place),
+            + [ANY] * len(kept + side),
+            out_specs=tuple(outs + [ANY] * len(side)),
             scratch_shapes=[
-                pltpu.VMEM((a.shape[1], group), BF),
                 pltpu.VMEM((2, blocks, 2, depth, tile), BF),
                 pltpu.VMEM((tiles, blocks, depth, tile), BF),
                 dma(tiles),
                 dma(tiles),
-            ],
+            ]
+            + extra
+            + ([] if flipped else [pltpu.VMEM((width, group), BF)]),
             input_output_aliases={} if into is None else {1 + len(bs): 0},
             compiler_params=comm_params(number),
-        )(a, *bs, *kept)
+        )(a, *bs, *kept, *side)
+        return result if side else result[0]
 
     same_core = [[core + 2 * i for i in range(nf // 2)] for core in range(2)]
 
@@ -1209,21 +1336,8 @@
         compiler_params=plain_params(),
     )(cg, after(dn, dn_grad), gate, up)
 
-    gu_grad = product(13, n2, dgate, dup)
-    part_n2 = pl.pallas_call(
-        two_nt,
-        grid=(blocks,),
-        out_shape=shape((group, width), BF),
-        in_specs=[
-            by_rows(256, fw),
-            by_rows(256, fw),
-            pl.BlockSpec((width, fw), lambda i: (0, 0)),
-            pl.BlockSpec((width, fw), lambda i: (0, 1)),
-        ],
-        out_specs=by_rows(256, width),
-        compiler_params=plain_params(),
-    )(after(dgate, gu_grad), dup, gu, gu)
-    gu_share = reduce_rows(after(gu_grad, (dn_share, part_n2)))
+    gu_grad = product(13, n2_turned, dgate, dup, flipped=True)
+    gu_share = reduce_rows(gu_grad)
 
     dx2, dz, dgain_two, part_y = pl.pallas_call(
         functools.partial(back_stage, n),
@@ -1233,9 +1347,10 @@
             shape((width // 128, 128), F32),
             shape((n, rows, width), BF),
         ),
-        in_specs=[VMEM] * 4 + [ANY] * 2,
+        in_specs=[ANY] * 3 + [VMEM] * 3 + [ANY] * 2,
         out_specs=(VMEM, ANY, VMEM, VMEM),
-        scratch_shapes=slots
+        scratch_shapes=[pltpu.VMEM((n, rows, width), BF)]
+        + slots
         + [pltpu.VMEM((rows, width), BF)]
         + sems
         + gather_sems
@@ -1244,17 +1359,20 @@
             pltpu.VMEM((group, fw), BF),
             pltpu.VMEM((width, fw), BF),
             dma(2),
+            pltpu.VMEM((group, fw), BF),
+            pltpu.VMEM((group, fw), BF),
+            pltpu.VMEM((width, 2 * fw), BF),
+            pltpu.SemaphoreType.DMA((2, n)),
+            dma(width // 512),
         ],
         compiler_params=comm_params(4),
     )(
-        after(part_n2, dn_share).reshape(n, rows, width), x2, cotangent, gain_two, hidden, dn,
+        after(dgate, gu_grad), dup, gu, x2, cotangent, gain_two, hidden, dn,
     )
     dz = dz.reshape(group, width)
 
-    wo_grad = product(14, attn, dz, dims=(n + width // cw, qw // 2, cw), spot=n)
-
     wide = ratio * head
-    dq, dk, dv, dgain_q, dgain_k, branch = pl.pallas_call(
+    dq, dk, dv, dgain_q, dgain_k, branch, wo_grad = pl.pallas_call(
         functools.partial(attend_back, n),
         grid=(kheads, blocks),
         out_shape=(
@@ -1264,6 +1382,7 @@
             shape((8, head), F32),
             shape((8, head), F32),
             shape((rows, width), F32),
+            shape((n + width // cw, width // n // 2, cw), BF),
         ),
         in_specs=[
             pl.BlockSpec((256, wide), lambda h, b: (b, h)),
@@ -1283,6 +1402,7 @@
             whole((group, head)),
             whole((1, head)),
             whole((1, head)),
+            pl.BlockSpec((256, wide), lambda h, b: (b, h)),
             VMEM,
         ],
         out_specs=(
@@ -1292,55 +1412,62 @@
             whole((8, head)),
             whole((8, head)),
             VMEM,
+            ANY,
         ),
         scratch_shapes=[pltpu.VMEM((group, head), F32), pltpu.VMEM((group, head), F32)]
         + slots
-        + sems,
+        + sems
+        + [
+            pltpu.VMEM((wide, width), F32),
+            pltpu.VMEM((kheads, wide // (2 * depth), 2, depth, width), BF),
+            pltpu.VMEM((kheads, wide // (2 * depth), depth, width), BF),
+            pltpu.VMEM((kheads, wide // 2, width), BF),
+            dma(kheads),
+            dma(kheads),
+            pltpu.SemaphoreType.DMA((kheads, width // cw)),
+        ],
         compiler_params=comm_params(5),
     )(
         q, qraw, k, kt, v, kraw, dz, wo, lse, low, high, cos, sin, cos, sin, gain_q, gain_k,
-        part_y,
+        attn, part_y,
     )
     output = (x2 + branch).astype(BF)
 
-    att_grad = product(15, n1, dq, dk, dv, into=wo_grad, dims=wo_grad.shape)
+    att_grad, dn_mine = product(
+        15, n1, dq, dk, dv, into=wo_grad, flipped=True, given=dn_share
+    )
     att_share = reduce_rows(after(att_grad, gu_share))
 
-    back_one, dgain_one = pl.pallas_call(
-        functools.partial(input_stage, n),
-        out_shape=(shape((rows, width), F32), shape((width // 128, 128), F32)),
-        in_specs=[VMEM] * 6,
-        out_specs=(VMEM, VMEM),
+    back_one, gu_mine, gains = pl.pallas_call(
+        functools.partial(last_stage, n, nf),
+        out_shape=(
+            shape((rows, width), F32),
+            shape(gu_share.shape, BF),
+            shape((8, 128), F32),
+        ),
+        in_specs=[VMEM] * 6 + [ANY] + [VMEM] * 3,
+        out_specs=(VMEM, ANY, VMEM),
         scratch_shapes=[pltpu.VMEM((n, rows, width), BF)]
         + slots
         + sems
-        + [pltpu.VMEM((1, width), F32)],
-        compiler_params=comm_params(10),
-    )(after(dq, att_grad), dk, dv, w_att, tokens, gain_one)
-    input_grad = (dx2 + back_one).astype(BF)
-
-    gu_mine, dn_mine, gains = pl.pallas_call(
-        functools.partial(exchange_gains, n, nf),
-        out_shape=(
-            shape(gu_share.shape, BF),
-            shape(dn_share.shape, BF),
-            shape((8, 128), F32),
-        ),
-        in_specs=[ANY] * 2 + [VMEM] * 4,
-        out_specs=(ANY, ANY, VMEM),
-        scratch_shapes=[
+        + [
+            pltpu.VMEM((1, width), F32),
             pltpu.VMEM((nf, n, 8, 128), F32),
             pltpu.VMEM((nf - 1, n, 8, 128), F32),
             pltpu.VMEM((n, 8, 128), F32),
             pltpu.VMEM((n - 1, 8, 128), F32),
-            dma(2 * (n - 1)),
-            dma(2 * (n - 1)),
-            dma(2),
+            dma(n - 1),
+            dma(n - 1),
+            dma(1),
             dma(n + nf - 2),
             dma(n + nf - 2),
         ],
         compiler_params=comm_params(7),
-    )(gu_share, dn_share, dgain_one, dgain_two, dgain_q, dgain_k)
+    )(
+        after(dq, att_grad), dk, dv, w_att, tokens, gain_one, gu_share,
+        dgain_two, dgain_q, dgain_k,
+    )
+    input_grad = (dx2 + back_one).astype(BF)
 
     def owned(row, count, mine):
         return lax.dynamic_slice_in_dim(row, mine * count, count, 0)

time: 575 us -> 541 us (0.941)
  Pallas kernels: 537 us -> 503 us
    pallas_call x8 -> x5, Pallas kernels: 177 us -> 136 us  [the longest x1 61.8 us: shards(): pl.pallas_call(functools.partial(last_stage, n, nf), out_shape=(shape((ro...]
    pallas_call x1, Pallas kernels: 78.9 us -> 87.6 us  [shards(): pl.pallas_call(functools.partial(back_stage, n), out_shape=(shape((rows,...]
  transfers between devices with their start and end apart: 6 -> 6, of which waited for: 2 -> 1; matrix products, arithmetic and copies ran while one was open for 2% -> 2% of each run, Pallas kernels for 89% -> 89%
where the time goes in v4:
time: 541 us; the launch traced here: 540 us
  Pallas kernels  503 us (93%)
  between operations  14.3 us (3%)
  local copies, waits for them, and re-layouts  9.12 us (2%)
  other arithmetic  6.63 us (1%)
  waiting for transfers between devices  5.98 us (1%)
    pallas_call x1, Pallas kernels, shards(): pl.pallas_call(functools.partial(back_stage, n), out_shape=(shape((rows,...  87.6 us
    pallas_call x1, Pallas kernels, shards(): pl.pallas_call(functools.partial(middle_stage, n), out_shape=(shape((rows...  73.3 us
    pallas_call x1, Pallas kernels, shards(): pl.pallas_call(functools.partial(last_stage, n, nf), out_shape=(shape((ro...  61.8 us
    pallas_call x3, Pallas kernels, product(): pl.pallas_call(functools.partial(gradient, n, counts, len(kept), flipped,...  53.2 us
    pallas_call x1, Pallas kernels, shards(): pl.pallas_call(functools.partial(entry_stage, n, nf, line, own_gain), out...  52.9 us
    pallas_call x1, Pallas kernels, shards(): pl.pallas_call(functools.partial(attend_back, n), grid=(kheads, blocks),...  41.7 us
    pallas_call x1, Pallas kernels, shards(): pl.pallas_call(functools.partial(gate_up_out, n, nf), out_shape=(shape((n...  23.8 us
    pallas_call x1, Pallas kernels, shards(): pl.pallas_call(functools.partial(project, n), grid=(blocks,), out_shape=(...  23.5 us
  transfers between devices with their start and end apart: 6, of which 1 were waited for; matrix products, arithmetic and copies ran while one was open for 2% of the time, Pallas kernels for 89%

profile of v4, /device:TPU:0, one launch (start us, length us, event | category | flops | bytes accessed | tf_op | source)
XLA Modules:
  0.0 539.9 jit_solution(13689062608511368653)
XLA Ops:
  7.2 0.0 all-gather.4.cloned.1.call-start
  7.2 11.1 %shard_map.264 = bf16[4,64,1024]{2,1,0:T(8,128)(2,1)} custom-call(bf16[64,2048]{1,0:T(8,128)(2,1)} %wq.1, bf16[64,1024]{1,0:T(8,128)(2,1)} %wk.1, bf16[64,1024]{1,0:T(8,128)(2,1)} %wv.1), custom_call_target="tpu_custom_call" | custom-call | tf_op jit(solution)/shard_map/pallas_call | solution.py:1102
  18.3 0.0 all-gather.4.cloned.1.call-update
  18.3 0.0 all-gather.8.cloned.1.call-start
  18.4 0.7 tile.8
  19.1 0.1 broadcast_in_dim_tile.12
  19.1 0.7 tile.9
  19.8 0.1 broadcast_in_dim_tile.13
  19.9 0.7 tile.10
  20.5 0.1 broadcast_in_dim_tile.14
  20.6 0.7 tile.11
  21.3 0.1 broadcast_in_dim_tile.15
  21.5 0.6 concatenate.3.gains
  22.1 23.8 %shard_map.265 = (bf16[4,64,3072]{2,1,0:T(8,128)(2,1)}, f32[8,4,8,128]{3,2,1,0:T(8,128)}) custom-call(bf16[64,6144]{1,0:T(8,128)(2,1)} %wg, bf16[64,6144]{1,0:T(8,128)(2,1)} %wu.1, f32[8,128]{1,0:T(8,128)} %concatenate.3.gains), custom_call_target="tpu_custom_call" | custom-call | tf_op jit(solution)/shard_map/pallas_call | solution.py:1110
  45.9 0.0 all-gather.6.cloned.1.call-start
  45.9 52.9 %shard_map.266 = (bf16[4,256,2048]{2,1,0:T(8,128)(2,1)}, bf16[4,64,1536]{2,1,0:T(8,128)(2,1)}, bf16[8,64,2048]{2,1,0:T(8,128)(2,1)}, f32[1,2048]{1,0:T(1,128)}, ...) custom-call(bf16[256,2048]{1,0:T(8,128)(2,1)} %x.4, ...), custom_call_target="tpu_custom_call" | custom-call | tf_op jit(solution)/shard_map/pallas_call | solution.py:1133
  98.9 0.0 reduce-scatter.4.cloned.1.call-start
  99.0 0.0 all-gather.4.cloned.1.call-done
  99.0 23.5 %shard_map.267 = (bf16[2048,1024]{1,0:T(8,128)(2,1)}, f32[1024,512]{1,0:T(8,128)}, f32[1024,256]{1,0:T(8,128)}, bf16[1024,512]{1,0:T(8,128)(2,1)}, bf16[1024,256...) custom-call(bf16[1024,2048]{1,0:T(8,128)(2,1)} %bitcast.37, ...), custom_call_target="tpu_custom_call" | custom-call | tf_op jit(solution)/shard_map/pallas_call | solution.py:1170
  122.5 21.7 %shard_map.268 = (bf16[1024,512]{1,0:T(8,128)(2,1)}, f32[8,1024]{1,0:T(8,128)}, bf16[1024,2048]{1,0:T(8,128)(2,1)}, bf16[4,256,2048]{2,1,0:T(8,128)(2,1)}) custom-call(bf16[1024,512]{1,0:T(8,128)(2,1)} %get-tuple-element.86.q_ref, bf16[1024,256]{1,0:T(8,128)(2,1)} %get-tuple-element.87.k_ref, ...), custom_call_target="tpu_custom_call", output_to_operand_aliasing={{3}: (7, {})} | custom-call | tf_op jit(solution)/shard_map/pallas_call | solution.py:1209
  144.2 73.3 %shard_map.269 = (f32[256,2048]{1,0:T(8,128)}, bf16[4,256,2048]{2,1,0:T(8,128)(2,1)}) custom-call(bf16[4,256,2048]{2,1,0:T(8,128)(2,1)} %bitcast.36, bf16[256,2048]{1,0:T(8,128)(2,1)} %x.4, f32[1,2048]{1,0:T(1,128)} %get-tuple-element.94.gain), custom_call_target="tpu_custom_call" | custom-call | tf_op jit(solution)/shard_map/pallas_call | solution.py:1241
  217.6 0.0 all-gather.8.cloned.1.call-done
  217.6 20.6 %shard_map.270 = (f32[1024,1536]{1,0:T(8,128)}, f32[1024,1536]{1,0:T(8,128)}, bf16[1024,1536]{1,0:T(8,128)(2,1)}, bf16[2048,1024]{1,0:T(8,128)(2,1)}) custom-call(bf16[1024,2048]{1,0:T(8,128)(2,1)} %bitcast.35, bf16[2048,3072]{1,0:T(8,128)(2,1)} %bitcast.23, bf16[2048,3072]{1,0:T(8,128)(2,1)} %bitcast.24), custom_call_target="tpu_custom_call" | custom-call | tf_op jit(solution)/shard_map/pallas_call | solution.py:1256
  238.2 15.3 %shard_map.271 = bf16[4,256,1536]{2,1,0:T(8,128)(2,1)} custom-call(bf16[1024,2048]{1,0:T(8,128)(2,1)} %bitcast.26, bf16[1024,1536]{1,0:T(8,128)(2,1)} %get-tuple-element.103.refs_1_.hidden_far), custom_call_target="tpu_custom_call" | custom-call | tf_op jit(solution)/shard_map/pallas_call | solution.py:1294
  253.5 0.2 reduce-scatter.6.cloned.1.call-start
  253.8 5.8 %all-gather.6.cloned.1.call-done = bf16[4,512,1536]{2,1,0:T(8,128)(2,1)} async-done(((bf16[4,64,1536]{2,1,0:T(8,128)(2,1)}), bf16[4,512,1536]{2,1,0:T(8,128)(2,1)}) %all-gather.6.cloned.1.call-update) | async-done | bytes 6291472 | tf_op jit(solution)/shard_map/all_gather | solution.py:1158
  259.6 15.6 %shard_map.272 = (bf16[1024,1536]{1,0:T(8,128)(2,1)}, bf16[1024,1536]{1,0:T(8,128)(2,1)}) custom-call(bf16[1024,2048]{1,0:T(8,128)(2,1)} %bitcast.27, bf16[2048,1536]{1,0:T(8,128)(2,1)} %bitcast.28, f32[1024,1536]{1,0:T(8,128)} %get-tuple-element.105.gate_ref, f32[1024,1536]{1,0:T(8,128)} %get-tuple-element.106.up_ref), custom_call_target="tpu_custom_call" | custom-call | tf_op jit(solution)/shard_map/pallas_call | solution.py:1325
  275.1 22.3 %shard_map.273 = bf16[4,256,3072]{2,1,0:T(8,128)(2,1)} custom-call(bf16[2048,1024]{1,0:T(8,128)(2,1)} %get-tuple-element.108.refs_0_, bf16[1024,1536]{1,0:T(8,128)(2,1)} %get-tuple-element.110.refs_1_.dgate_far, bf16[1024,1536]{1,0:T(8,128)(2,1)} %get-tuple-element.109.refs_2_.dup_far), custom_call_target="tpu_custom_call" | custom-call | tf_op jit(solution)/shard_map/pallas_call | solution.py:1294
  297.5 0.0 reduce-scatter.8.cloned.1.call-start
  297.5 87.6 %shard_map.274 = (f32[256,2048]{1,0:T(8,128)}, bf16[4,256,2048]{2,1,0:T(8,128)(2,1)}, f32[16,128]{1,0:T(8,128)}, bf16[4,256,2048]{2,1,0:T(8,128)(2,1)}) custom-call(bf16[1024,1536]{1,0:T(8,128)(2,1)} %get-tuple-element.110.refs_1_.dgate_far, bf16[1024,1536]{1,0:T(8,128)(2,1)} %get-tuple-element.109.refs_2_.dup_far, bf16[2048,3072]{1,0:T(8,128)(2,1)} %bitcast.25, ...), custom_call_target="tpu_custom_call" | custom-call | tf_op jit(solution)/shard_map/pallas_call | solution.py:1342
  385.2 41.7 %shard_map.275 = (bf16[1024,512]{1,0:T(8,128)(2,1)}, bf16[1024,256]{1,0:T(8,128)(2,1)}, bf16[1024,256]{1,0:T(8,128)(2,1)}, f32[8,128]{1,0:T(8,128)}, f32[8,128]{...) custom-call(bf16[1024,512]{1,0:T(8,128)(2,1)} %get-tuple-element.86.q_ref, ...), custom_call_target="tpu_custom_call" | custom-call | tf_op jit(solution)/shard_map/pallas_call | solution.py:1375
  426.9 0.0 reduce-scatter.4.cloned.1.call-done.refs_5_
  426.9 15.6 %shard_map.276 = (bf16[6,256,1024]{2,1,0:T(8,128)(2,1)}, bf16[4,64,1536]{2,1,0:T(8,128)(2,1)}) custom-call(bf16[2048,1024]{1,0:T(8,128)(2,1)} %get-tuple-element.118.refs_0_, bf16[1024,512]{1,0:T(8,128)(2,1)} %get-tuple-element.123.refs_1_.dq, bf16[1024,256]{1,0:T(8,128)(2,1)} %get-tuple-element.119.refs_2_.dk, ...), custom_call_target="tpu_custom_call", output_to_operand_aliasing={{0}: (4, {})} | custom-call | tf_op jit(solution)/shard_map/pallas_call | solution.py:1294
  442.6 0.0 reduce-scatter.6.cloned.1.call-done.gu
  442.7 1.5 copy-done
  444.2 2.8 add_convert_fusion.1
  447.0 61.8 %shard_map.277 = (f32[256,2048]{1,0:T(8,128)}, bf16[4,64,3072]{2,1,0:T(8,128)(2,1)}, f32[8,128]{1,0:T(8,128)}) custom-call(bf16[1024,512]{1,0:T(8,128)(2,1)} %get-tuple-element.123.refs_1_.dq, bf16[1024,256]{1,0:T(8,128)(2,1)} %get-tuple-element.119.refs_2_.dk, bf16[1024,256]{1,0:T(8,128)(2,1)} %get-tuple-element.120.refs_3_.dv, ...), custom_call_target="tpu_custom_call" | custom-call | tf_op jit(solution)/shard_map/pallas_call | solution.py:1441
  508.8 4.4 shard_map.278
  513.2 0.8 fusion.4
  514.1 0.6 fusion.3
  514.7 0.6 fusion.2
  515.2 0.6 fusion.1
  515.8 0.6 fusion
  516.4 2.8 add_convert_fusion
  519.2 1.0 convert_bitcast_fusion
  520.2 0.8 copy.33
  521.1 8.8 %shard_map.279.refs_0_ = bf16[4,64,1024]{2,1,0:T(8,128)(2,1)} custom-call(bf16[6,64,1024]{2,1,0:T(8,128)(2,1)} %reduce-scatter.8.cloned.1.call-done.source), custom_call_target="tpu_custom_call" | custom-call | tf_op jit(solution)/shard_map/pallas_call | solution.py:1500
  529.8 3.2 shard_map.280
  (12 shorter events, 0.1 us)
Async XLA Ops:
  7.2 91.8 %all-gather.4.cloned.1.call-start = ((), (), s32[]{:S(2)}) async-start(), calls=%async_computation.3 | async-start | bytes 4718592 | tf_op jit(solution)/shard_map/all_gather | solution.py:1128
  18.3 199.2 %all-gather.8.cloned.1.call-start = ((), (), s32[]{:S(2)}) async-start(), calls=%async_computation.5 | async-start | bytes 14155776 | tf_op jit(solution)/shard_map/all_gather | solution.py:1157
  45.9 213.7 %all-gather.6.cloned.1.call-start = ((), (), s32[]{:S(2)}) async-start(), calls=%async_computation.4 | async-start | bytes 7077888 | tf_op jit(solution)/shard_map/all_gather | solution.py:1158
  98.9 328.0 %reduce-scatter.4.cloned.1.call-start = ((), (), s32[]{:S(2)}) async-start(), calls=%async_computation.6 | async-start | bytes 3932160 | tf_op jit(solution)/shard_map/reduce_scatter | solution.py:1318
  253.5 189.1 %reduce-scatter.6.cloned.1.call-start = ((), (), s32[]{:S(2)}) async-start(), calls=%async_computation.7 | async-start | bytes 7864320 | tf_op jit(solution)/shard_map/reduce_scatter | solution.py:1318
  297.5 221.7 %reduce-scatter.8.cloned.1.call-start = ((), (), s32[]{:S(2)}) async-start(), calls=%async_computation.8 | async-start | bytes 3932160 | tf_op jit(solution)/shard_map/reduce_scatter | solution.py:1318
  442.6 1.6 copy-start
  508.8 7.6 %copy-start.1 = (f32[256,2048]{1,0:T(8,128)S(1)}, f32[256,2048]{1,0:T(8,128)}, u32[]{:S(2)}) copy-start(f32[256,2048]{1,0:T(8,128)} %get-tuple-element.116) | copy-start | bytes 6291460
Sparse Core Ops, SparseCore 0:
  18.5 58.1 all-gather.3
  78.2 116.7 all-gather.7
  196.6 62.8 all-gather.5
  261.7 58.9 reduce-scatter.3
  322.8 110.7 reduce-scatter.5
  442.8 60.1 reduce-scatter.7

commit v5 on v4

--- a/solution.py
+++ b/solution.py
@@ -179,8 +179,9 @@
         for i, (src, dst, to) in enumerate(moves)
     ]
 
-    def start(begin=0, end=4):
-        for copy in copies[begin:end] if n == 4 else copies:
+    def start(*chosen):
+        chosen = chosen if chosen else (0, 1, 3)
+        for copy in [copies[i] for i in chosen] if n == 4 else copies:
             copy.start()
 
     def relay():
@@ -188,6 +189,7 @@
             copies[0].wait_recv()
             stage[low] = (part[across, low].astype(F32) + slots[2, low].astype(F32)).astype(BF)
             copies[4].start()
+            copies[2].start()
             copies[1].wait_recv()
             stage[high] = (part[along, high].astype(F32) + slots[2, high].astype(F32)).astype(BF)
             copies[5].start()
@@ -231,40 +233,7 @@
     return back, jnp.sum(grad * values * inverse, axis=0, keepdims=True)
 
 
-def attention_weights_out(n, wq, wk, wv, out, send, recv, local):
-    me = lax.axis_index("seq")
-    greet(others("seq", n))
-    widths = [wq.shape[1] // n, wk.shape[1] // n, wv.shape[1] // n]
-    begins = [0, widths[0], widths[0] + widths[1]]
-    copies = []
-    for j in range(1, n):
-        to = lax.rem(me + j, n)
-        for i, ref in enumerate((wq, wk, wv)):
-            columns = pl.ds(pl.multiple_of(to * widths[i], 128), widths[i])
-            copies.append(
-                remote(
-                    ref.at[:, columns],
-                    out.at[me, :, pl.ds(begins[i], widths[i])],
-                    send.at[3 * j - 3 + i],
-                    recv.at[3 * j - 3 + i],
-                    "seq",
-                    to,
-                )
-            )
-    for i, ref in enumerate((wq, wk, wv)):
-        columns = pl.ds(pl.multiple_of(me * widths[i], 128), widths[i])
-        copies.append(
-            pltpu.make_async_copy(
-                ref.at[:, columns], out.at[me, :, pl.ds(begins[i], widths[i])], local.at[i]
-            )
-        )
-    for copy in copies:
-        copy.start()
-    for copy in copies:
-        copy.wait()
-
-
-def start_columns(n, views, send, recv, local):
+def start_columns(n, views, send, recv, local, begin=True):
     me = lax.axis_index("seq")
     width = views[0][0].shape[1] // n
     copies, keeps = [], []
@@ -289,92 +258,46 @@
                 ref.at[:, columns], out.at[me, :, pl.ds(place * width, width)], local.at[i]
             )
         )
-    for copy in copies + keeps:
-        copy.start()
+    if begin:
+        for copy in copies + keeps:
+            copy.start()
     return copies + keeps
 
 
-def gate_up_out(n, nf, wg, wu, gains, gu, all_gains, seen, send, recv, local, gsend, grecv, glocal):
-    me, spot = lax.axis_index("seq"), lax.axis_index("fsdp")
-    greet(others("seq", n) + others("fsdp", nf))
-    small = []
-    for j in range(1, n):
-        to = lax.rem(me + j, n)
-        small.append(
-            remote(gains, seen.at[me], gsend.at[j - 1], grecv.at[j - 1], "seq", to)
-        )
-    keep = pltpu.make_async_copy(gains, seen.at[me], glocal.at[0])
-    for copy in small + [keep]:
-        copy.start()
-    copies = start_columns(n, [(wg, gu, 0), (wu, gu, 1)], send, recv, local)
-    for copy in small + [keep]:
-        copy.wait()
-    wide = [pltpu.make_async_copy(seen, all_gains.at[spot], glocal.at[1])]
-    for j in range(1, nf):
-        to = lax.rem(spot + j, nf)
-        k = n + j - 2
-        wide.append(
-            remote(seen, all_gains.at[spot], gsend.at[k], grecv.at[k], "fsdp", to)
-        )
-    for copy in wide:
-        copy.start()
-    for copy in copies + wide:
-        copy.wait()
-
-
-def line_gather(own, out, send, recv, local, between):
+def line_gather(cell, own, send, recv):
     spot = lax.axis_index("fsdp")
     z = lax.div(spot, 2)
     twin = spot + 1 - 2 * lax.rem(spot, 2)
-    keep = pltpu.make_async_copy(own, out.at[spot], local)
-    keep.start()
+
+    def hop(number, block, to):
+        source = own if isinstance(block, str) else cell(block)
+        target = cell(spot if isinstance(block, str) else block)
+        return remote(source, target, send.at[number], recv.at[number], "fsdp", to)
 
     def up(k):
-        block = spot - 2 * k
-        return remote(
-            own if k == 0 else out.at[block], out.at[block], send.at[k], recv.at[k], "fsdp", spot + 2
-        )
+        return hop(k, "own" if k == 0 else spot - 2 * k, spot + 2)
 
     def down(k):
-        block = spot + 2 * k
-        return remote(
-            own if k == 0 else out.at[block],
-            out.at[block],
-            send.at[3 + k],
-            recv.at[3 + k],
-            "fsdp",
-            spot - 2,
-        )
+        return hop(3 + k, "own" if k == 0 else spot + 2 * k, spot - 2)
 
     def over(offset):
-        block = spot + 2 * offset
-        return remote(
-            own if offset == 0 else out.at[block],
-            out.at[block],
-            send.at[6 + lax.div(block, 2)],
-            recv.at[6 + lax.div(block, 2)],
-            "fsdp",
-            twin,
-        )
+        return hop(6 + z + offset, "own" if offset == 0 else spot + 2 * offset, twin)
 
     def from_twin(offset):
-        block = twin + 2 * offset
-        return remote(
-            own, out.at[block], send.at[6 + lax.div(block, 2)], recv.at[6 + lax.div(block, 2)], "fsdp", twin
-        )
-
-    @pl.when(z < 3)
-    def _():
-        up(0).start()
-
-    @pl.when(z > 0)
-    def _():
-        down(0).start()
-
-    over(0).start()
-    between()
-    for k in range(1, 4):
-
+        return hop(6 + z + offset, twin + 2 * offset, twin)
+
+    def first():
+        @pl.when(z < 3)
+        def _():
+            up(0).start()
+
+        @pl.when(z > 0)
+        def _():
+            down(0).start()
+
+        over(0).start()
+
+    def step(k):
         @pl.when(z >= k)
         def _():
             up(k - 1).wait_recv()
@@ -397,63 +320,147 @@
 
             over(k).start()
 
-    from_twin(0).wait_recv()
-    over(0).wait_send()
-    for k in range(1, 4):
-
-        @pl.when(z >= k)
-        def _():
-            from_twin(-k).wait_recv()
-            over(-k).wait_send()
-
-        @pl.when(z + k <= 3)
-        def _():
-            from_twin(k).wait_recv()
-            over(k).wait_send()
-
-    for k in range(3):
-
-        @pl.when((z >= k) & (z < 3))
-        def _():
-            up(k).wait_send()
-
-        @pl.when((z + k <= 3) & (z > 0))
-        def _():
-            down(k).wait_send()
-
-    keep.wait()
-
-
-def greet_line(places):
-    spot = lax.axis_index("fsdp")
-    z = lax.div(spot, 2)
-    twin = spot + 1 - 2 * lax.rem(spot, 2)
-    barrier = pltpu.get_barrier_semaphore()
-    for axis, index in places + [("fsdp", twin)]:
-        pl.semaphore_signal(barrier, inc=1, device_id={axis: index}, device_id_type=MESH)
-
-    @pl.when(z < 3)
-    def _():
-        pl.semaphore_signal(barrier, inc=1, device_id={"fsdp": spot + 2}, device_id_type=MESH)
-
-    @pl.when(z > 0)
-    def _():
-        pl.semaphore_signal(barrier, inc=1, device_id={"fsdp": spot - 2}, device_id_type=MESH)
-
-    inner = (z < 3).astype(jnp.int32) + (z > 0).astype(jnp.int32)
-    pl.semaphore_wait(barrier, len(places) + 1 + inner)
-
-
-def entry_stage(n, nf, line, own_gain, x, wd, w_out, gains, lengths, starts, sizes, freq, xg, dn, wo, gain_one, gain_two, gain_q, gain_k, cos, sin, low, high, send, recv, local, wsend, wrecv, wlocal, lsend, lrecv, llocal):
+    def finish():
+        from_twin(0).wait_recv()
+        over(0).wait_send()
+        for k in range(1, 4):
+
+            @pl.when(z >= k)
+            def _():
+                from_twin(-k).wait_recv()
+                over(-k).wait_send()
+
+            @pl.when(z + k <= 3)
+            def _():
+                from_twin(k).wait_recv()
+                over(k).wait_send()
+
+        for k in range(3):
+
+            @pl.when((z >= k) & (z < 3))
+            def _():
+                up(k).wait_send()
+
+            @pl.when((z + k <= 3) & (z > 0))
+            def _():
+                down(k).wait_send()
+
+    return first, step, finish
+
+
+def entry_stage(n, nf, line, own_gain, own_head, wq, wk, wv, wg, wu, x, w_out, raw, lengths, starts, sizes, freq, w_att, gu, xg, wo, gain_one, gain_two, gain_q, gain_k, cos, sin, low, high, mine, seen, gains, qsend, qrecv, qlocal, wsend, wrecv, wlocal, send, recv, local, gsend, grecv, glocal, asend, arecv, osend, orecv, olocal):
+    me, spot = lax.axis_index("seq"), lax.axis_index("fsdp")
+    greet(others("seq", n) + others("fsdp", nf))
+    place = spot if line else 0
     if line:
-        greet_line(others("seq", n))
-    else:
-        greet(others("seq", n))
+        o_first, o_step, o_finish = line_gather(lambda f: wo.at[f], w_out, osend, orecv)
+        a_first, a_step, a_finish = line_gather(
+            lambda f: w_att.at[:, f], w_att.at[:, spot], asend, arecv
+        )
+        o_first()
+    widths = [wq.shape[1] // n, wk.shape[1] // n, wv.shape[1] // n]
+    begins = [0, widths[0], widths[0] + widths[1]]
+    near = []
+    for j in range(1, n):
+        to = lax.rem(me + j, n)
+        for i, ref in enumerate((wq, wk, wv)):
+            columns = pl.ds(pl.multiple_of(to * widths[i], 128), widths[i])
+            near.append(
+                remote(
+                    ref.at[:, columns],
+                    w_att.at[me, place, :, pl.ds(begins[i], widths[i])],
+                    qsend.at[3 * j - 3 + i],
+                    qrecv.at[3 * j - 3 + i],
+                    "seq",
+                    to,
+                )
+            )
+    for i, ref in enumerate((wq, wk, wv)):
+        columns = pl.ds(pl.multiple_of(me * widths[i], 128), widths[i])
+        near.append(
+            pltpu.make_async_copy(
+                ref.at[:, columns],
+                w_att.at[me, place, :, pl.ds(begins[i], widths[i])],
+                qlocal.at[i],
+            )
+        )
+    for copy in near:
+        copy.start()
+    mine[...] = jnp.zeros_like(mine)
+    for count, first, index in (
+        (own_gain, 0, lax.rem(spot, 128 // own_gain)),
+        (own_head, 2, me * nf + spot),
+    ):
+        for at in range(128 // count):
+
+            @pl.when(index == at)
+            def _():
+                for i in (first, first + 1):
+                    mine[i : i + 1, at * count : at * count + count] = raw[
+                        :, i * 128 : i * 128 + count
+                    ]
+
+    small = [pltpu.make_async_copy(mine, seen.at[me], glocal.at[0])]
+    for j in range(1, n):
+        to = lax.rem(me + j, n)
+        small.append(remote(mine, seen.at[me], gsend.at[j - 1], grecv.at[j - 1], "seq", to))
+    keep = pltpu.make_async_copy(w_out, wo.at[place], olocal)
+    for copy in small + [keep]:
+        copy.start()
+    def rope():
+        group = cos.shape[0]
+        border_one = lengths[0, 0]
+        border_two = border_one + lengths[0, 1]
+
+        def begin_of(places):
+            later = jnp.where(places >= border_one, border_one, 0)
+            return jnp.where(places >= border_two, border_two, later)
+
+        step = 128
+        lane = lax.broadcasted_iota(jnp.int32, (step, 128), 1)
+
+        def turn(number, carry):
+            at = pl.ds(pl.multiple_of(number * step, step), step)
+            places = lax.broadcasted_iota(jnp.int32, (step, 128), 0) + number * step
+            angle = (places - begin_of(places)).astype(F32) * freq[...]
+            cos[at, :] = jnp.cos(angle)
+            sine = jnp.sin(angle)
+            sin[at, :] = jnp.where(lane < 64, -sine, sine)
+            return carry
+
+        lax.fori_loop(0, group // step, turn, 0)
+        places = lax.broadcasted_iota(jnp.int32, (8, group), 1)
+        end = jnp.where(places >= border_one, border_two, border_one)
+        end = jnp.where(places >= border_two, group, end)
+        picture = jnp.zeros_like(places)
+        for i in range(starts.shape[1]):
+            first, count = starts[0, i], sizes[0, i]
+            inside = (places >= first) & (places < first + count)
+            picture = jnp.where(inside, jnp.maximum(picture, first + count), picture)
+        low[...] = begin_of(places)
+        high[...] = jnp.maximum(places, jnp.minimum(picture, end) - 1)
+
+    rope()
+    for copy in near:
+        copy.wait()
+    if line:
+        a_first()
+    copies = start_columns(n, [(wg, gu, 0), (wu, gu, 1)], wsend, wrecv, wlocal)
     start, relay, finish = gather_parts(n, x, xg, send, recv, local)
     start()
-    copies = start_columns(n, [(wd, dn, 0)], wsend, wrecv, wlocal)
-
-    def tables():
+    if line:
+        o_step(1)
+    for copy in small:
+        copy.wait()
+    wide = [pltpu.make_async_copy(seen, gains.at[spot], glocal.at[1])]
+    for j in range(1, nf):
+        to = lax.rem(spot + j, nf)
+        k = n + j - 2
+        wide.append(remote(seen, gains.at[spot], gsend.at[k], grecv.at[k], "fsdp", to))
+    for copy in wide:
+        copy.start()
+
+    def unpack():
         per = 128 // own_gain
         for row in range(n * nf // per):
             seq, first = row * per // nf, row * per % nf
@@ -471,60 +478,35 @@
         gain_q[...] = total[2:3, :]
         gain_k[...] = total[3:4, :]
 
-        group = cos.shape[0]
-        border_one = lengths[0, 0]
-        border_two = border_one + lengths[0, 1]
-
-        def begin_of(places):
-            later = jnp.where(places >= border_one, border_one, 0)
-            return jnp.where(places >= border_two, border_two, later)
-
-        step = 128
-        lane = lax.broadcasted_iota(jnp.int32, (step, 128), 1)
-
-        def turn(number, carry):
-            at = pl.ds(pl.multiple_of(number * step, step), step)
-            places = lax.broadcasted_iota(jnp.int32, (step, 128), 0) + number * step
-            angle = (places - begin_of(places)).astype(F32) * freq[...]
-            cos[at, :] = jnp.cos(angle)
-            sine = jnp.sin(angle)
-            sin[at, :] = jnp.where(lane < 64, -sine, sine)
-            return carry
-
-        lax.fori_loop(0, group // step, turn, 0)
-        places = lax.broadcasted_iota(jnp.int32, (8, group), 1)
-        end = jnp.where(places >= border_one, border_two, border_one)
-        end = jnp.where(places >= border_two, group, end)
-        picture = jnp.zeros_like(places)
-        for i in range(starts.shape[1]):
-            first, count = starts[0, i], sizes[0, i]
-            inside = (places >= first) & (places < first + count)
-            picture = jnp.where(inside, jnp.maximum(picture, first + count), picture)
-        low[...] = begin_of(places)
-        high[...] = jnp.maximum(places, jnp.minimum(picture, end) - 1)
-
     if line:
-        line_gather(w_out, wo, lsend, lrecv, llocal, relay)
-    else:
-        keep = pltpu.make_async_copy(w_out, wo.at[0], llocal)
-        keep.start()
-        relay()
-        keep.wait()
-    tables()
+        o_step(2)
+        a_step(1)
+    relay()
+    if line:
+        o_step(3)
+        a_step(2)
+        a_step(3)
+        o_finish()
+        a_finish()
     finish()
+    keep.wait()
+    for copy in wide:
+        copy.wait()
+    unpack()
     for copy in copies:
         copy.wait()
 
 
-def half_gather(n, begin, cot, cg, send, recv, local):
+def half_gather(n, begin, cot, cg, send, recv, local, places, beside):
     at = pl.ds(begin, cot.shape[0] // 2)
     start, relay, finish = gather_parts(n, cot.at[at], cg.at[:, at], send, recv, local)
     step, steps = pl.program_id(0), pl.num_programs(0)
 
     @pl.when(step == 0)
     def _():
-        greet(ring_places(n))
+        greet(places)
         start()
+        beside()
 
     @pl.when(step == steps - 1)
     def _():
@@ -534,7 +516,7 @@
 
 
 def project(n, x_ref, gain_ref, w_ref, gq_ref, gk_ref, cos_ref, sin_ref, cot, n1_ref, qraw_ref, kraw_ref, q_ref, k_ref, v_ref, kt_ref, vt_ref, cg, send, recv, local):
-    finish_half = half_gather(n, 0, cot, cg, send, recv, local)
+    finish_half = half_gather(n, 0, cot, cg, send, recv, local, ring_places(n), lambda: None)
     x = x_ref[...].astype(F32)
     normed = (x * inverse_rms(x) * gain_ref[...]).astype(BF)
     n1_ref[...] = normed.T
@@ -571,8 +553,16 @@
     return jnp.where(fine, 0.0, masked_score)
 
 
-def attend(n, q_ref, k_ref, vt_ref, wo_ref, low_ref, high_ref, cot, cg_half, attn_ref, lse_ref, part_ref, cg, bias, send, recv, local):
-    finish_half = half_gather(n, cot.shape[0] // 2, cot, cg, send, recv, local)
+def attend(n, q_ref, k_ref, vt_ref, wo_ref, low_ref, high_ref, cot, cg_half, wd, attn_ref, lse_ref, part_ref, cg, dn, bias, send, recv, local, wsend, wrecv, wlocal):
+    copies = start_columns(n, [(wd, dn, 0)], wsend, wrecv, wlocal, False)
+
+    def beside():
+        for copy in copies:
+            copy.start()
+
+    finish_half = half_gather(
+        n, cot.shape[0] // 2, cot, cg, send, recv, local, others("seq", n), beside
+    )
     keys = k_ref.shape[0]
     bias[...] = bias_of(low_ref, high_ref, keys)
     heads = q_ref.shape[1] // 128
@@ -595,6 +585,8 @@
     @pl.when(pl.program_id(0) == pl.num_programs(0) - 1)
     def _():
         finish_half()
+        for copy in copies:
+            copy.wait()
 
 
 def middle_stage(n, part, x, gain, x2, n2, slots, stage, own, send, recv, asend, arecv, local):
@@ -627,17 +619,17 @@
 
     gate = dot(n2_ref[...], wg_ref[...])
     up = dot(n2_ref[...], wu_ref[...])
-    gate_ref[...] = gate
-    up_ref[...] = up
-    hidden_ref[...] = (gate * jax.nn.sigmoid(gate) * up).astype(BF)
+    s = jax.nn.sigmoid(gate)
+    silu = gate * s
+    gate_ref[...] = up * (s * (1.0 + gate * (1.0 - s)))
+    up_ref[...] = silu
+    hidden_ref[...] = (silu * up).astype(BF)
 
 
 def ffn_back(cot_ref, wd_ref, gate_ref, up_ref, dgate_ref, dup_ref):
     dh = dot(cot_ref[...], wd_ref[...])
-    gate = gate_ref[...]
-    s = jax.nn.sigmoid(gate)
-    dgate_ref[...] = (dh * up_ref[...] * (s * (1.0 + gate * (1.0 - s)))).astype(BF)
-    dup_ref[...] = (dh * (gate * s)).astype(BF)
+    dgate_ref[...] = (dh * gate_ref[...]).astype(BF)
+    dup_ref[...] = (dh * up_ref[...]).astype(BF)
 
 
 def spread_rows(row, out):
@@ -671,15 +663,20 @@
         copy.start()
     for number in range(width // step):
         weight_load(number).start()
-    for to in order[1:]:
-        for copy in row_loads(to):
-            copy.start()
+    for copy in row_loads(order[1]):
+        copy.start()
     loads = [
         pltpu.make_async_copy(hidden_far, hidden, load.at[0]),
         pltpu.make_async_copy(dn_far, dn, load.at[1]),
     ]
-    for copy in loads:
-        copy.start()
+
+    def others_loads():
+        for to in order[2:]:
+            for copy in row_loads(to):
+                copy.start()
+        for copy in loads:
+            copy.start()
+
     row[...] = jnp.zeros_like(row)
 
     def block(to, first=False):
@@ -719,15 +716,16 @@
     send_on, pass_on, end = gather_parts(n, own, dz, asend, arecv, local)
     if n == 4:
         block(corner, True)
-        start(0, 2)
+        start(0, 1)
+        others_loads()
         block(across)
-        start(2, 3)
         block(along)
-        start(3, 4)
+        start(3)
         relay()
         block(me)
     else:
         block(order[0], True)
+        others_loads()
         for to in order[1:]:
             block(to)
         start()
@@ -744,14 +742,14 @@
     end()
 
 
-def attend_back(n, q_ref, qraw_ref, k_ref, kt_ref, v_ref, kraw_ref, dz_ref, wo_ref, lse_ref, low_ref, high_ref, cq_ref, sq_ref, ck_ref, sk_ref, gq_ref, gk_ref, attn_ref, part, dq_ref, dk_ref, dv_ref, dgq_ref, dgk_ref, out, grads, dk_sum, dv_sum, slots, stage, send, recv, wo_sum, both, got, done, tsend, trecv, put):
+def attend_back(n, q_ref, qraw_ref, k_ref, kt_ref, v_ref, kraw_ref, dz_ref, wo_ref, lse_ref, low_ref, high_ref, cq_ref, sq_ref, ck_ref, sk_ref, gq_ref, gk_ref, attn_ref, part, x2, dq_ref, dk_ref, dv_ref, dgq_ref, dgk_ref, out, grads, dk_sum, dv_sum, slots, stage, send, recv, wo_sum, both, got, done, tsend, trecv, put):
     kv, block = pl.program_id(0), pl.program_id(1)
     keys = k_ref.shape[0]
     ratio = q_ref.shape[1] // 128
     scale = 128 ** (-0.5)
 
     def finish(at, total):
-        out[at] = total
+        out[at] = (x2[at] + total).astype(BF)
 
     start, relay, lower, upper = scatter_parts(n, part, slots, stage, send, recv, finish)
     core = lax.rem(lax.axis_index("fsdp"), 2)
@@ -942,13 +940,33 @@
         copy.wait()
 
 
-def widen(pieces, *refs):
-    ins, outs = refs[: -len(pieces)], refs[-len(pieces) :]
-    for out, (i, begin, count) in zip(outs, pieces):
-        out[...] = ins[i][0, :, begin : begin + count].astype(F32)
-
-
-def last_stage(n, nf, dq, dk, dv, w, x, gain, gu, two, gq, gk, out, gu_out, gains, part, slots, stage, send, recv, row, small, wide, mid, seen, esend, erecv, local, gsend, grecv):
+def write_out(nf, own_gain, own_head, y, dx, gains, att, o, gu, dn, out, dx_out, g_one, q_out, k_out, v_out, g_q, g_k, o_out, g_two, gate_out, up_out, down_out):
+    out[...] = y[...]
+    dx_out[...] = dx[...]
+    qw, kw = q_out.shape[1], k_out.shape[1]
+    q_out[...] = att[0, :, :qw].astype(F32)
+    k_out[...] = att[0, :, qw : qw + kw].astype(F32)
+    v_out[...] = att[0, :, qw + kw :].astype(F32)
+    o_out[...] = o[0].astype(F32)
+    units = gate_out.shape[1]
+    gate_out[...] = gu[0, :, :units].astype(F32)
+    up_out[...] = gu[0, :, units:].astype(F32)
+    down_out[...] = dn[0].astype(F32)
+
+    @pl.when(pl.program_id(0) == 0)
+    def _():
+        spot = lax.axis_index("fsdp")
+        owner = lax.axis_index("seq") * nf + spot
+        begin = lax.rem(spot, 128 // own_gain) * own_gain
+        wide = pltpu.roll(gains[...], lax.rem(128 - begin, 128), 1)
+        g_one[...] = wide[0:1, :own_gain]
+        g_two[...] = wide[1:2, :own_gain]
+        heads = pltpu.roll(gains[...], lax.rem(128 - owner * own_head, 128), 1)
+        g_q[...] = heads[2:3, :own_head]
+        g_k[...] = heads[3:4, :own_head]
+
+
+def last_stage(n, nf, dq, dk, dv, w, x, dx2, gain, gu, two, gq, gk, out, gu_out, gains, part, slots, stage, send, recv, row, small, wide, mid, seen, esend, erecv, local, gsend, grecv):
     me, spot = lax.axis_index("seq"), lax.axis_index("fsdp")
     greet(others("seq", n) + others("fsdp", nf))
     row[...] = jnp.zeros_like(row)
@@ -971,7 +989,7 @@
 
     def finish(at, total):
         back, dg = norm_back(x[at].astype(F32), gain[...], total)
-        out[at] = back
+        out[at] = (dx2[at] + back).astype(BF)
         row[...] += dg
 
     start, relay, lower, upper = scatter_parts(n, part, slots, stage, send, recv, finish)
@@ -979,11 +997,10 @@
     if n == 4:
         across, along, corner = square(me)
         block(corner)
-        start(0, 2)
+        start(0, 1)
         block(across)
-        start(2, 3)
         block(along)
-        start(3, 4)
+        start(3)
         relay()
         for copy in exchanges:
             copy.start()
@@ -1079,63 +1096,25 @@
     own_gain = norm1_gain.shape[0]
     own_head = q_gain.shape[0]
 
-    spot = lax.axis_index("fsdp")
-    owner = lax.axis_index("seq") * nf + spot
-    lanes = jnp.arange(128, dtype=jnp.int32)[None, :]
-
-    def placed(gain, mine):
-        count = gain.shape[0]
-        wide = jnp.tile(gain.astype(F32), 128 // count)[None, :]
-        return jnp.where(lax.div(lanes, count) == mine, wide, 0.0)
-
-    sharing = 128 // own_gain
-    packed = jnp.concatenate(
-        [
-            placed(norm1_gain, lax.rem(spot, sharing)),
-            placed(norm2_gain, lax.rem(spot, sharing)),
-            placed(q_gain, owner),
-            placed(k_gain, owner),
-            jnp.zeros((4, 128), F32),
-        ],
-        axis=0,
-    )
-    w_att = pl.pallas_call(
-        functools.partial(attention_weights_out, n),
-        out_shape=shape((n, depth, cw), BF),
-        in_specs=[ANY] * 3,
-        out_specs=ANY,
-        scratch_shapes=[dma(3 * (n - 1)), dma(3 * (n - 1)), dma(3)],
-        compiler_params=comm_params(0),
-    )(w_query, w_key, w_value)
-    gu, all_gains = pl.pallas_call(
-        functools.partial(gate_up_out, n, nf),
-        out_shape=(shape((n, depth, 2 * fw), BF), shape((nf, n, 8, 128), F32)),
-        in_specs=[ANY] * 3,
-        out_specs=(ANY, ANY),
-        scratch_shapes=[
-            pltpu.VMEM((n, 8, 128), F32),
-            dma(2 * (n - 1)),
-            dma(2 * (n - 1)),
-            dma(2),
-            dma(n + nf - 2),
-            dma(n + nf - 2),
-            dma(2),
-        ],
-        compiler_params=comm_params(8),
-    )(after(w_gate, w_att), w_up, packed)
+    entries = []
+    for gain in (norm1_gain, norm2_gain, q_gain, k_gain):
+        entries += [gain, jnp.zeros((128 - gain.shape[0],), BF)]
+    packed = jnp.concatenate(entries).astype(F32)[None, :]
+
     gather_sems = [dma(gather_copies(n)), dma(gather_copies(n)), pltpu.SemaphoreType.DMA]
     line = nf == 8
-    w_att = lax.all_gather(w_att, "fsdp", axis=1, tiled=True).reshape(width, cw)
     half = head // 2
     powers = -(np.arange(half, dtype=np.float32) * np.float32(2.0) / np.float32(head))
     freq = np.tile((np.float32(theta) ** powers).astype(np.float32), 2)[None, :]
     small = pl.BlockSpec(memory_space=pltpu.SMEM)
-    xg, dn, wo, gain_one, gain_two, gain_q, gain_k, cos, sin, low, high = pl.pallas_call(
-        functools.partial(entry_stage, n, nf, line, own_gain),
+    held = nf if line else 1
+    w_att, gu, xg, wo, gain_one, gain_two, gain_q, gain_k, cos, sin, low, high = pl.pallas_call(
+        functools.partial(entry_stage, n, nf, line, own_gain, own_head),
         out_shape=(
+            shape((n, held, depth, cw), BF),
+            shape((n, depth, 2 * fw), BF),
             shape((n, rows, width), BF),
-            shape((n, depth, fw), BF),
-            shape((nf if line else 1, depth, width), BF),
+            shape((held, depth, width), BF),
             shape((1, width), F32),
             shape((1, width), F32),
             shape((1, head), F32),
@@ -1145,17 +1124,42 @@
             shape((8, group), jnp.int32),
             shape((8, group), jnp.int32),
         ),
-        in_specs=[ANY] * 3 + [VMEM] + [small] * 3 + [VMEM],
-        out_specs=(ANY,) * 3 + (VMEM,) * 8,
-        scratch_shapes=gather_sems
-        + [dma(n - 1), dma(n - 1), dma(1), dma(10), dma(10), pltpu.SemaphoreType.DMA],
-        compiler_params=comm_params(1),
-    )(after(tokens, gu), w_down.T, w_out, all_gains, seq_lengths, pic_starts, pic_lengths, jnp.asarray(freq))
+        in_specs=[ANY] * 7 + [VMEM] + [small] * 3 + [VMEM],
+        out_specs=(ANY,) * 4 + (VMEM,) * 8,
+        scratch_shapes=[
+            pltpu.VMEM((8, 128), F32),
+            pltpu.VMEM((n, 8, 128), F32),
+            pltpu.VMEM((nf, n, 8, 128), F32),
+            dma(3 * (n - 1)),
+            dma(3 * (n - 1)),
+            dma(3),
+            dma(2 * (n - 1)),
+            dma(2 * (n - 1)),
+            dma(2),
+        ]
+        + gather_sems
+        + [
+            dma(n + nf - 2),
+            dma(n + nf - 2),
+            dma(2),
+            dma(10),
+            dma(10),
+            dma(10),
+            dma(10),
+            pltpu.SemaphoreType.DMA,
+        ],
+        compiler_params=comm_params(0),
+    )(
+        w_query, w_key, w_value, w_gate, w_up, tokens, w_out, packed,
+        seq_lengths, pic_starts, pic_lengths, jnp.asarray(freq),
+    )
     wo = wo.reshape(-1, width)
+    w_att = w_att.reshape(n, -1, cw)
     if not line:
         wo = lax.all_gather(wo, "fsdp", axis=0, tiled=True)
+        w_att = lax.all_gather(w_att, "fsdp", axis=1, tiled=True)
+    w_att = w_att.reshape(width, cw)
     gu = lax.all_gather(gu, "fsdp", axis=1, tiled=True).reshape(width, 2 * fw)
-    dn = lax.all_gather(dn, "fsdp", axis=1, tiled=True).reshape(width, fw)
 
     def whole(dims):
         return pl.BlockSpec(dims, lambda *ids: (0,) * len(dims))
@@ -1206,7 +1210,7 @@
         compiler_params=comm_params(11),
     )(xg.reshape(group, width), gain_one, w_att, gain_q, gain_k, cos, sin, cotangent)
 
-    attn, lse, part_out, cg = pl.pallas_call(
+    attn, lse, part_out, cg, dn = pl.pallas_call(
         functools.partial(attend, n),
         grid=(blocks,),
         out_shape=(
@@ -1214,6 +1218,7 @@
             shape((8, group), F32),
             shape((group, width), BF),
             shape((n, rows, width), BF),
+            shape((n, depth, fw), BF),
         ),
         in_specs=[
             by_rows(256, qw),
@@ -1224,13 +1229,17 @@
             by_cols(8, 256),
             ANY,
             ANY,
+            ANY,
         ],
-        out_specs=(by_rows(256, qw), by_cols(8, 256), by_rows(256, width), ANY),
-        scratch_shapes=[pltpu.VMEM((group, 256), F32)] + gather_sems,
+        out_specs=(by_rows(256, qw), by_cols(8, 256), by_rows(256, width), ANY, ANY),
+        scratch_shapes=[pltpu.VMEM((group, 256), F32)]
+        + gather_sems
+        + [dma(n - 1), dma(n - 1), dma(1)],
         input_output_aliases={7: 3},
         compiler_params=comm_params(3),
-    )(q, k, vt, wo, low, high, cotangent, cg)
+    )(q, k, vt, wo, low, high, cotangent, cg, w_down.T)
     cg = cg.reshape(group, width)
+    dn = lax.all_gather(dn, "fsdp", axis=1, tiled=True).reshape(width, fw)
 
     slots = [
         pltpu.VMEM((scatter_slots(n), rows, width), BF),
@@ -1381,7 +1390,7 @@
             shape((group, kw), BF),
             shape((8, head), F32),
             shape((8, head), F32),
-            shape((rows, width), F32),
+            shape((rows, width), BF),
             shape((n + width // cw, width // n // 2, cw), BF),
         ),
         in_specs=[
@@ -1403,6 +1412,7 @@
             whole((1, head)),
             whole((1, head)),
             pl.BlockSpec((256, wide), lambda h, b: (b, h)),
+            VMEM,
             VMEM,
         ],
         out_specs=(
@@ -1429,23 +1439,22 @@
         compiler_params=comm_params(5),
     )(
         q, qraw, k, kt, v, kraw, dz, wo, lse, low, high, cos, sin, cos, sin, gain_q, gain_k,
-        attn, part_y,
+        attn, part_y, x2,
     )
-    output = (x2 + branch).astype(BF)
 
     att_grad, dn_mine = product(
         15, n1, dq, dk, dv, into=wo_grad, flipped=True, given=dn_share
     )
     att_share = reduce_rows(after(att_grad, gu_share))
 
-    back_one, gu_mine, gains = pl.pallas_call(
+    input_raw, gu_mine, gains = pl.pallas_call(
         functools.partial(last_stage, n, nf),
         out_shape=(
-            shape((rows, width), F32),
+            shape((rows, width), BF),
             shape(gu_share.shape, BF),
             shape((8, 128), F32),
         ),
-        in_specs=[VMEM] * 6 + [ANY] + [VMEM] * 3,
+        in_specs=[VMEM] * 7 + [ANY] + [VMEM] * 3,
         out_specs=(VMEM, ANY, VMEM),
         scratch_shapes=[pltpu.VMEM((n, rows, width), BF)]
         + slots
@@ -1464,39 +1473,9 @@
         ],
         compiler_params=comm_params(7),
     )(
-        after(dq, att_grad), dk, dv, w_att, tokens, gain_one, gu_share,
+        after(dq, att_grad), dk, dv, w_att, tokens, dx2, gain_one, gu_share,
         dgain_two, dgain_q, dgain_k,
     )
-    input_grad = (dx2 + back_one).astype(BF)
-
-    def owned(row, count, mine):
-        return lax.dynamic_slice_in_dim(row, mine * count, count, 0)
-
-    gain_grads = (
-        owned(gains[0], own_gain, lax.rem(spot, sharing)),
-        owned(gains[1], own_gain, lax.rem(spot, sharing)),
-        owned(gains[2], own_head, owner),
-        owned(gains[3], own_head, owner),
-    )
-
-    def spread(arrays, pieces):
-        ins = [pl.BlockSpec((1, depth, a.shape[2]), lambda i: (i, 0, 0)) for a in arrays]
-        outs = [by_cols(depth, count) for _, _, count in pieces]
-        shapes = [shape((depth, n * count), F32) for _, _, count in pieces]
-        return pl.pallas_call(
-            functools.partial(widen, pieces),
-            grid=(n,),
-            out_shape=tuple(shapes),
-            in_specs=ins,
-            out_specs=tuple(outs),
-            compiler_params=plain_params(),
-        )(*arrays)
-
-    gate_grad, up_grad, down_grad = spread(
-        [gu_mine, dn_mine], [(0, 0, fw), (0, fw, fw), (1, 0, fw)]
-    )
-    wide_grads = (gate_grad, up_grad, down_grad.T)
-    wo_out = att_share[n:].transpose(1, 0, 2).reshape(depth, width).astype(F32)
     att_mine = pl.pallas_call(
         functools.partial(exchange, n),
         out_shape=shape((n, depth, cw), BF),
@@ -1504,23 +1483,61 @@
         out_specs=ANY,
         scratch_shapes=[dma(n - 1), dma(n - 1), dma(1)],
         compiler_params=comm_params(9),
-    )(after(att_share, (gain_grads, wide_grads, input_grad, output)))
-    wq_grad, wk_grad, wv_grad = spread(
-        [att_mine], [(0, 0, qw), (0, qw, kw), (0, qw + kw, kw)]
-    )
-
-    return (
-        output,
-        input_grad,
-        gain_grads[0],
-        wq_grad,
-        wk_grad,
-        wv_grad,
-        gain_grads[2],
-        gain_grads[3],
-        wo_out,
-        gain_grads[1],
-    ) + wide_grads
+    )(after(att_share, gains))
+
+    def slab(count):
+        return pl.BlockSpec((1, depth, count), lambda i: (i, 0, 0))
+
+    each = width // n
+    per = cw // each
+    results = pl.pallas_call(
+        functools.partial(write_out, nf, own_gain, own_head),
+        grid=(n,),
+        out_shape=(
+            shape((rows, width), BF),
+            shape((rows, width), BF),
+            shape((1, own_gain), F32),
+            shape(w_query.shape, F32),
+            shape(w_key.shape, F32),
+            shape(w_value.shape, F32),
+            shape((1, own_head), F32),
+            shape((1, own_head), F32),
+            shape(w_out.shape, F32),
+            shape((1, own_gain), F32),
+            shape(w_gate.shape, F32),
+            shape(w_up.shape, F32),
+            shape(w_gate.shape, F32),
+        ),
+        in_specs=[
+            by_rows(rows // n, width),
+            by_rows(rows // n, width),
+            whole((8, 128)),
+            slab(cw),
+            pl.BlockSpec(
+                (1, depth, each), lambda i: (n + lax.div(i, per), 0, lax.rem(i, per))
+            ),
+            slab(2 * fw),
+            slab(fw),
+        ],
+        out_specs=(
+            by_rows(rows // n, width),
+            by_rows(rows // n, width),
+            whole((1, own_gain)),
+            by_cols(depth, qw),
+            by_cols(depth, kw),
+            by_cols(depth, kw),
+            whole((1, own_head)),
+            whole((1, own_head)),
+            by_cols(depth, each),
+            whole((1, own_gain)),
+            by_cols(depth, fw),
+            by_cols(depth, fw),
+            by_cols(depth, fw),
+        ),
+        compiler_params=plain_params(),
+    )(branch, input_raw, gains, att_mine, att_share, gu_mine, dn_mine)
+    flat = [r.reshape(-1) if i in (2, 6, 7, 9) else r for i, r in enumerate(results)]
+    return tuple(flat[:-1]) + (flat[-1].T,)
 
 
 def solution(mesh):

time: 541 us -> 523 us (0.967)
  Pallas kernels: 503 us -> 491 us
  waiting for transfers between devices: 5.98 us -> 15.5 us
  local copies, waits for them, and re-layouts: 9.12 us -> 0.81 us
  other arithmetic: 6.63 us -> 0.58 us
    pallas_call x5 -> x2, Pallas kernels: 95.5 us -> 75.5 us  [the longest x1 69.3 us: shards(): pl.pallas_call(functools.partial(entry_stage, n, nf, line, own_gain, own_...]
    all_gather x1, waiting for transfers between devices: 5.8 us -> 15.3 us  [shards(): dn = lax.all_gather(dn, 'fsdp', axis=1, tiled=True).reshape(width, fw)]
    pallas_call x1, Pallas kernels: 21.7 us -> 30.6 us  [shards(): pl.pallas_call(functools.partial(attend, n), grid=(blocks,), out_shape=(s...]
  transfers between devices with their start and end apart: 6 -> 5, of which waited for: 1 -> 1; matrix products, arithmetic and copies ran while one was open for 2% -> 0% of each run, Pallas kernels for 89% -> 78%
where the time goes in v5:
time: 523 us; the launch traced here: 522 us
  Pallas kernels  491 us (94%)
  waiting for transfers between devices  15.5 us (3%)
  between operations  13.9 us (3%)
    pallas_call x1, Pallas kernels, shards(): pl.pallas_call(functools.partial(back_stage, n), out_shape=(shape((rows,...  83.9 us
    pallas_call x1, Pallas kernels, shards(): pl.pallas_call(functools.partial(middle_stage, n), out_shape=(shape((rows...  73 us
    pallas_call x1, Pallas kernels, shards(): pl.pallas_call(functools.partial(entry_stage, n, nf, line, own_gain, own_...  69.3 us
    pallas_call x1, Pallas kernels, shards(): pl.pallas_call(functools.partial(last_stage, n, nf), out_shape=(shape((ro...  63.9 us
    pallas_call x3, Pallas kernels, product(): pl.pallas_call(functools.partial(gradient, n, counts, len(kept), flipped,...  52.5 us
    pallas_call x1, Pallas kernels, shards(): pl.pallas_call(functools.partial(attend_back, n), grid=(kheads, blocks),...  44.3 us
    pallas_call x1, Pallas kernels, shards(): pl.pallas_call(functools.partial(attend, n), grid=(blocks,), out_shape=(s...  30.6 us
    pallas_call x1, Pallas kernels, shards(): pl.pallas_call(functools.partial(project, n), grid=(blocks,), out_shape=(...  23.9 us
  transfers between devices with their start and end apart: 5, of which 1 were waited for; matrix products, arithmetic and copies ran while one was open for 0% of the time, Pallas kernels for 78%

profile of v5, /device:TPU:0, one launch (start us, length us, event | category | flops | bytes accessed | tf_op | source)
XLA Modules:
  0.0 522.5 jit_solution(12823877679145193465)
XLA Ops:
  7.2 0.0 all-gather.5.cloned.1.call-start
  7.2 0.8 concatenate.28
  8.0 0.6 convert_element_type.10.raw
  8.6 69.3 %shard_map.264 = (bf16[4,8,64,1024]{3,2,1,0:T(8,128)(2,1)}, bf16[4,64,3072]{2,1,0:T(8,128)(2,1)}, bf16[4,256,2048]{2,1,0:T(8,128)(2,1)}, bf16[8,64,2048]{2,1,0:T...) custom-call(bf16[64,2048]{1,0:T(8,128)(2,1)} %wq.1, ...), custom_call_target="tpu_custom_call" | custom-call | tf_op jit(solution)/shard_map/pallas_call | solution.py:1111
  78.0 0.0 all-gather.5.cloned.1.call-update
  78.0 0.0 all-gather.3.cloned.1.call-start
  78.0 23.9 %shard_map.265 = (bf16[2048,1024]{1,0:T(8,128)(2,1)}, f32[1024,512]{1,0:T(8,128)}, f32[1024,256]{1,0:T(8,128)}, bf16[1024,512]{1,0:T(8,128)(2,1)}, bf16[1024,256...) custom-call(bf16[1024,2048]{1,0:T(8,128)(2,1)} %bitcast.32, ...), custom_call_target="tpu_custom_call" | custom-call | tf_op jit(solution)/shard_map/pallas_call | solution.py:1174
  102.0 30.6 %shard_map.266 = (bf16[1024,512]{1,0:T(8,128)(2,1)}, f32[8,1024]{1,0:T(8,128)}, bf16[1024,2048]{1,0:T(8,128)(2,1)}, bf16[4,256,2048]{2,1,0:T(8,128)(2,1)}, bf16[4,64,1536]{2,1,0:T(8,128)(2,1)}) custom-call(bf16[1024,512]{1,0:T(8,128)(2,1)} %get-tuple-element.88.q_ref, bf16[1024,256]{1,0:T(8,128)(2,1)} %get-tuple-element.90.k_ref, ...), custom_call_target="tpu_custom_call", output_to_operand_aliasing={{3}: (7, {})} | custom-call | tf_op jit(solution)/shard_map/pallas_call | solution.py:1213
  132.6 0.0 all-gather.3.cloned.1.call-update
  132.7 0.2 reduce-scatter.4.cloned.1.call-start
  132.9 73.0 %shard_map.267 = (f32[256,2048]{1,0:T(8,128)}, bf16[4,256,2048]{2,1,0:T(8,128)(2,1)}) custom-call(bf16[4,256,2048]{2,1,0:T(8,128)(2,1)} %bitcast.31, bf16[256,2048]{1,0:T(8,128)(2,1)} %x.5, f32[1,2048]{1,0:T(1,128)} %get-tuple-element.102.gain), custom_call_target="tpu_custom_call" | custom-call | tf_op jit(solution)/shard_map/pallas_call | solution.py:1250
  205.9 0.0 all-gather.5.cloned.1.call-done
  205.9 20.8 %shard_map.268 = (f32[1024,1536]{1,0:T(8,128)}, f32[1024,1536]{1,0:T(8,128)}, bf16[1024,1536]{1,0:T(8,128)(2,1)}, bf16[2048,1024]{1,0:T(8,128)(2,1)}) custom-call(bf16[1024,2048]{1,0:T(8,128)(2,1)} %bitcast.30, bf16[2048,3072]{1,0:T(8,128)(2,1)} %bitcast.19, bf16[2048,3072]{1,0:T(8,128)(2,1)} %bitcast.20), custom_call_target="tpu_custom_call" | custom-call | tf_op jit(solution)/shard_map/pallas_call | solution.py:1265
  226.8 15.2 %shard_map.269 = bf16[4,256,1536]{2,1,0:T(8,128)(2,1)} custom-call(bf16[1024,2048]{1,0:T(8,128)(2,1)} %bitcast.22, bf16[1024,1536]{1,0:T(8,128)(2,1)} %get-tuple-element.105.refs_1_.hidden_far), custom_call_target="tpu_custom_call" | custom-call | tf_op jit(solution)/shard_map/pallas_call | solution.py:1303
  242.0 0.0 reduce-scatter.4.cloned.1.call-update
  242.0 0.0 reduce-scatter.6.cloned.1.call-start
  242.1 15.3 %all-gather.3.cloned.1.call-done = bf16[4,512,1536]{2,1,0:T(8,128)(2,1)} async-done(((bf16[4,64,1536]{2,1,0:T(8,128)(2,1)}), bf16[4,512,1536]{2,1,0:T(8,128)(2,1)}) %all-gather.3.cloned.1.call-update) | async-done | bytes 6291472 | tf_op jit(solution)/shard_map/all_gather | solution.py:1242
  257.4 15.0 %shard_map.270 = (bf16[1024,1536]{1,0:T(8,128)(2,1)}, bf16[1024,1536]{1,0:T(8,128)(2,1)}) custom-call(bf16[1024,2048]{1,0:T(8,128)(2,1)} %bitcast.23, bf16[2048,1536]{1,0:T(8,128)(2,1)} %bitcast.24, f32[1024,1536]{1,0:T(8,128)} %get-tuple-element.107.gate_ref, f32[1024,1536]{1,0:T(8,128)} %get-tuple-element.108.up_ref), custom_call_target="tpu_custom_call" | custom-call | tf_op jit(solution)/shard_map/pallas_call | solution.py:1334
  272.3 22.3 %shard_map.271 = bf16[4,256,3072]{2,1,0:T(8,128)(2,1)} custom-call(bf16[2048,1024]{1,0:T(8,128)(2,1)} %get-tuple-element.110.refs_0_, bf16[1024,1536]{1,0:T(8,128)(2,1)} %get-tuple-element.112.refs_1_.dgate_far, bf16[1024,1536]{1,0:T(8,128)(2,1)} %get-tuple-element.111.refs_2_.dup_far), custom_call_target="tpu_custom_call" | custom-call | tf_op jit(solution)/shard_map/pallas_call | solution.py:1303
  294.7 0.0 reduce-scatter.6.cloned.1.call-update
  294.7 0.3 reduce-scatter.8.cloned.1.call-start
  295.0 83.9 %shard_map.272 = (f32[256,2048]{1,0:T(8,128)}, bf16[4,256,2048]{2,1,0:T(8,128)(2,1)}, f32[16,128]{1,0:T(8,128)}, bf16[4,256,2048]{2,1,0:T(8,128)(2,1)}) custom-call(bf16[1024,1536]{1,0:T(8,128)(2,1)} %get-tuple-element.112.refs_1_.dgate_far, bf16[1024,1536]{1,0:T(8,128)(2,1)} %get-tuple-element.111.refs_2_.dup_far, bf16[2048,3072]{1,0:T(8,128)(2,1)} %bitcast.21, ...), custom_call_target="tpu_custom_call" | custom-call | tf_op jit(solution)/shard_map/pallas_call | solution.py:1351
  378.9 44.3 %shard_map.273 = (bf16[1024,512]{1,0:T(8,128)(2,1)}, bf16[1024,256]{1,0:T(8,128)(2,1)}, bf16[1024,256]{1,0:T(8,128)(2,1)}, f32[8,128]{1,0:T(8,128)}, f32[8,128]{...) custom-call(bf16[1024,512]{1,0:T(8,128)(2,1)} %get-tuple-element.88.q_ref, ...), custom_call_target="tpu_custom_call" | custom-call | tf_op jit(solution)/shard_map/pallas_call | solution.py:1384
  423.2 0.0 reduce-scatter.4.cloned.1.call-done.refs_5_
  423.2 15.0 %shard_map.274 = (bf16[6,256,1024]{2,1,0:T(8,128)(2,1)}, bf16[4,64,1536]{2,1,0:T(8,128)(2,1)}) custom-call(bf16[2048,1024]{1,0:T(8,128)(2,1)} %get-tuple-element.120.refs_0_, bf16[1024,512]{1,0:T(8,128)(2,1)} %get-tuple-element.125.refs_1_.dq, bf16[1024,256]{1,0:T(8,128)(2,1)} %get-tuple-element.121.refs_2_.dk, ...), custom_call_target="tpu_custom_call", output_to_operand_aliasing={{0}: (4, {})} | custom-call | tf_op jit(solution)/shard_map/pallas_call | solution.py:1303
  438.2 0.0 reduce-scatter.6.cloned.1.call-done.gu
  438.2 0.0 reduce-scatter.8.cloned.1.call-update
  438.3 63.9 %shard_map.275 = (bf16[256,2048]{1,0:T(8,128)(2,1)}, bf16[4,64,3072]{2,1,0:T(8,128)(2,1)}, f32[8,128]{1,0:T(8,128)}) custom-call(bf16[1024,512]{1,0:T(8,128)(2,1)} %get-tuple-element.125.refs_1_.dq, bf16[1024,256]{1,0:T(8,128)(2,1)} %get-tuple-element.121.refs_2_.dk, bf16[1024,256]{1,0:T(8,128)(2,1)} %get-tuple-element.122.refs_3_.dv, ...), custom_call_target="tpu_custom_call" | custom-call | tf_op jit(solution)/shard_map/pallas_call | solution.py:1450
  502.1 0.0 reduce-scatter.8.cloned.1.call-done.source.o
  502.2 7.5 %shard_map.276.att = bf16[4,64,1024]{2,1,0:T(8,128)(2,1)} custom-call(bf16[6,64,1024]{2,1,0:T(8,128)(2,1)} %reduce-scatter.8.cloned.1.call-done.source.o), custom_call_target="tpu_custom_call" | custom-call | tf_op jit(solution)/shard_map/pallas_call | solution.py:1479
  509.7 6.2 %shard_map.277 = (bf16[256,2048]{1,0:T(8,128)(2,1)}, bf16[256,2048]{1,0:T(8,128)(2,1)}, f32[1,64]{1,0:T(1,128)}, f32[64,2048]{1,0:T(8,128)}, f32[64,1024]{1,0:T(...) custom-call(bf16[256,2048]{1,0:T(8,128)(2,1)} %get-tuple-element.118, ...), custom_call_target="tpu_custom_call" | custom-call | tf_op jit(solution)/shard_map/pallas_call | solution.py:1493
  (2 shorter events, 0.0 us)
Async XLA Ops:
  7.2 198.7 %all-gather.5.cloned.1.call-start = ((), (), s32[]{:S(2)}) async-start(), calls=%async_computation.4 | async-start | bytes 14155776 | tf_op jit(solution)/shard_map/all_gather | solution.py:1162
  78.0 179.4 %all-gather.3.cloned.1.call-start = ((), (), s32[]{:S(2)}) async-start(), calls=%async_computation.3 | async-start | bytes 7077888 | tf_op jit(solution)/shard_map/all_gather | solution.py:1242
  132.7 290.5 %reduce-scatter.4.cloned.1.call-start = ((), (), s32[]{:S(2)}) async-start(), calls=%async_computation.5 | async-start | bytes 3932160 | tf_op jit(solution)/shard_map/reduce_scatter | solution.py:1327
  242.0 196.2 %reduce-scatter.6.cloned.1.call-start = ((), (), s32[]{:S(2)}) async-start(), calls=%async_computation.6 | async-start | bytes 7864320 | tf_op jit(solution)/shard_map/reduce_scatter | solution.py:1327
  294.7 207.5 %reduce-scatter.8.cloned.1.call-start = ((), (), s32[]{:S(2)}) async-start(), calls=%async_computation.7 | async-start | bytes 3932160 | tf_op jit(solution)/shard_map/reduce_scatter | solution.py:1327
Sparse Core Ops, SparseCore 0:
  78.1 114.6 all-gather.4
  194.4 62.8 all-gather.2
  259.7 58.9 reduce-scatter.3
  320.8 110.7 reduce-scatter.5
  438.4 60.9 reduce-scatter.7

commit v6 on v5

--- a/solution.py
+++ b/solution.py
@@ -135,24 +135,11 @@
     return start, relay, finish
 
 
-def gather(n, own, out, send, recv, local):
-    for part in gather_parts(n, own, out, send, recv, local):
-        part()
-
-
 def scatter_slots(n):
     return 4 if n == 4 else n - 1
 
 
-def scatter_sum(n, part, slots, stage, send, recv, finish):
-    start, relay, lower, upper = scatter_parts(n, part, slots, stage, send, recv, finish)
-    start()
-    relay()
-    lower()
-    upper()
-
-
-def scatter_parts(n, part, slots, stage, send, recv, finish):
+def scatter_parts(n, part, slots, stage, send, recv, finish, held=False):
     me = lax.axis_index("seq")
     rows = part.shape[1]
     half = rows // 2
@@ -180,7 +167,7 @@
     ]
 
     def start(*chosen):
-        chosen = chosen if chosen else (0, 1, 3)
+        chosen = chosen if chosen else (0, 1, 3) if held else (0, 1, 2, 3)
         for copy in [copies[i] for i in chosen] if n == 4 else copies:
             copy.start()
 
@@ -189,7 +176,8 @@
             copies[0].wait_recv()
             stage[low] = (part[across, low].astype(F32) + slots[2, low].astype(F32)).astype(BF)
             copies[4].start()
-            copies[2].start()
+            if held:
+                copies[2].start()
             copies[1].wait_recv()
             stage[high] = (part[along, high].astype(F32) + slots[2, high].astype(F32)).astype(BF)
             copies[5].start()
@@ -597,7 +585,7 @@
         x2[at] = value
         own[at] = (value * inverse_rms(value) * gain[...]).astype(BF)
 
-    start, relay, lower, upper = scatter_parts(n, part, slots, stage, send, recv, finish)
+    start, relay, lower, upper = scatter_parts(n, part, slots, stage, send, recv, finish, True)
     send_on, pass_on, end = gather_parts(n, own, n2, asend, arecv, local)
     start()
     relay()
@@ -712,7 +700,7 @@
         own[at] = value.astype(BF)
         row[...] += dg
 
-    start, relay, lower, upper = scatter_parts(n, part, slots, stage, send, recv, finish)
+    start, relay, lower, upper = scatter_parts(n, part, slots, stage, send, recv, finish, True)
     send_on, pass_on, end = gather_parts(n, own, dz, asend, arecv, local)
     if n == 4:
         block(corner, True)
@@ -771,7 +759,7 @@
         dgq_ref[...] = jnp.zeros_like(dgq_ref)
         dgk_ref[...] = jnp.zeros_like(dgk_ref)
 
-    @pl.when(step == steps // 2)
+    @pl.when(step == steps * 3 // 8)
     def _():
         relay()
 
@@ -999,6 +987,7 @@
         block(corner)
         start(0, 1)
         block(across)
+        start(2)
         block(along)
         start(3)
         relay()

time: 523 us -> 521 us (level)
  no operation moved by 1% of the time
where the time goes in v6:
time: 521 us; the launch traced here: 520 us
  Pallas kernels  489 us (94%)
  waiting for transfers between devices  15.5 us (3%)
  between operations  13.9 us (3%)
    pallas_call x1, Pallas kernels, shards(): pl.pallas_call(functools.partial(back_stage, n), out_shape=(shape((rows,...  83.9 us
    pallas_call x1, Pallas kernels, shards(): pl.pallas_call(functools.partial(middle_stage, n), out_shape=(shape((rows...  73 us
    pallas_call x1, Pallas kernels, shards(): pl.pallas_call(functools.partial(entry_stage, n, nf, line, own_gain, own_...  69.3 us
    pallas_call x1, Pallas kernels, shards(): pl.pallas_call(functools.partial(last_stage, n, nf), out_shape=(shape((ro...  62.3 us
    pallas_call x3, Pallas kernels, product(): pl.pallas_call(functools.partial(gradient, n, counts, len(kept), flipped,...  52.4 us
    pallas_call x1, Pallas kernels, shards(): pl.pallas_call(functools.partial(attend_back, n), grid=(kheads, blocks),...  43 us
    pallas_call x1, Pallas kernels, shards(): pl.pallas_call(functools.partial(attend, n), grid=(blocks,), out_shape=(s...  30.6 us
    pallas_call x1, Pallas kernels, shards(): pl.pallas_call(functools.partial(project, n), grid=(blocks,), out_shape=(...  23.9 us
  transfers between devices with their start and end apart: 5, of which 1 were waited for; matrix products, arithmetic and copies ran while one was open for 0% of the time, Pallas kernels for 78%

profile of v6, /device:TPU:0, one launch (start us, length us, event | category | flops | bytes accessed | tf_op | source)
XLA Modules:
  0.0 520.5 jit_solution(10869622941001473081)
XLA Ops:
  7.2 0.0 all-gather.5.cloned.1.call-start
  7.2 0.8 concatenate.28
  8.0 0.6 convert_element_type.10.raw
  8.6 69.3 %shard_map.264 = (bf16[4,8,64,1024]{3,2,1,0:T(8,128)(2,1)}, bf16[4,64,3072]{2,1,0:T(8,128)(2,1)}, bf16[4,256,2048]{2,1,0:T(8,128)(2,1)}, bf16[8,64,2048]{2,1,0:T...) custom-call(bf16[64,2048]{1,0:T(8,128)(2,1)} %wq.1, ...), custom_call_target="tpu_custom_call" | custom-call | tf_op jit(solution)/shard_map/pallas_call | solution.py:1100
  78.0 0.0 all-gather.5.cloned.1.call-update
  78.0 0.0 all-gather.3.cloned.1.call-start
  78.0 23.9 %shard_map.265 = (bf16[2048,1024]{1,0:T(8,128)(2,1)}, f32[1024,512]{1,0:T(8,128)}, f32[1024,256]{1,0:T(8,128)}, bf16[1024,512]{1,0:T(8,128)(2,1)}, bf16[1024,256...) custom-call(bf16[1024,2048]{1,0:T(8,128)(2,1)} %bitcast.32, ...), custom_call_target="tpu_custom_call" | custom-call | tf_op jit(solution)/shard_map/pallas_call | solution.py:1163
  102.0 30.6 %shard_map.266 = (bf16[1024,512]{1,0:T(8,128)(2,1)}, f32[8,1024]{1,0:T(8,128)}, bf16[1024,2048]{1,0:T(8,128)(2,1)}, bf16[4,256,2048]{2,1,0:T(8,128)(2,1)}, bf16[4,64,1536]{2,1,0:T(8,128)(2,1)}) custom-call(bf16[1024,512]{1,0:T(8,128)(2,1)} %get-tuple-element.88.q_ref, bf16[1024,256]{1,0:T(8,128)(2,1)} %get-tuple-element.90.k_ref, ...), custom_call_target="tpu_custom_call", output_to_operand_aliasing={{3}: (7, {})} | custom-call | tf_op jit(solution)/shard_map/pallas_call | solution.py:1202
  132.6 0.0 all-gather.3.cloned.1.call-update
  132.7 0.2 reduce-scatter.4.cloned.1.call-start
  132.9 73.0 %shard_map.267 = (f32[256,2048]{1,0:T(8,128)}, bf16[4,256,2048]{2,1,0:T(8,128)(2,1)}) custom-call(bf16[4,256,2048]{2,1,0:T(8,128)(2,1)} %bitcast.31, bf16[256,2048]{1,0:T(8,128)(2,1)} %x.5, f32[1,2048]{1,0:T(1,128)} %get-tuple-element.102.gain), custom_call_target="tpu_custom_call" | custom-call | tf_op jit(solution)/shard_map/pallas_call | solution.py:1239
  205.9 0.0 all-gather.5.cloned.1.call-done
  205.9 20.8 %shard_map.268 = (f32[1024,1536]{1,0:T(8,128)}, f32[1024,1536]{1,0:T(8,128)}, bf16[1024,1536]{1,0:T(8,128)(2,1)}, bf16[2048,1024]{1,0:T(8,128)(2,1)}) custom-call(bf16[1024,2048]{1,0:T(8,128)(2,1)} %bitcast.30, bf16[2048,3072]{1,0:T(8,128)(2,1)} %bitcast.19, bf16[2048,3072]{1,0:T(8,128)(2,1)} %bitcast.20), custom_call_target="tpu_custom_call" | custom-call | tf_op jit(solution)/shard_map/pallas_call | solution.py:1254
  226.8 15.2 %shard_map.269 = bf16[4,256,1536]{2,1,0:T(8,128)(2,1)} custom-call(bf16[1024,2048]{1,0:T(8,128)(2,1)} %bitcast.22, bf16[1024,1536]{1,0:T(8,128)(2,1)} %get-tuple-element.105.refs_1_.hidden_far), custom_call_target="tpu_custom_call" | custom-call | tf_op jit(solution)/shard_map/pallas_call | solution.py:1292
  242.0 0.0 reduce-scatter.4.cloned.1.call-update
  242.0 0.0 reduce-scatter.6.cloned.1.call-start
  242.1 15.3 %all-gather.3.cloned.1.call-done = bf16[4,512,1536]{2,1,0:T(8,128)(2,1)} async-done(((bf16[4,64,1536]{2,1,0:T(8,128)(2,1)}), bf16[4,512,1536]{2,1,0:T(8,128)(2,1)}) %all-gather.3.cloned.1.call-update) | async-done | bytes 6291472 | tf_op jit(solution)/shard_map/all_gather | solution.py:1231
  257.4 15.0 %shard_map.270 = (bf16[1024,1536]{1,0:T(8,128)(2,1)}, bf16[1024,1536]{1,0:T(8,128)(2,1)}) custom-call(bf16[1024,2048]{1,0:T(8,128)(2,1)} %bitcast.23, bf16[2048,1536]{1,0:T(8,128)(2,1)} %bitcast.24, f32[1024,1536]{1,0:T(8,128)} %get-tuple-element.107.gate_ref, f32[1024,1536]{1,0:T(8,128)} %get-tuple-element.108.up_ref), custom_call_target="tpu_custom_call" | custom-call | tf_op jit(solution)/shard_map/pallas_call | solution.py:1323
  272.3 22.3 %shard_map.271 = bf16[4,256,3072]{2,1,0:T(8,128)(2,1)} custom-call(bf16[2048,1024]{1,0:T(8,128)(2,1)} %get-tuple-element.110.refs_0_, bf16[1024,1536]{1,0:T(8,128)(2,1)} %get-tuple-element.112.refs_1_.dgate_far, bf16[1024,1536]{1,0:T(8,128)(2,1)} %get-tuple-element.111.refs_2_.dup_far), custom_call_target="tpu_custom_call" | custom-call | tf_op jit(solution)/shard_map/pallas_call | solution.py:1292
  294.7 0.0 reduce-scatter.6.cloned.1.call-update
  294.7 0.3 reduce-scatter.8.cloned.1.call-start
  295.0 83.9 %shard_map.272 = (f32[256,2048]{1,0:T(8,128)}, bf16[4,256,2048]{2,1,0:T(8,128)(2,1)}, f32[16,128]{1,0:T(8,128)}, bf16[4,256,2048]{2,1,0:T(8,128)(2,1)}) custom-call(bf16[1024,1536]{1,0:T(8,128)(2,1)} %get-tuple-element.112.refs_1_.dgate_far, bf16[1024,1536]{1,0:T(8,128)(2,1)} %get-tuple-element.111.refs_2_.dup_far, bf16[2048,3072]{1,0:T(8,128)(2,1)} %bitcast.21, ...), custom_call_target="tpu_custom_call" | custom-call | tf_op jit(solution)/shard_map/pallas_call | solution.py:1340
  378.9 43.0 %shard_map.273 = (bf16[1024,512]{1,0:T(8,128)(2,1)}, bf16[1024,256]{1,0:T(8,128)(2,1)}, bf16[1024,256]{1,0:T(8,128)(2,1)}, f32[8,128]{1,0:T(8,128)}, f32[8,128]{...) custom-call(bf16[1024,512]{1,0:T(8,128)(2,1)} %get-tuple-element.88.q_ref, ...), custom_call_target="tpu_custom_call" | custom-call | tf_op jit(solution)/shard_map/pallas_call | solution.py:1373
  421.9 0.0 reduce-scatter.4.cloned.1.call-done.refs_5_
  421.9 14.9 %shard_map.274 = (bf16[6,256,1024]{2,1,0:T(8,128)(2,1)}, bf16[4,64,1536]{2,1,0:T(8,128)(2,1)}) custom-call(bf16[2048,1024]{1,0:T(8,128)(2,1)} %get-tuple-element.120.refs_0_, bf16[1024,512]{1,0:T(8,128)(2,1)} %get-tuple-element.125.refs_1_.dq, bf16[1024,256]{1,0:T(8,128)(2,1)} %get-tuple-element.121.refs_2_.dk, ...), custom_call_target="tpu_custom_call", output_to_operand_aliasing={{0}: (4, {})} | custom-call | tf_op jit(solution)/shard_map/pallas_call | solution.py:1292
  436.8 0.0 reduce-scatter.6.cloned.1.call-done.gu
  436.8 0.0 reduce-scatter.8.cloned.1.call-update
  436.9 62.3 %shard_map.275 = (bf16[256,2048]{1,0:T(8,128)(2,1)}, bf16[4,64,3072]{2,1,0:T(8,128)(2,1)}, f32[8,128]{1,0:T(8,128)}) custom-call(bf16[1024,512]{1,0:T(8,128)(2,1)} %get-tuple-element.125.refs_1_.dq, bf16[1024,256]{1,0:T(8,128)(2,1)} %get-tuple-element.121.refs_2_.dk, bf16[1024,256]{1,0:T(8,128)(2,1)} %get-tuple-element.122.refs_3_.dv, ...), custom_call_target="tpu_custom_call" | custom-call | tf_op jit(solution)/shard_map/pallas_call | solution.py:1439
  499.2 0.0 reduce-scatter.8.cloned.1.call-done.source.o
  499.2 8.5 %shard_map.276.att = bf16[4,64,1024]{2,1,0:T(8,128)(2,1)} custom-call(bf16[6,64,1024]{2,1,0:T(8,128)(2,1)} %reduce-scatter.8.cloned.1.call-done.source.o), custom_call_target="tpu_custom_call" | custom-call | tf_op jit(solution)/shard_map/pallas_call | solution.py:1468
  507.7 6.2 %shard_map.277 = (bf16[256,2048]{1,0:T(8,128)(2,1)}, bf16[256,2048]{1,0:T(8,128)(2,1)}, f32[1,64]{1,0:T(1,128)}, f32[64,2048]{1,0:T(8,128)}, f32[64,1024]{1,0:T(...) custom-call(bf16[256,2048]{1,0:T(8,128)(2,1)} %get-tuple-element.118, ...), custom_call_target="tpu_custom_call" | custom-call | tf_op jit(solution)/shard_map/pallas_call | solution.py:1482
  (2 shorter events, 0.0 us)
Async XLA Ops:
  7.2 198.7 %all-gather.5.cloned.1.call-start = ((), (), s32[]{:S(2)}) async-start(), calls=%async_computation.4 | async-start | bytes 14155776 | tf_op jit(solution)/shard_map/all_gather | solution.py:1151
  78.0 179.4 %all-gather.3.cloned.1.call-start = ((), (), s32[]{:S(2)}) async-start(), calls=%async_computation.3 | async-start | bytes 7077888 | tf_op jit(solution)/shard_map/all_gather | solution.py:1231
  132.7 289.2 %reduce-scatter.4.cloned.1.call-start = ((), (), s32[]{:S(2)}) async-start(), calls=%async_computation.5 | async-start | bytes 3932160 | tf_op jit(solution)/shard_map/reduce_scatter | solution.py:1316
  242.0 194.8 %reduce-scatter.6.cloned.1.call-start = ((), (), s32[]{:S(2)}) async-start(), calls=%async_computation.6 | async-start | bytes 7864320 | tf_op jit(solution)/shard_map/reduce_scatter | solution.py:1316
  294.7 204.5 %reduce-scatter.8.cloned.1.call-start = ((), (), s32[]{:S(2)}) async-start(), calls=%async_computation.7 | async-start | bytes 3932160 | tf_op jit(solution)/shard_map/reduce_scatter | solution.py:1316
Sparse Core Ops, SparseCore 0:
  78.1 114.6 all-gather.4
  194.4 62.8 all-gather.2
  259.7 58.9 reduce-scatter.3
  320.8 110.7 reduce-scatter.5
  437.0 61.1 reduce-scatter.7

commit v7 on v6

--- a/solution.py
+++ b/solution.py
@@ -111,11 +111,11 @@
     def start(part=None):
         chosen = range(len(copies))
         if n == 4:
-            chosen = {None: (0, 1, 2, 3), 0: (0, 3), 1: (1, 2)}[part]
-        if n == 4 or part != 0:
+            chosen = {None: (0, 1, 2, 3), 0: (0, 3), 1: (1, 2), 2: (0, 1), 3: (2, 3)}[part]
+        if n == 4 or part not in (0, 2):
             for i in chosen:
                 copies[i].start()
-        if part != 0:
+        if part not in (0, 2):
             keep.start()
 
     def relay():
@@ -386,7 +386,7 @@
                 for i in (first, first + 1):
                     mine[i : i + 1, at * count : at * count + count] = raw[
                         :, i * 128 : i * 128 + count
-                    ]
+                    ].astype(F32)
 
     small = [pltpu.make_async_copy(mine, seen.at[me], glocal.at[0])]
     for j in range(1, n):
@@ -428,16 +428,18 @@
         low[...] = begin_of(places)
         high[...] = jnp.maximum(places, jnp.minimum(picture, end) - 1)
 
+    start, relay, finish = gather_parts(n, x, xg, send, recv, local)
+    start(2)
     rope()
+    if line:
+        o_step(1)
+        o_step(2)
     for copy in near:
         copy.wait()
     if line:
         a_first()
     copies = start_columns(n, [(wg, gu, 0), (wu, gu, 1)], wsend, wrecv, wlocal)
-    start, relay, finish = gather_parts(n, x, xg, send, recv, local)
-    start()
-    if line:
-        o_step(1)
+    start(3)
     for copy in small:
         copy.wait()
     wide = [pltpu.make_async_copy(seen, gains.at[spot], glocal.at[1])]
@@ -466,12 +468,10 @@
         gain_q[...] = total[2:3, :]
         gain_k[...] = total[3:4, :]
 
-    if line:
-        o_step(2)
-        a_step(1)
     relay()
     if line:
         o_step(3)
+        a_step(1)
         a_step(2)
         a_step(3)
         o_finish()
@@ -1088,7 +1088,7 @@
     entries = []
     for gain in (norm1_gain, norm2_gain, q_gain, k_gain):
         entries += [gain, jnp.zeros((128 - gain.shape[0],), BF)]
-    packed = jnp.concatenate(entries).astype(F32)[None, :]
+    packed = jnp.concatenate(entries)[None, :]
 
     gather_sems = [dma(gather_copies(n)), dma(gather_copies(n)), pltpu.SemaphoreType.DMA]
     line = nf == 8

time: 521 us -> 523 us (level)
  no operation moved by 1% of the time
where the time goes in v7:
time: 523 us
  Pallas kernels  488 us (93%)
  waiting for transfers between devices  16.3 us (3%)
  between operations  13.9 us (3%)
    pallas_call x1, Pallas kernels, shards(): pl.pallas_call(functools.partial(back_stage, n), out_shape=(shape((rows,...  83.9 us
    pallas_call x1, Pallas kernels, shards(): pl.pallas_call(functools.partial(middle_stage, n), out_shape=(shape((rows...  73 us
    pallas_call x1, Pallas kernels, shards(): pl.pallas_call(functools.partial(entry_stage, n, nf, line, own_gain, own_...  68.2 us
    pallas_call x1, Pallas kernels, shards(): pl.pallas_call(functools.partial(last_stage, n, nf), out_shape=(shape((ro...  62.3 us
    pallas_call x3, Pallas kernels, product(): pl.pallas_call(functools.partial(gradient, n, counts, len(kept), flipped,...  52.4 us
    pallas_call x1, Pallas kernels, shards(): pl.pallas_call(functools.partial(attend_back, n), grid=(kheads, blocks),...  43 us
    pallas_call x1, Pallas kernels, shards(): pl.pallas_call(functools.partial(attend, n), grid=(blocks,), out_shape=(s...  30.4 us
    pallas_call x1, Pallas kernels, shards(): pl.pallas_call(functools.partial(project, n), grid=(blocks,), out_shape=(...  24.7 us
  transfers between devices with their start and end apart: 5, of which 1 were waited for; matrix products, arithmetic and copies ran while one was open for 0% of the time, Pallas kernels for 78%

profile of v7, /device:TPU:0, one launch (start us, length us, event | category | flops | bytes accessed | tf_op | source)
XLA Modules:
  0.0 522.6 jit_solution(3901535416673065211)
XLA Ops:
  7.2 0.0 all-gather.5.cloned.1.call-start
  7.2 2.8 concatenate.3
  10.0 0.6 broadcast_in_dim.3.raw
  10.6 68.2 %shard_map.264 = (bf16[4,8,64,1024]{3,2,1,0:T(8,128)(2,1)}, bf16[4,64,3072]{2,1,0:T(8,128)(2,1)}, bf16[4,256,2048]{2,1,0:T(8,128)(2,1)}, bf16[8,64,2048]{2,1,0:T...) custom-call(bf16[64,2048]{1,0:T(8,128)(2,1)} %wq.1, ...), custom_call_target="tpu_custom_call" | custom-call | tf_op jit(solution)/shard_map/pallas_call | solution.py:1100
  78.8 0.0 all-gather.5.cloned.1.call-update
  78.8 0.0 all-gather.3.cloned.1.call-start
  78.9 24.7 %shard_map.265 = (bf16[2048,1024]{1,0:T(8,128)(2,1)}, f32[1024,512]{1,0:T(8,128)}, f32[1024,256]{1,0:T(8,128)}, bf16[1024,512]{1,0:T(8,128)(2,1)}, bf16[1024,256...) custom-call(bf16[1024,2048]{1,0:T(8,128)(2,1)} %bitcast.28, ...), custom_call_target="tpu_custom_call" | custom-call | tf_op jit(solution)/shard_map/pallas_call | solution.py:1163
  103.5 30.4 %shard_map.266 = (bf16[1024,512]{1,0:T(8,128)(2,1)}, f32[8,1024]{1,0:T(8,128)}, bf16[1024,2048]{1,0:T(8,128)(2,1)}, bf16[4,256,2048]{2,1,0:T(8,128)(2,1)}, bf16[4,64,1536]{2,1,0:T(8,128)(2,1)}) custom-call(bf16[1024,512]{1,0:T(8,128)(2,1)} %get-tuple-element.88.q_ref, bf16[1024,256]{1,0:T(8,128)(2,1)} %get-tuple-element.90.k_ref, ...), custom_call_target="tpu_custom_call", output_to_operand_aliasing={{3}: (7, {})} | custom-call | tf_op jit(solution)/shard_map/pallas_call | solution.py:1202
  133.9 0.0 all-gather.3.cloned.1.call-update
  133.9 0.2 reduce-scatter.4.cloned.1.call-start
  134.2 73.0 %shard_map.267 = (f32[256,2048]{1,0:T(8,128)}, bf16[4,256,2048]{2,1,0:T(8,128)(2,1)}) custom-call(bf16[4,256,2048]{2,1,0:T(8,128)(2,1)} %bitcast.27, bf16[256,2048]{1,0:T(8,128)(2,1)} %x.5, f32[1,2048]{1,0:T(1,128)} %get-tuple-element.102.gain), custom_call_target="tpu_custom_call" | custom-call | tf_op jit(solution)/shard_map/pallas_call | solution.py:1239
  207.2 0.0 all-gather.5.cloned.1.call-done
  207.3 20.8 %shard_map.268 = (f32[1024,1536]{1,0:T(8,128)}, f32[1024,1536]{1,0:T(8,128)}, bf16[1024,1536]{1,0:T(8,128)(2,1)}, bf16[2048,1024]{1,0:T(8,128)(2,1)}) custom-call(bf16[1024,2048]{1,0:T(8,128)(2,1)} %bitcast.26, bf16[2048,3072]{1,0:T(8,128)(2,1)} %bitcast.15, bf16[2048,3072]{1,0:T(8,128)(2,1)} %bitcast.16), custom_call_target="tpu_custom_call" | custom-call | tf_op jit(solution)/shard_map/pallas_call | solution.py:1254
  228.1 15.2 %shard_map.269 = bf16[4,256,1536]{2,1,0:T(8,128)(2,1)} custom-call(bf16[1024,2048]{1,0:T(8,128)(2,1)} %bitcast.18, bf16[1024,1536]{1,0:T(8,128)(2,1)} %get-tuple-element.105.refs_1_.hidden_far), custom_call_target="tpu_custom_call" | custom-call | tf_op jit(solution)/shard_map/pallas_call | solution.py:1292
  243.3 0.0 reduce-scatter.4.cloned.1.call-update
  243.3 0.0 reduce-scatter.6.cloned.1.call-start
  243.3 16.1 %all-gather.3.cloned.1.call-done = bf16[4,512,1536]{2,1,0:T(8,128)(2,1)} async-done(((bf16[4,64,1536]{2,1,0:T(8,128)(2,1)}), bf16[4,512,1536]{2,1,0:T(8,128)(2,1)}) %all-gather.3.cloned.1.call-update) | async-done | bytes 6291472 | tf_op jit(solution)/shard_map/all_gather | solution.py:1231
  259.5 15.0 %shard_map.270 = (bf16[1024,1536]{1,0:T(8,128)(2,1)}, bf16[1024,1536]{1,0:T(8,128)(2,1)}) custom-call(bf16[1024,2048]{1,0:T(8,128)(2,1)} %bitcast.19, bf16[2048,1536]{1,0:T(8,128)(2,1)} %bitcast.20, f32[1024,1536]{1,0:T(8,128)} %get-tuple-element.107.gate_ref, f32[1024,1536]{1,0:T(8,128)} %get-tuple-element.108.up_ref), custom_call_target="tpu_custom_call" | custom-call | tf_op jit(solution)/shard_map/pallas_call | solution.py:1323
  274.5 22.3 %shard_map.271 = bf16[4,256,3072]{2,1,0:T(8,128)(2,1)} custom-call(bf16[2048,1024]{1,0:T(8,128)(2,1)} %get-tuple-element.110.refs_0_, bf16[1024,1536]{1,0:T(8,128)(2,1)} %get-tuple-element.112.refs_1_.dgate_far, bf16[1024,1536]{1,0:T(8,128)(2,1)} %get-tuple-element.111.refs_2_.dup_far), custom_call_target="tpu_custom_call" | custom-call | tf_op jit(solution)/shard_map/pallas_call | solution.py:1292
  296.8 0.0 reduce-scatter.6.cloned.1.call-update
  296.8 0.3 reduce-scatter.8.cloned.1.call-start
  297.1 83.9 %shard_map.272 = (f32[256,2048]{1,0:T(8,128)}, bf16[4,256,2048]{2,1,0:T(8,128)(2,1)}, f32[16,128]{1,0:T(8,128)}, bf16[4,256,2048]{2,1,0:T(8,128)(2,1)}) custom-call(bf16[1024,1536]{1,0:T(8,128)(2,1)} %get-tuple-element.112.refs_1_.dgate_far, bf16[1024,1536]{1,0:T(8,128)(2,1)} %get-tuple-element.111.refs_2_.dup_far, bf16[2048,3072]{1,0:T(8,128)(2,1)} %bitcast.17, ...), custom_call_target="tpu_custom_call" | custom-call | tf_op jit(solution)/shard_map/pallas_call | solution.py:1340
  381.0 43.0 %shard_map.273 = (bf16[1024,512]{1,0:T(8,128)(2,1)}, bf16[1024,256]{1,0:T(8,128)(2,1)}, bf16[1024,256]{1,0:T(8,128)(2,1)}, f32[8,128]{1,0:T(8,128)}, f32[8,128]{...) custom-call(bf16[1024,512]{1,0:T(8,128)(2,1)} %get-tuple-element.88.q_ref, ...), custom_call_target="tpu_custom_call" | custom-call | tf_op jit(solution)/shard_map/pallas_call | solution.py:1373
  424.0 0.0 reduce-scatter.4.cloned.1.call-done.refs_5_
  424.0 14.9 %shard_map.274 = (bf16[6,256,1024]{2,1,0:T(8,128)(2,1)}, bf16[4,64,1536]{2,1,0:T(8,128)(2,1)}) custom-call(bf16[2048,1024]{1,0:T(8,128)(2,1)} %get-tuple-element.120.refs_0_, bf16[1024,512]{1,0:T(8,128)(2,1)} %get-tuple-element.125.refs_1_.dq, bf16[1024,256]{1,0:T(8,128)(2,1)} %get-tuple-element.121.refs_2_.dk, ...), custom_call_target="tpu_custom_call", output_to_operand_aliasing={{0}: (4, {})} | custom-call | tf_op jit(solution)/shard_map/pallas_call | solution.py:1292
  438.9 0.0 reduce-scatter.6.cloned.1.call-done.gu
  439.0 0.0 reduce-scatter.8.cloned.1.call-update
  439.0 62.3 %shard_map.275 = (bf16[256,2048]{1,0:T(8,128)(2,1)}, bf16[4,64,3072]{2,1,0:T(8,128)(2,1)}, f32[8,128]{1,0:T(8,128)}) custom-call(bf16[1024,512]{1,0:T(8,128)(2,1)} %get-tuple-element.125.refs_1_.dq, bf16[1024,256]{1,0:T(8,128)(2,1)} %get-tuple-element.121.refs_2_.dk, bf16[1024,256]{1,0:T(8,128)(2,1)} %get-tuple-element.122.refs_3_.dv, ...), custom_call_target="tpu_custom_call" | custom-call | tf_op jit(solution)/shard_map/pallas_call | solution.py:1439
  501.3 0.0 reduce-scatter.8.cloned.1.call-done.source.o
  501.3 8.5 %shard_map.276.att = bf16[4,64,1024]{2,1,0:T(8,128)(2,1)} custom-call(bf16[6,64,1024]{2,1,0:T(8,128)(2,1)} %reduce-scatter.8.cloned.1.call-done.source.o), custom_call_target="tpu_custom_call" | custom-call | tf_op jit(solution)/shard_map/pallas_call | solution.py:1468
  509.8 6.2 %shard_map.277 = (bf16[256,2048]{1,0:T(8,128)(2,1)}, bf16[256,2048]{1,0:T(8,128)(2,1)}, f32[1,64]{1,0:T(1,128)}, f32[64,2048]{1,0:T(8,128)}, f32[64,1024]{1,0:T(...) custom-call(bf16[256,2048]{1,0:T(8,128)(2,1)} %get-tuple-element.118, ...), custom_call_target="tpu_custom_call" | custom-call | tf_op jit(solution)/shard_map/pallas_call | solution.py:1482
  (2 shorter events, 0.0 us)
Async XLA Ops:
  7.2 200.1 %all-gather.5.cloned.1.call-start = ((), (), s32[]{:S(2)}) async-start(), calls=%async_computation.4 | async-start | bytes 14155776 | tf_op jit(solution)/shard_map/all_gather | solution.py:1151
  78.8 180.7 %all-gather.3.cloned.1.call-start = ((), (), s32[]{:S(2)}) async-start(), calls=%async_computation.3 | async-start | bytes 7077888 | tf_op jit(solution)/shard_map/all_gather | solution.py:1231
  133.9 290.1 %reduce-scatter.4.cloned.1.call-start = ((), (), s32[]{:S(2)}) async-start(), calls=%async_computation.5 | async-start | bytes 3932160 | tf_op jit(solution)/shard_map/reduce_scatter | solution.py:1316
  243.3 195.7 %reduce-scatter.6.cloned.1.call-start = ((), (), s32[]{:S(2)}) async-start(), calls=%async_computation.6 | async-start | bytes 7864320 | tf_op jit(solution)/shard_map/reduce_scatter | solution.py:1316
  296.8 204.5 %reduce-scatter.8.cloned.1.call-start = ((), (), s32[]{:S(2)}) async-start(), calls=%async_computation.7 | async-start | bytes 3932160 | tf_op jit(solution)/shard_map/reduce_scatter | solution.py:1316
Sparse Core Ops, SparseCore 0:
  78.9 115.9 all-gather.4
  196.6 62.8 all-gather.2
  261.8 58.9 reduce-scatter.3
  323.0 110.7 reduce-scatter.5
  439.1 61.1 reduce-scatter.7
